TPU v7x, 128 devices: a whole 4x4x4 slice. The times are simulated.
128 devices in a mesh: bx: 8 (over y, core), by: 16 (over x, z).
Axes of the slice: x: 4, y: 4, z: 4, core: 2. Of those that a mesh axis runs over, the one named last changes fastest.
Arguments:
- src_pos: int32 [2, 128, 16384], P(None, ('bx', 'by')), may hold values from 0 to 4095, as said below
- src_amp: float32 [2, 128, 16384], P(None, ('bx', 'by')), may hold values from -18 to 18
- box_slots: int32 [128, 256, 64], P(('bx', 'by')), may hold values from -1 to 16383, as said below
Outputs:
- weights: float32 [16, 8, 16, 16, 2, 256], P(None, 'bx', None, 'by')
Inputs may be any that keep to these rules, and one draw needn't show every extreme that they name: `box_slots`: each row lists the received slots of the sources in that leaf box of that owner: 1 to 64 distinct slots first, then -1; in every owner some box lists exactly 64; no slot is listed twice for one owner. `src_pos`: A send slot to owner g holds a source inside g's block of leaf boxes, and inside leaf box b of g where g lists that slot for b.
All inputs are finite; a program needn't handle non-finite values.
Results may differ from a plain program's by a relative error of at most 0.0038.
Values sent between devices are 32-bit elements; how exact they have to be, the bound alone decides.
No kernel may reach another device: no remote copies, remote signals or barrier semaphores. Data moves between devices by JAX's collectives and lax.ppermute only.
A program may use at most 128 MiB of HBM per device.

v0:
```python
import functools
import math

import jax
import jax.numpy as jnp
import numpy as np
from jax import lax
from jax.experimental import pallas as pl
from jax.experimental.pallas import tpu as pltpu
from jax.sharding import PartitionSpec as P

NODES = 16
BOX_NODES = 256
DEVICES = 128
LEAVES = 16
BX = 8
BY = 16
BAND = 1024
F32 = jnp.float32
BF16 = jnp.bfloat16
ROUNDER = 12582912.0
SIN = (6.28305581, -41.33121471, 81.36682035, -74.47802935, 32.78144238)
COS = (0.99995995, -19.73105034, 64.67355678, -82.40422428, 45.64775943)


def chebyshev_points(point_count):
    indices = np.arange(point_count)
    return (1.0 - np.cos(np.pi * (2 * indices + 1) / (2 * point_count))) / 2.0


def lagrange_matrix(locations):
    points = chebyshev_points(NODES)
    matrix = np.ones((len(locations), NODES))
    for own in range(NODES):
        for other in range(NODES):
            if other != own:
                matrix[:, own] *= (locations - points[other]) / (points[own] - points[other])
    return matrix


def child_matrix(halves, child):
    if halves == 1:
        return np.eye(NODES)
    return lagrange_matrix((child + chebyshev_points(NODES)) / 2.0)


def stacked_matrix(halves_first, halves_second):
    pieces = [
        np.kron(child_matrix(halves_first, a), child_matrix(halves_second, b))
        for a in range(halves_first)
        for b in range(halves_second)
    ]
    return np.concatenate(pieces, axis=0)


def two_parts(matrix):
    exact = np.asarray(matrix, np.float32)
    high = exact.astype(jnp.bfloat16)
    low = (exact - high.astype(np.float32)).astype(jnp.bfloat16)
    return high, low


def velocity(first, second):
    return (2.0 + np.sin(2 * np.pi * first) * np.sin(2 * np.pi * second)) / 8.0


def bits(value, count):
    return [(value >> (count - 1 - k)) & 1 for k in range(count)]


def speed_change(first, second, level, split_first=True):
    count_second = 2.0**level
    count_first = 2.0 ** (level if split_first else level - 1)
    new = velocity((first + 0.5) / count_first, (second + 0.5) / count_second)
    above_first = first >> 1 if split_first else first
    old = velocity(
        (above_first + 0.5) / 2.0 ** (level - 1), ((second >> 1) + 0.5) / 2.0 ** (level - 1)
    )
    return new - old


def inner_speeds():
    table = np.zeros((4, 4, 8, 8))
    for child in range(4):
        x, y = bits(child, 2)
        for row in range(8):
            r0, r1, r2 = bits(row, 3)
            for sub in range(8):
                s0, s1, s2 = bits(sub, 3)
                table[0, child, row, sub] = speed_change(x, y, 1)
                table[1, child, row, sub] = speed_change(2 * r0 + x, 2 * r1 + y, 2)
                first, second = 2 * s0 + r2, 2 * s1 + s2
                table[2, child, row, sub] = speed_change(2 * first + x, 2 * second + y, 3)
                first, second = 2 * first + r0, 2 * second + r1
                table[3, child, row, sub] = speed_change(2 * first + x, 2 * second + y, 4)
    return table.reshape(1024).astype(np.float32)


def outer_speeds():
    tables = np.zeros((DEVICES, 7, 256))
    for device in range(DEVICES):
        coarse_first = device >> 3
        for child in range(4):
            x, y = bits(child, 2)
            for row in range(8):
                r0, r1, r2 = bits(row, 3)
                for sub in range(8):
                    s0, s1, s2 = bits(sub, 3)
                    place = child * 64 + row * 8 + sub
                    second = 2 * (device & 7) + s2
                    tables[device, 0, place] = speed_change(
                        2 * coarse_first + x, 2 * second + y, 5
                    )
                    tables[device, 1, place] = speed_change(
                        4 * coarse_first + 2 * r0 + x, 4 * second + 2 * r1 + y, 6
                    )
                    second = 2 * (device & 7) + r2
                    tables[device, 2, place] = speed_change(
                        8 * coarse_first + 4 * s0 + 2 * r0 + x,
                        8 * second + 4 * s1 + 2 * s2 + y,
                        7,
                    )
        for child in range(2):
            for row in range(16):
                r0, r1, r2, r3 = bits(row, 4)
                for sub in range(8):
                    s0, s1, s2 = bits(sub, 3)
                    place = child * 128 + row * 8 + sub
                    first = 8 * coarse_first + 4 * s0 + 2 * r2 + r0
                    second = 2 * (device & 7) + r3
                    second = 16 * second + 8 * s1 + 4 * s2 + 2 * r1 + child
                    tables[device, 3, place] = speed_change(first, second, 8, False)
                    tables[device, 4, place] = velocity((first + 0.5) / 128, (second + 0.5) / 256)
                    tables[device, 5, place] = 8 * (first + 0.5)
                    tables[device, 6, place] = 4 * (second + 0.5)
    return tables.reshape(DEVICES, 7 * 256).astype(np.float32)


def node_tables():
    points = chebyshev_points(NODES).astype(np.float32).astype(np.float64)
    first = np.repeat(points, NODES)
    second = np.tile(points, NODES)
    rows = np.zeros((16, BOX_NODES))
    for child in range(4):
        x, y = bits(child, 2)
        turns = (2 * x - 1) * 2 * first + (2 * y - 1) * second
        rows[child] = turns - np.round(turns)
    for child in range(2):
        rows[4 + child] = (2 * child - 1) * second
    rows[6] = 2 * first
    rows[7] = second
    rows[8] = np.round(first * 8192) / 8192
    rows[9] = first - rows[8]
    rows[10] = np.round(second * 8192) / 8192
    rows[11] = second - rows[10]
    rows[12] = BAND * np.sqrt(first * first + second * second)
    return rows.astype(np.float32)


def basis_factors():
    points = chebyshev_points(NODES)
    return [
        float(np.float32(1.0 / np.prod([points[own] - points[k] for k in range(NODES) if k != own])))
        for own in range(NODES)
    ]


def second_basis():
    small = lagrange_matrix((np.arange(16) + 0.5) / 16.0)
    whole = np.zeros((16, 32, 32, 16))
    for k in range(32):
        whole[:, k, k, :] = small
    return whole.reshape(512, 512)


def turn(turns):
    part = turns - ((turns + ROUNDER) - ROUNDER)
    square = part * part
    sine = SIN[4]
    cosine = COS[4]
    for k in (3, 2, 1, 0):
        sine = sine * square + SIN[k]
        cosine = cosine * square + COS[k]
    return cosine, sine * part


def split(value):
    high = value.astype(BF16)
    return high, (value - high.astype(F32)).astype(BF16)


def bit(value, place):
    return (value >> place) & 1


def make_turns(table, first_line, box, level_number, speeds, speed_row, node, base_row, children, rows):
    scale = 4.0 * 2.0 ** (level_number - 1)
    pairs = rows // 2

    def step(index, carry):
        source = index // pairs
        pair = lax.rem(index, pairs)
        radius = []
        for k in range(2):
            first, second = box(source, 2 * pair + k)
            along = first + node[6:7, :]
            across = second + node[7:8, :]
            radius.append(scale * jnp.sqrt(along * along + across * across))
        radius = jnp.concatenate([jnp.broadcast_to(value, (8, BOX_NODES)) for value in radius])
        for child in range(children):
            place = pl.multiple_of(speed_row + child * rows * 8 + pair * 16, 16)
            change = speeds[pl.ds(place, 16), :]
            change = jnp.concatenate([change, change], axis=1)
            cosine, sine = turn(change * radius + node[base_row + child : base_row + child + 1, :])
            line = first_line + index * children + child
            table[line, 0] = cosine
            table[line, 1] = sine
        return carry

    lax.fori_loop(0, (4 if children == 4 else 2) * pairs, step, 0)


def level(read, table, first_line, high, low, matrix, children, rows):
    sources = 4 if children == 4 else 2
    pairs = rows // 2
    for source in range(sources):
        lanes = slice(source * BOX_NODES, (source + 1) * BOX_NODES)
        for pair in range(pairs):
            group = source * rows + 2 * pair
            real, imaginary = (
                jnp.concatenate([read(group, part), read(group + 1, part)]) for part in range(2)
            )
            for child in range(children):
                line = first_line + (source * pairs + pair) * children + child
                cosine = table[line, 0]
                sine = table[line, 1]
                for part, value in enumerate(
                    (real * cosine - imaginary * sine, real * sine + imaginary * cosine)
                ):
                    place = (child * 2 + part) * rows * 8 + pair * 16
                    value_high, value_low = split(value)
                    high[place : place + 16, lanes] = value_high
                    low[place : place + 16, lanes] = value_low
        operand = jnp.concatenate([high[:, lanes], low[:, lanes], high[:, lanes]], axis=1)
        weights = matrix[source * 768 : (source + 1) * 768, :]
        part = jnp.dot(operand, weights, preferred_element_type=F32)
        total = part if source == 0 else total + part
    return total


def three_parts(matrix):
    high, low = two_parts(matrix)
    high = high.reshape(-1, BOX_NODES, BOX_NODES)
    low = low.reshape(-1, BOX_NODES, BOX_NODES)
    return np.stack([high, high, low], axis=1).reshape(-1, BOX_NODES)


def sub_bits():
    row = lax.broadcasted_iota(jnp.int32, (8, BOX_NODES), 0)
    return [bit(row, 2 - k).astype(F32) for k in range(3)]


def find_mask(slots, mask, high_hot, low_hot, total):
    iota = lax.broadcasted_iota(jnp.int32, (16, 128), 0).astype(F32)
    rows = [(iota + 16.0 * k).astype(BF16) for k in range(8)]
    one = jnp.ones((16, 128), BF16)
    zero = jnp.zeros((16, 128), BF16)
    total[...] = jnp.zeros_like(total)

    def step(index, carry):
        block = slots[pl.ds(pl.multiple_of(index * 16, 16), 16), :]
        block = jnp.concatenate([block[:8], block[8:]], axis=1)
        high = (block >> 7).astype(F32)
        low = (block & 127).astype(F32)
        for k in range(8):
            for source, hot in ((high, high_hot), (low, low_hot)):
                value = jnp.broadcast_to(source[k : k + 1], (16, 128)).astype(BF16)
                for place in range(8):
                    hot[16 * place : 16 * (place + 1), 128 * k : 128 * (k + 1)] = jnp.where(
                        value == rows[place], one, zero
                    )
        total[...] += lax.dot_general(
            high_hot[...], low_hot[...], (((1,), (1,)), ((), ())), preferred_element_type=F32
        )
        return carry

    lax.fori_loop(0, 16, step, 0)
    mask[...] = jnp.where(total[...] > 0.5, 1.0, 0.0)


def store_level(table, table_far, leave, index, size=64):
    lines = pl.ds(64 * index, size)
    return pltpu.make_async_copy(table.at[lines], table_far.at[lines], leave.at[index])


def fetch_level(table_far, table, arrive, index, size=64):
    lines = pl.ds(64 * index, size)
    return pltpu.make_async_copy(table_far.at[lines], table.at[lines], arrive.at[index])


def inner_turns_kernel(
    block,
    slots_far,
    node_far,
    speeds_far,
    mask,
    table_far,
    slots,
    node,
    speeds,
    table,
    high_hot,
    low_hot,
    total,
    arrive,
    leave,
):
    fetches = [
        pltpu.make_async_copy(far, near, arrive.at[k])
        for k, (far, near) in enumerate(
            ((slots_far, slots), (node_far, node), (speeds_far, speeds))
        )
    ]
    for fetch in fetches:
        fetch.start()
    fetches[0].wait()
    find_mask(slots, mask, high_hot, low_hot, total)
    for fetch in fetches[1:]:
        fetch.wait()
    stores = [store_level(table, table_far, leave, k) for k in range(4)]
    sub = sub_bits()
    block_first = block[0]
    block_second = block[1]

    def box(source, row):
        first = block_first * 16 + bit(source, 1) + 2 * bit(row, 2)
        second = block_second * 16 + bit(source, 0) + 2 * bit(row, 1) + 8 * bit(row, 0)
        return (
            2.0 * first.astype(F32) + (8.0 * sub[0] + 16.0 * sub[2]),
            second.astype(F32) + 4.0 * sub[1],
        )

    make_turns(table, 0, box, 1, speeds, 0, node, 0, 4, 8)
    stores[0].start()

    def box(source, row):
        first = block_first * 8 + bit(source, 1)
        second = block_second * 8 + bit(source, 0) + 4 * bit(row, 0)
        return (
            2.0 * first.astype(F32) + (4.0 * sub[0] + 8.0 * sub[2]),
            second.astype(F32) + 2.0 * sub[1],
        )

    make_turns(table, 64, box, 2, speeds, 256, node, 0, 4, 8)
    stores[1].start()

    def box(source, row):
        first = block_first * 4 + bit(source, 1) + 2 * bit(row, 2)
        second = block_second * 4 + bit(source, 0) + 2 * bit(row, 1)
        return 2.0 * first.astype(F32), second.astype(F32)

    make_turns(table, 128, box, 3, speeds, 512, node, 0, 4, 8)
    stores[2].start()

    def box(source, row):
        first = block_first * 2 + bit(source, 1)
        second = block_second * 2 + bit(source, 0)
        return 2.0 * first.astype(F32), second.astype(F32)

    make_turns(table, 192, box, 4, speeds, 768, node, 0, 4, 8)
    stores[3].start()
    for store in stores:
        store.wait()


def outer_turns_kernel(node, speeds, table_far, table, leave):
    stores = [store_level(table, table_far, leave, k, 64 if k < 3 else 48) for k in range(4)]
    sub = sub_bits()

    def box(source, row):
        first = bit(source, 1) + 2 * bit(row, 2) + 4 * bit(row, 1)
        second = bit(source, 0) + 2 * bit(row, 0)
        return 2.0 * first.astype(F32), second.astype(F32) + (4.0 * sub[0] + 8.0 * sub[1])

    make_turns(table, 0, box, 5, speeds, 0, node, 0, 4, 8)
    stores[0].start()

    def box(source, row):
        first = bit(source, 1) + 2 * bit(row, 0)
        second = bit(source, 0)
        return 2.0 * first.astype(F32), second.astype(F32) + (2.0 * sub[0] + 4.0 * sub[1])

    make_turns(table, 64, box, 6, speeds, 256, node, 0, 4, 8)
    stores[1].start()

    def box(source, row):
        first = bit(source, 1)
        second = bit(source, 0) + 2 * bit(row, 1)
        return 2.0 * first.astype(F32), second.astype(F32)

    make_turns(table, 128, box, 7, speeds, 512, node, 0, 4, 8)
    stores[2].start()

    def box(source, row):
        return jnp.float32(0.0), source.astype(F32)

    make_turns(table, 192, box, 8, speeds, 768, node, 4, 2, 16)

    def last(index, carry):
        def column(table):
            value = speeds[pl.ds(pl.multiple_of(256 * table + index * 16, 16), 16), :]
            return jnp.concatenate([value, value], axis=1)

        first = column(5)
        second = column(6)
        turns = first * node[8:9, :]
        turns = turns - ((turns + ROUNDER) - ROUNDER)
        across = second * node[10:11, :]
        across = across - ((across + ROUNDER) - ROUNDER)
        around = column(4) * node[12:13, :]
        around = around - ((around + ROUNDER) - ROUNDER)
        turns = turns + across + around + first * node[9:10, :] + second * node[11:12, :]
        cosine, sine = turn(turns)
        table[224 + index, 0] = cosine
        table[224 + index, 1] = sine
        return carry

    lax.fori_loop(0, 16, last, 0)
    stores[3].start()
    for store in stores:
        store.wait()


def deposit(
    arrived, mask, second, fetch_second, state, wide, cells, hots, spreads, grid
):
    points = [float(value) for value in chebyshev_points(NODES).astype(np.float32)]
    factors = basis_factors()

    def source_step(index, carry):
        rows = pl.ds(pl.multiple_of(index * 16, 16), 16)
        first, second, real, imaginary = (
            arrived[pl.ds(index * 64 + k, 16, stride=4), :] for k in range(4)
        )
        whole_first = first.astype(jnp.int32)
        whole_second = second.astype(jnp.int32)
        along = first + 0.5
        across = second + 0.5
        eighths = jnp.bitwise_and(whole_first + whole_second + 1, 7).astype(F32)
        cosine, sine = turn(
            0.125 * eighths + 0.0625 * jnp.sqrt(along * along + across * across)
        )
        live = mask[rows, :]
        real = real * live
        imaginary = imaginary * live
        turned = (real * cosine - imaginary * sine, real * sine + imaginary * cosine)
        place = jnp.bitwise_and(whole_first, 31).astype(F32) * 0.03125 + 0.015625
        cells[0, rows, :] = jnp.bitwise_and(whole_second, 15).astype(F32)
        x = [bit(whole_first, 5 + k) for k in range(4)]
        y = [bit(whole_second, 4 + k) for k in range(4)]
        cells[1, rows, :] = (x[0] * 8 + y[0] * 4 + x[1] * 2 + y[1]).astype(F32)
        cells[2, rows, :] = (y[3] * 8 + x[2] * 4 + y[2] * 2 + x[3]).astype(F32)
        away = [place - value for value in points]
        before = [None] * NODES
        after = [None] * NODES
        for p in range(1, NODES):
            before[p] = away[p - 1] if p == 1 else before[p - 1] * away[p - 1]
            q = NODES - 1 - p
            after[q] = away[q + 1] if p == 1 else after[q + 1] * away[q + 1]
        for p in range(NODES):
            if p == 0:
                value = after[0]
            elif p == NODES - 1:
                value = before[p]
            else:
                value = before[p] * after[p]
            value = value * factors[p]
            for part in range(2):
                wide[pl.ds(index * 512 + part * 16 + p, 16, stride=32), :] = value * turned[part]
        return carry

    lax.fori_loop(0, 8, source_step, 0)

    iota = lax.broadcasted_iota(jnp.int32, (16, 128), 0).astype(F32).astype(BF16)
    one = jnp.ones((16, 128), BF16)
    zero = jnp.zeros((16, 128), BF16)
    both = jnp.zeros((32, 128), BF16)

    def build(chunk, hot, spread):
        for k in range(8):
            sender = chunk * 8 + k
            lanes = slice(128 * k, 128 * (k + 1))

            def row(number, height):
                value = cells[number, pl.ds(sender, 1), :]
                return jnp.broadcast_to(value, (height, 128)).astype(BF16)

            value = wide[pl.ds(pl.multiple_of(sender * 32, 32), 32), :].astype(BF16)
            cell = row(0, 32)
            for c in range(16):
                spread[32 * c : 32 * (c + 1), lanes] = jnp.where(
                    cell == jnp.full((32, 128), c, BF16), value, both
                )
            inside = jnp.where(row(2, 16) == iota, one, zero)
            above = row(1, 16)
            for c in range(16):
                hot[16 * c : 16 * (c + 1), lanes] = jnp.where(
                    above == jnp.full((16, 128), c, BF16), inside, zero
                )

    def add(hot, spread):
        grid[...] += lax.dot_general(
            spread[...], hot[...], (((1,), (1,)), ((), ())), preferred_element_type=F32
        )

    grid[...] = jnp.zeros_like(grid)
    build(0, hots[0], spreads[0])

    def spread_step(index, carry):
        build(2 * index + 1, hots[1], spreads[1])
        add(hots[0], spreads[0])
        build(jnp.minimum(2 * index + 2, 15), hots[0], spreads[0])
        add(hots[1], spreads[1])
        return carry

    lax.fori_loop(0, 8, spread_step, 0)

    grid_high, grid_low = split(grid[...].T)
    fetch_second.wait()
    result = jnp.dot(
        jnp.concatenate([grid_high, grid_low, grid_high], axis=1),
        second[...],
        preferred_element_type=F32,
    )
    for group in range(32):
        for part in range(2):
            state[group, part] = result[
                8 * group : 8 * group + 8, BOX_NODES * part : BOX_NODES * (part + 1)
            ]


def pieces(result):
    for child in range(4):
        for row in range(8):
            start = child * 128 + row * 8
            yield bits(child, 2), bits(row, 3), [
                result[start + 64 * part : start + 64 * part + 8, :] for part in range(2)
            ]


def halves(value):
    return value[:, :128], value[:, 128:]


def inner_kernel(
    arrived,
    mask,
    second_far,
    table_far,
    matrix,
    out,
    second,
    table,
    arrive,
    wide,
    cells,
    hots,
    spreads,
    grid,
    state,
    turned,
    high,
    low,
):
    fetch_second = pltpu.make_async_copy(second_far, second, arrive.at[4])
    fetch_second.start()
    fetches = [fetch_level(table_far, table, arrive, k) for k in range(4)]
    for fetch in fetches:
        fetch.start()
    deposit(arrived, mask, second, fetch_second, state, wide, cells, hots, spreads, grid)

    def run(number, read):
        fetches[number - 1].wait()
        return level(read, table, 64 * (number - 1), high, low, matrix, 4, 8)

    def read(group, part):
        return state[group, part]

    for (x, y), (r0, r1, r2), values in pieces(run(1, read)):
        for part in range(2):
            state[(2 * r0 + r1) * 8 + x * 4 + y * 2 + r2, part] = values[part]

    for (x, y), (r0, r1, r2), values in pieces(run(2, read)):
        start = ((r2 * 2 + x) * 8 + r0 * 4 + r1 * 2 + y) * 8
        for part in range(2):
            for half, value in enumerate(halves(values[part])):
                turned[2 * part + half, start : start + 8, :] = value

    def across(group, part):
        b2x, b2y, b3x, b3y, t2x = bits(group, 5)
        start = (b3y * 2 + t2x) * 64 + b2x * 4 + b2y * 2 + b3x
        return jnp.concatenate(
            [turned.at[2 * part + half][pl.ds(start, 8, stride=8), :] for half in range(2)], axis=1
        )

    for (x, y), (r0, r1, r2), values in pieces(run(3, across)):
        for part in range(2):
            state[(2 * r0 + r1) * 8 + x * 4 + y * 2 + r2, part] = values[part]

    for (x, y), (r0, r1, r2), values in pieces(run(4, read)):
        device = r2 * 32 + r0 * 16 + x * 8 + r1
        for upper in range(2):
            for part in range(2):
                for half, value in enumerate(halves(values[part])):
                    start = (device + 64 * upper) * 8 + y * 4 + half * 2 + part
                    out[pl.ds(start, 4, stride=16), :] = value[4 * upper : 4 * upper + 4]


def outer_kernel(
    arrived, table_far, matrix, last_far, out, table, last, arrive, state, turned, high, low
):
    fetches = [
        fetch_level(table_far, table, arrive, k, 64 if k < 3 else 48) for k in range(4)
    ]
    fetch_last = pltpu.make_async_copy(last_far, last, arrive.at[4])
    for fetch in fetches:
        fetch.start()
    fetch_last.start()

    def first_read(group, part):
        i2, j3, i1, i0, j2 = bits(group, 5)
        source = i2 * 64 + i1 * 32 + i0 * 16 + j3 * 8 + j2 * 4
        return jnp.concatenate(
            [
                arrived[pl.ds(source * 8 + half * 2 + part, 8, stride=4), :]
                for half in range(2)
            ],
            axis=1,
        )

    def run(number, read):
        fetches[number - 5].wait()
        return level(read, table, 64 * (number - 5), high, low, matrix, 4, 8)

    def read(group, part):
        return state[group, part]

    for (x, y), (i1, i0, j2), values in pieces(run(5, first_read)):
        for part in range(2):
            state[(2 * i1 + j2) * 8 + x * 4 + y * 2 + i0, part] = values[part]

    for (x, y), (r0, r1, i0), values in pieces(run(6, read)):
        start = ((i0 * 2 + x) * 8 + r0 * 4 + r1 * 2 + y) * 8
        for part in range(2):
            for half, value in enumerate(halves(values[part])):
                turned[2 * part + half, start : start + 8, :] = value

    def across(group, part):
        i0, j1, t6x, j0, pair = bits(group, 5)
        start = (i0 * 2 + t6x) * 64 + j1 * 4 + j0 * 2 + pair
        return jnp.concatenate(
            [turned.at[2 * part + half][pl.ds(start, 8, stride=8), :] for half in range(2)], axis=1
        )

    for (x, y), (t6x, j0, pair), values in pieces(run(7, across)):
        for part in range(2):
            state[j0 * 16 + x * 8 + y * 4 + t6x * 2 + pair, part] = values[part]

    fetches[3].wait()
    fetch_last.wait()
    result = level(read, table, 192, high, low, last, 2, 16)
    for child in range(2):
        for row in range(16):
            t7x, t7y, t6x, pair = bits(row, 4)
            start = child * 256 + row * 8
            line = 224 + child * 8 + row // 2
            cosine = table[line, 0, 8 * (row % 2) : 8 * (row % 2) + 8, :]
            sine = table[line, 1, 8 * (row % 2) : 8 * (row % 2) + 8, :]
            real = result[start : start + 8, :]
            imaginary = result[start + 128 : start + 136, :]
            device = t6x * 32 + t7x * 16 + t7y * 2 + child
            for part, whole in enumerate(
                (real * cosine + imaginary * sine, imaginary * cosine - real * sine)
            ):
                for half, value in enumerate(halves(whole)):
                    for upper in range(2):
                        place = (device + 64 * upper) * 8 + pair * 4 + half * 2 + part
                        out[pl.ds(place, 4, stride=32), :] = value[4 * upper : 4 * upper + 4]


def vmem(count):
    return [pl.BlockSpec(memory_space=pltpu.VMEM)] * count


def smem(count):
    return [pl.BlockSpec(memory_space=pltpu.SMEM)] * count


def far(count):
    return [pl.BlockSpec(memory_space=pl.ANY)] * count


def inner_turns(block, slots):
    speeds = np.repeat(inner_speeds()[:, None], 128, axis=1)
    return pl.pallas_call(
        inner_turns_kernel,
        out_shape=[
            jax.ShapeDtypeStruct((128, 128), F32),
            jax.ShapeDtypeStruct((256, 2, 16, 256), F32),
        ],
        in_specs=smem(1) + far(3),
        out_specs=vmem(1) + far(1),
        scratch_shapes=[
            pltpu.VMEM((256, 64), jnp.int32),
            pltpu.VMEM((16, 256), F32),
            pltpu.VMEM((1024, 128), F32),
            pltpu.VMEM((256, 2, 16, 256), F32),
            pltpu.VMEM((128, 1024), BF16),
            pltpu.VMEM((128, 1024), BF16),
            pltpu.VMEM((128, 128), F32),
            pltpu.SemaphoreType.DMA((3,)),
            pltpu.SemaphoreType.DMA((4,)),
        ],
        name="inner_turns",
        compiler_params=pltpu.CompilerParams(vmem_limit_bytes=48 << 20),
    )(block, slots, jnp.asarray(node_tables()), jnp.asarray(speeds))


def outer_turns(speeds):
    return pl.pallas_call(
        outer_turns_kernel,
        out_shape=jax.ShapeDtypeStruct((240, 2, 16, 256), F32),
        in_specs=vmem(2),
        out_specs=far(1)[0],
        scratch_shapes=[
            pltpu.VMEM((240, 2, 16, 256), F32),
            pltpu.SemaphoreType.DMA((4,)),
        ],
        name="outer_turns",
        compiler_params=pltpu.CompilerParams(vmem_limit_bytes=48 << 20),
    )(jnp.asarray(node_tables()), speeds)


LEVEL_SCRATCH = [
    pltpu.VMEM((32, 2, 8, 256), F32),
    pltpu.VMEM((4, 256, 128), F32),
    pltpu.VMEM((512, 1024), BF16),
    pltpu.VMEM((512, 1024), BF16),
]


def inner_levels(arrived, mask, table):
    second_high, second_low = two_parts(second_basis())
    second = np.concatenate([second_high, second_high, second_low], axis=0)
    return pl.pallas_call(
        inner_kernel,
        out_shape=jax.ShapeDtypeStruct((1024, 128), F32),
        in_specs=vmem(2) + far(2) + vmem(1),
        out_specs=vmem(1)[0],
        scratch_shapes=[
            pltpu.VMEM((1536, 512), BF16),
            pltpu.VMEM((256, 2, 16, 256), F32),
            pltpu.SemaphoreType.DMA((5,)),
            pltpu.VMEM((4096, 128), F32),
            pltpu.VMEM((3, 128, 128), F32),
            [pltpu.VMEM((256, 1024), BF16)] * 2,
            [pltpu.VMEM((512, 1024), BF16)] * 2,
            pltpu.VMEM((512, 256), F32),
        ]
        + LEVEL_SCRATCH,
        name="inner",
        compiler_params=pltpu.CompilerParams(vmem_limit_bytes=48 << 20),
    )(
        arrived,
        mask,
        jnp.asarray(second),
        table,
        jnp.asarray(three_parts(stacked_matrix(2, 2))),
    )


def outer_levels(arrived, table):
    return pl.pallas_call(
        outer_kernel,
        out_shape=jax.ShapeDtypeStruct((1024, 128), F32),
        in_specs=vmem(1) + far(1) + vmem(1) + far(1),
        out_specs=vmem(1)[0],
        scratch_shapes=[
            pltpu.VMEM((240, 2, 16, 256), F32),
            pltpu.VMEM((1536, 256), BF16),
            pltpu.SemaphoreType.DMA((5,)),
        ]
        + LEVEL_SCRATCH,
        name="outer",
        compiler_params=pltpu.CompilerParams(vmem_limit_bytes=48 << 20),
    )(
        arrived,
        table,
        jnp.asarray(three_parts(stacked_matrix(2, 2))),
        jnp.asarray(three_parts(stacked_matrix(1, 2))),
    )


def reverse_bits(number, bit_count):
    result = jnp.zeros_like(number)
    for position in range(bit_count):
        result = result + jnp.left_shift(
            jnp.bitwise_and(jnp.right_shift(number, position), 1), bit_count - 1 - position
        )
    return result


def exchange(array):
    return lax.all_to_all(array, ("bx", "by"), split_axis=0, concat_axis=0, tiled=True)


def shards(src_pos, src_amp, box_slots):
    column = lax.axis_index("bx")
    row = lax.axis_index("by")
    device = column * BY + row
    block = jnp.stack([reverse_bits(column, 3), reverse_bits(row, 4)]).astype(jnp.int32)
    payload = jnp.concatenate([src_pos[:, 0, :].astype(F32), src_amp[:, 0, :]], axis=0)
    payload = payload.reshape(4, DEVICES, 128).transpose(1, 0, 2)
    arrived = exchange(payload).reshape(512, 128)
    mask, table = inner_turns(block, box_slots[0])
    arrived, mask, table = lax.optimization_barrier((arrived, mask, table))
    weights = inner_levels(arrived, mask, table)
    weights = exchange(weights.reshape(DEVICES, 8, 128)).reshape(1024, 128)
    speeds = lax.dynamic_index_in_dim(jnp.asarray(outer_speeds()), device, 0, keepdims=False)
    speeds = jnp.broadcast_to(speeds[:, None], (7 * 256, 128))
    weights = outer_levels(weights, outer_turns(speeds))
    weights = exchange(weights.reshape(DEVICES, 8, 128))
    weights = weights.reshape(LEAVES, LEAVES, 2, 2, 128).transpose(0, 1, 3, 2, 4)
    return weights.reshape(LEAVES, 1, LEAVES, 1, 2, BOX_NODES)


def solution(mesh):
    return jax.shard_map(
        shards,
        mesh=mesh,
        in_specs=(
            P(None, ("bx", "by"), None),
            P(None, ("bx", "by"), None),
            P(("bx", "by"), None, None),
        ),
        out_specs=P(None, "bx", None, "by", None, None),
        check_vma=False,
    )
```

profile of v0, /device:TPU:1, one launch (start us, length us, event | category | flops | bytes accessed | tf_op | source)
XLA Modules:
  0.0 100.7 jit_solution(4200458890572754334)
XLA Ops:
  0.0 1.0 convert_element_type.7
  1.0 0.1 copy.12
  1.1 1.0 %copy.13 = f32[2,128,128]{2,0,1:T(2,128)S(1)} copy(f32[2,128,128]{2,1,0:T(8,128)} %bitcast.22) | data formatting | bytes 262144 | tf_op jit(solution)/shard_map/concatenate | solution.py:822
  2.1 0.8 maximum_bitcast_fusion
  2.9 0.0 copy-start.6
  2.9 11.5 %all-to-all-start = ((f32[128,4,128]{2,1,0:T(4,128)}), f32[128,4,128]{2,1,0:T(4,128)S(1)}, u32[]{:S(2)}, u32[]{:S(2)}) async-start(f32[128,4,128]{2,1,0:T(4,128)} %maximum_bitcast_fusion), calls=%async_computation | async-start | bytes 524288 | tf_op jit(solution)/shard_map/all_to_all | solution.py:814
  14.5 0.9 copy.14
  15.4 0.1 pad_add_fusion.block
  15.5 0.0 copy-start.4
  15.5 1.0 %copy-done.4 = f32[1024,128]{1,0:T(8,128)S(1)} copy-done((f32[1024,128]{1,0:T(8,128)S(1)}, f32[1024,128]{1,0:T(8,128)}, u32[]{:S(2)}) %copy-start.4) | copy-done | bytes 524312
  16.5 0.0 copy-start.5
  16.5 0.7 copy-done.5
  17.3 12.6 %inner_turns.1 = (f32[128,128]{1,0:T(8,128)S(1)}, f32[256,2,16,256]{3,2,1,0:T(8,128)}) custom-call(s32[2]{0:T(128)S(1)} %pad_add_fusion.block, s32[256,64]{1,0:T(8,128)S(1)} %bitcast.18, f32[16,256]{1,0:T(8,128)S(1)} %copy-done.5, f32[1024,128]{1,0:T(8,128)S(1)} %copy-done.4), custom_call_target="tpu_custom_call" | custom-call | tf_op jit(solution)/shard_map/inner_turns/pallas_call | solution.py:705
  29.8 0.0 all-to-all-done
  29.8 0.0 copy-start
  29.9 1.4 %copy-done = bf16[3072,256]{1,0:T(8,128)(2,1)S(1)} copy-done((bf16[3072,256]{1,0:T(8,128)(2,1)S(1)}, bf16[3072,256]{1,0:T(8,128)(2,1)}, u32[]{:S(2)}) %copy-start) | copy-done | bytes 1572888
  31.3 0.0 copy-start.2
  31.3 1.4 %copy-done.2 = bf16[1536,512]{1,0:T(8,128)(2,1)S(1)} copy-done((bf16[1536,512]{1,0:T(8,128)(2,1)S(1)}, bf16[1536,512]{1,0:T(8,128)(2,1)}, u32[]{:S(2)}) %copy-start.2) | copy-done | bytes 1572888
  32.7 17.6 %inner.1 = f32[1024,128]{1,0:T(8,128)} custom-call(f32[512,128]{1,0:T(8,128)S(1)} %bitcast.17, f32[128,128]{1,0:T(8,128)S(1)} %get-tuple-element.13.mask, bf16[1536,512]{1,0:T(8,128)(2,1)S(1)} %copy-done.2, f32[256,2,16,256]{3,2,1,0:T(8,128)} %get-tuple-element.14.table_far, bf16[3072,256]{1,0:T(8,128)(2,1)S(1)} %copy-done), custom_call_target="tpu_custom_call" | custom-call | tf_op jit(solution)/shard_map/inner/pallas_call | solution.py:755
  50.2 0.0 copy-start.1
  50.3 0.0 copy-start.3
  50.3 9.8 %all-to-all-start.1 = ((f32[128,8,128]{2,1,0:T(8,128)}), f32[128,8,128]{2,1,0:T(8,128)S(1)}, u32[]{:S(2)}, u32[]{:S(2)}) async-start(f32[128,8,128]{2,1,0:T(8,128)} %bitcast.7), calls=%async_computation.1 | async-start | bytes 1048576 | tf_op jit(solution)/shard_map/all_to_all | solution.py:814
  60.1 0.9 dynamic-slice_reduce_fusion
  60.9 0.3 broadcast_in_dim.9.speeds
  61.2 0.0 copy-done.6
  61.2 6.1 %outer_turns.1.table_far = f32[240,2,16,256]{3,2,1,0:T(8,128)} custom-call(f32[16,256]{1,0:T(8,128)S(1)} %copy-done.6, f32[1792,128]{1,0:T(8,128)S(1)} %broadcast_in_dim.9.speeds), custom_call_target="tpu_custom_call" | custom-call | tf_op jit(solution)/shard_map/outer_turns/pallas_call | solution.py:730
  67.3 6.1 %all-to-all-done.1 = f32[128,8,128]{2,1,0:T(8,128)S(1)} async-done(((f32[128,8,128]{2,1,0:T(8,128)}), f32[128,8,128]{2,1,0:T(8,128)S(1)}, u32[]{:S(2)}, u32[]{:S(2)}) %all-to-all-start.1) | async-done | bytes 524320 | tf_op jit(solution)/shard_map/all_to_all | solution.py:814
  73.4 0.0 copy-done.1
  73.5 0.0 copy-done.3
  73.5 7.7 %outer.1 = f32[1024,128]{1,0:T(8,128)S(1)} custom-call(f32[1024,128]{1,0:T(8,128)S(1)} %bitcast.15, f32[240,2,16,256]{3,2,1,0:T(8,128)} %outer_turns.1.table_far, bf16[3072,256]{1,0:T(8,128)(2,1)S(1)} %copy-done.1, bf16[1536,256]{1,0:T(8,128)(2,1)S(1)} %copy-done.3), custom_call_target="tpu_custom_call" | custom-call | tf_op jit(solution)/shard_map/outer/pallas_call | solution.py:783
  81.2 17.8 %all_to_all.15 = f32[128,8,128]{2,1,0:T(8,128)S(1)} all-to-all(f32[128,8,128]{2,1,0:T(8,128)S(1)} %bitcast.16), channel_id=1, replica_groups=mesh['bx'=8,'by'=16] {'bx','by'}, dimensions={0} | all-to-all | bytes 1048576 | tf_op jit(solution)/shard_map/all_to_all | solution.py:814
  99.0 0.3 copy.17
  99.3 1.4 %reshape.31 = f32[16,1,16,1,2,256]{5,4,3,2,1,0:T(2,128)} reshape(f32[16,16,2,2,128]{4,3,2,1,0:T(2,128)S(1)} %bitcast.20) | data formatting | bytes 1048576 | tf_op jit(solution)/shard_map/reshape | solution.py:834
Async XLA Ops:
  2.9 58.3 %copy-start.6 = (f32[16,256]{1,0:T(8,128)S(1)}, f32[16,256]{1,0:T(8,128)}, u32[]{:S(2)}) copy-start(f32[16,256]{1,0:T(8,128)} %constant.36.clone.node_far.node) | copy-start | bytes 49156
  2.9 26.9 %all-to-all-start = ((f32[128,4,128]{2,1,0:T(4,128)}), f32[128,4,128]{2,1,0:T(4,128)S(1)}, u32[]{:S(2)}, u32[]{:S(2)}) async-start(f32[128,4,128]{2,1,0:T(4,128)} %maximum_bitcast_fusion), calls=%async_computation | async-start | bytes 524288 | tf_op jit(solution)/shard_map/all_to_all | solution.py:814
  15.5 1.0 %copy-start.4 = (f32[1024,128]{1,0:T(8,128)S(1)}, f32[1024,128]{1,0:T(8,128)}, u32[]{:S(2)}) copy-start(f32[1024,128]{1,0:T(8,128)} %constant.37.clone.speeds_far) | copy-start | bytes 1572868
  16.5 0.7 copy-start.5
  29.8 1.4 %copy-start = (bf16[3072,256]{1,0:T(8,128)(2,1)S(1)}, bf16[3072,256]{1,0:T(8,128)(2,1)}, u32[]{:S(2)}) copy-start(bf16[3072,256]{1,0:T(8,128)(2,1)} %constant.39.clone.matrix) | copy-start | bytes 4718596
  31.3 1.4 %copy-start.2 = (bf16[1536,512]{1,0:T(8,128)(2,1)S(1)}, bf16[1536,512]{1,0:T(8,128)(2,1)}, u32[]{:S(2)}) copy-start(bf16[1536,512]{1,0:T(8,128)(2,1)} %constant.38.clone.second_far) | copy-start | bytes 4718596
  50.2 23.2 %copy-start.1 = (bf16[3072,256]{1,0:T(8,128)(2,1)S(1)}, bf16[3072,256]{1,0:T(8,128)(2,1)}, u32[]{:S(2)}) copy-start(bf16[3072,256]{1,0:T(8,128)(2,1)} %constant.39.clone.matrix) | copy-start | bytes 4718596
  50.3 23.2 %copy-start.3 = (bf16[1536,256]{1,0:T(8,128)(2,1)S(1)}, bf16[1536,256]{1,0:T(8,128)(2,1)}, u32[]{:S(2)}) copy-start(bf16[1536,256]{1,0:T(8,128)(2,1)} %constant.41.clone.last_far) | copy-start | bytes 2359300
  50.3 23.2 %all-to-all-start.1 = ((f32[128,8,128]{2,1,0:T(8,128)}), f32[128,8,128]{2,1,0:T(8,128)S(1)}, u32[]{:S(2)}, u32[]{:S(2)}) async-start(f32[128,8,128]{2,1,0:T(8,128)} %bitcast.7), calls=%async_computation.1 | async-start | bytes 1048576 | tf_op jit(solution)/shard_map/all_to_all | solution.py:814
where the time goes:
time: 101 us
  Pallas kernels  44 us (44%)
  starting transfers between devices  21.3 us (21%)
  blocking collectives  17.8 us (18%)
  local copies, waits for them, and re-layouts  9.44 us (9%)
  waiting for transfers between devices  6.12 us (6%)
  other arithmetic  1.89 us (2%)
    all_to_all x2, starting transfers between devices, exchange(): lax.all_to_all(array, ('bx', 'by'), split_axis=0, concat_axis=0, tiled=True)  21.3 us
    all_to_all x1, blocking collectives, exchange(): lax.all_to_all(array, ('bx', 'by'), split_axis=0, concat_axis=0, tiled=True)  17.8 us
    pallas_call x1, Pallas kernels, inner_levels(): pl.pallas_call(inner_kernel, out_shape=jax.ShapeDtypeStruct((1024, 128),...  17.6 us
    pallas_call x1, Pallas kernels, inner_turns(): pl.pallas_call(inner_turns_kernel, out_shape=[jax.ShapeDtypeStruct((128,...  12.6 us
    pallas_call x1, Pallas kernels, outer_levels(): pl.pallas_call(outer_kernel, out_shape=jax.ShapeDtypeStruct((1024, 128),...  7.73 us
    all_to_all x2, waiting for transfers between devices, exchange(): lax.all_to_all(array, ('bx', 'by'), split_axis=0, concat_axis=0, tiled=True)  6.12 us
    pallas_call x1, Pallas kernels, outer_turns(): pl.pallas_call(outer_turns_kernel, out_shape=jax.ShapeDtypeStruct((240, 2...  6.11 us
    unnamed x15, local copies, waits for them, and re-layouts  5.52 us
  transfers between devices with their start and end apart: 2, of which 1 were waited for; matrix products, arithmetic and copies ran while one was open for 2% of the time, Pallas kernels for 19%

commit v1 on v0

--- a/solution.py
+++ b/solution.py
@@ -223,29 +223,34 @@
 def level(read, table, first_line, high, low, matrix, children, rows):
     sources = 4 if children == 4 else 2
     pairs = rows // 2
+
+    def step(index, carry):
+        source = index // pairs
+        pair = index % pairs
+        lanes = pl.ds(pl.multiple_of(source * BOX_NODES, BOX_NODES), BOX_NODES)
+        group = source * rows + 2 * pair
+        real, imaginary = (
+            jnp.concatenate([read(group, part), read(group + 1, part)]) for part in range(2)
+        )
+        for child in range(children):
+            line = first_line + index * children + child
+            cosine = table[line, 0]
+            sine = table[line, 1]
+            for part, value in enumerate(
+                (real * cosine - imaginary * sine, real * sine + imaginary * cosine)
+            ):
+                place = pl.multiple_of((child * 2 + part) * rows * 8 + pair * 16, 16)
+                value_high, value_low = split(value)
+                high[pl.ds(place, 16), lanes] = value_high
+                low[pl.ds(place, 16), lanes] = value_low
+        return carry
+
+    lax.fori_loop(0, sources * pairs, step, 0)
+    pieces = []
     for source in range(sources):
         lanes = slice(source * BOX_NODES, (source + 1) * BOX_NODES)
-        for pair in range(pairs):
-            group = source * rows + 2 * pair
-            real, imaginary = (
-                jnp.concatenate([read(group, part), read(group + 1, part)]) for part in range(2)
-            )
-            for child in range(children):
-                line = first_line + (source * pairs + pair) * children + child
-                cosine = table[line, 0]
-                sine = table[line, 1]
-                for part, value in enumerate(
-                    (real * cosine - imaginary * sine, real * sine + imaginary * cosine)
-                ):
-                    place = (child * 2 + part) * rows * 8 + pair * 16
-                    value_high, value_low = split(value)
-                    high[place : place + 16, lanes] = value_high
-                    low[place : place + 16, lanes] = value_low
-        operand = jnp.concatenate([high[:, lanes], low[:, lanes], high[:, lanes]], axis=1)
-        weights = matrix[source * 768 : (source + 1) * 768, :]
-        part = jnp.dot(operand, weights, preferred_element_type=F32)
-        total = part if source == 0 else total + part
-    return total
+        pieces += [high[:, lanes], low[:, lanes], high[:, lanes]]
+    return jnp.dot(jnp.concatenate(pieces, axis=1), matrix[...], preferred_element_type=F32)
 
 
 def three_parts(matrix):
@@ -260,28 +265,31 @@
     return [bit(row, 2 - k).astype(F32) for k in range(3)]
 
 
-def find_mask(slots, mask, high_hot, low_hot, total):
+def find_mask(slots, mask, columns, high_hot, low_hot, total):
     iota = lax.broadcasted_iota(jnp.int32, (16, 128), 0).astype(F32)
     rows = [(iota + 16.0 * k).astype(BF16) for k in range(8)]
+    lane = lax.broadcasted_iota(jnp.int32, (128, 128), 1).astype(F32).astype(BF16)
     one = jnp.ones((16, 128), BF16)
     zero = jnp.zeros((16, 128), BF16)
+    ones = jnp.ones((128, 128), BF16)
+    zeros = jnp.zeros((128, 128), BF16)
     total[...] = jnp.zeros_like(total)
+    block = jnp.concatenate([slots[:128, :], slots[128:, :]], axis=1)
+    columns[0] = (block >> 7).astype(F32)
+    columns[1] = (block & 127).astype(F32).T
 
     def step(index, carry):
-        block = slots[pl.ds(pl.multiple_of(index * 16, 16), 16), :]
-        block = jnp.concatenate([block[:8], block[8:]], axis=1)
-        high = (block >> 7).astype(F32)
-        low = (block & 127).astype(F32)
+        high = columns[0, pl.ds(pl.multiple_of(index * 8, 8), 8), :]
+        low = pltpu.roll(columns[1], lax.rem(128 - index * 8, 128), 1)
         for k in range(8):
-            for source, hot in ((high, high_hot), (low, low_hot)):
-                value = jnp.broadcast_to(source[k : k + 1], (16, 128)).astype(BF16)
-                for place in range(8):
-                    hot[16 * place : 16 * (place + 1), 128 * k : 128 * (k + 1)] = jnp.where(
-                        value == rows[place], one, zero
-                    )
-        total[...] += lax.dot_general(
-            high_hot[...], low_hot[...], (((1,), (1,)), ((), ())), preferred_element_type=F32
-        )
+            value = jnp.broadcast_to(high[k : k + 1], (16, 128)).astype(BF16)
+            for place in range(8):
+                high_hot[16 * place : 16 * (place + 1), 128 * k : 128 * (k + 1)] = jnp.where(
+                    value == rows[place], one, zero
+                )
+            value = jnp.broadcast_to(low[:, k : k + 1], (128, 128)).astype(BF16)
+            low_hot[128 * k : 128 * (k + 1), :] = jnp.where(value == lane, ones, zeros)
+        total[...] += jnp.dot(high_hot[...], low_hot[...], preferred_element_type=F32)
         return carry
 
     lax.fori_loop(0, 16, step, 0)
@@ -309,6 +317,7 @@
     node,
     speeds,
     table,
+    columns,
     high_hot,
     low_hot,
     total,
@@ -324,7 +333,7 @@
     for fetch in fetches:
         fetch.start()
     fetches[0].wait()
-    find_mask(slots, mask, high_hot, low_hot, total)
+    find_mask(slots, mask, columns, high_hot, low_hot, total)
     for fetch in fetches[1:]:
         fetch.wait()
     stores = [store_level(table, table_far, leave, k) for k in range(4)]
@@ -458,8 +467,9 @@
         cells[0, rows, :] = jnp.bitwise_and(whole_second, 15).astype(F32)
         x = [bit(whole_first, 5 + k) for k in range(4)]
         y = [bit(whole_second, 4 + k) for k in range(4)]
-        cells[1, rows, :] = (x[0] * 8 + y[0] * 4 + x[1] * 2 + y[1]).astype(F32)
-        cells[2, rows, :] = (y[3] * 8 + x[2] * 4 + y[2] * 2 + x[3]).astype(F32)
+        high = x[0] * 128 + y[0] * 64 + x[1] * 32 + y[1] * 16
+        low = y[3] * 8 + x[2] * 4 + y[2] * 2 + x[3]
+        cells[1, rows, :] = (high + low).astype(F32)
         away = [place - value for value in points]
         before = [None] * NODES
         after = [None] * NODES
@@ -480,38 +490,32 @@
         return carry
 
     lax.fori_loop(0, 8, source_step, 0)
-
-    iota = lax.broadcasted_iota(jnp.int32, (16, 128), 0).astype(F32).astype(BF16)
-    one = jnp.ones((16, 128), BF16)
-    zero = jnp.zeros((16, 128), BF16)
+    cells[1] = cells[1].T
+
+    lanes_low = lax.broadcasted_iota(jnp.int32, (128, 128), 1).astype(F32)
+    lanes_high = (lanes_low + 128.0).astype(BF16)
+    lanes_low = lanes_low.astype(BF16)
+    one = jnp.ones((128, 128), BF16)
+    zero = jnp.zeros((128, 128), BF16)
     both = jnp.zeros((32, 128), BF16)
 
     def build(chunk, hot, spread):
+        boxes = pltpu.roll(cells[1], lax.rem(128 - chunk * 8, 128), 1)
         for k in range(8):
             sender = chunk * 8 + k
             lanes = slice(128 * k, 128 * (k + 1))
-
-            def row(number, height):
-                value = cells[number, pl.ds(sender, 1), :]
-                return jnp.broadcast_to(value, (height, 128)).astype(BF16)
-
             value = wide[pl.ds(pl.multiple_of(sender * 32, 32), 32), :].astype(BF16)
-            cell = row(0, 32)
+            cell = jnp.broadcast_to(cells[0, pl.ds(sender, 1), :], (32, 128)).astype(BF16)
             for c in range(16):
                 spread[32 * c : 32 * (c + 1), lanes] = jnp.where(
                     cell == jnp.full((32, 128), c, BF16), value, both
                 )
-            inside = jnp.where(row(2, 16) == iota, one, zero)
-            above = row(1, 16)
-            for c in range(16):
-                hot[16 * c : 16 * (c + 1), lanes] = jnp.where(
-                    above == jnp.full((16, 128), c, BF16), inside, zero
-                )
+            box = jnp.broadcast_to(boxes[:, k : k + 1], (128, 128)).astype(BF16)
+            hot[lanes, :128] = jnp.where(box == lanes_low, one, zero)
+            hot[lanes, 128:] = jnp.where(box == lanes_high, one, zero)
 
     def add(hot, spread):
-        grid[...] += lax.dot_general(
-            spread[...], hot[...], (((1,), (1,)), ((), ())), preferred_element_type=F32
-        )
+        grid[...] += jnp.dot(spread[...], hot[...], preferred_element_type=F32)
 
     grid[...] = jnp.zeros_like(grid)
     build(0, hots[0], spreads[0])
@@ -557,9 +561,10 @@
     mask,
     second_far,
     table_far,
-    matrix,
+    matrix_far,
     out,
     second,
+    matrix,
     table,
     arrive,
     wide,
@@ -577,7 +582,10 @@
     fetches = [fetch_level(table_far, table, arrive, k) for k in range(4)]
     for fetch in fetches:
         fetch.start()
+    fetch_matrix = pltpu.make_async_copy(matrix_far, matrix, arrive.at[5])
+    fetch_matrix.start()
     deposit(arrived, mask, second, fetch_second, state, wide, cells, hots, spreads, grid)
+    fetch_matrix.wait()
 
     def run(number, read):
         fetches[number - 1].wait()
@@ -617,15 +625,19 @@
 
 
 def outer_kernel(
-    arrived, table_far, matrix, last_far, out, table, last, arrive, state, turned, high, low
+    arrived, table_far, matrix_far, last_far, out, table, matrix, last, arrive, state, turned, high, low
 ):
     fetches = [
         fetch_level(table_far, table, arrive, k, 64 if k < 3 else 48) for k in range(4)
     ]
     fetch_last = pltpu.make_async_copy(last_far, last, arrive.at[4])
-    for fetch in fetches:
+    fetch_matrix = pltpu.make_async_copy(matrix_far, matrix, arrive.at[5])
+    fetches[0].start()
+    fetch_matrix.start()
+    for fetch in fetches[1:]:
         fetch.start()
     fetch_last.start()
+    fetch_matrix.wait()
 
     def first_read(group, part):
         i2, j3, i1, i0, j2 = bits(group, 5)
@@ -697,7 +709,7 @@
 
 
 def far(count):
-    return [pl.BlockSpec(memory_space=pl.ANY)] * count
+    return [pl.BlockSpec(memory_space=pltpu.HBM)] * count
 
 
 def inner_turns(block, slots):
@@ -715,8 +727,9 @@
             pltpu.VMEM((16, 256), F32),
             pltpu.VMEM((1024, 128), F32),
             pltpu.VMEM((256, 2, 16, 256), F32),
+            pltpu.VMEM((2, 128, 128), F32),
             pltpu.VMEM((128, 1024), BF16),
-            pltpu.VMEM((128, 1024), BF16),
+            pltpu.VMEM((1024, 128), BF16),
             pltpu.VMEM((128, 128), F32),
             pltpu.SemaphoreType.DMA((3,)),
             pltpu.SemaphoreType.DMA((4,)),
@@ -755,15 +768,16 @@
     return pl.pallas_call(
         inner_kernel,
         out_shape=jax.ShapeDtypeStruct((1024, 128), F32),
-        in_specs=vmem(2) + far(2) + vmem(1),
+        in_specs=vmem(2) + far(3),
         out_specs=vmem(1)[0],
         scratch_shapes=[
             pltpu.VMEM((1536, 512), BF16),
+            pltpu.VMEM((3072, 256), BF16),
             pltpu.VMEM((256, 2, 16, 256), F32),
-            pltpu.SemaphoreType.DMA((5,)),
+            pltpu.SemaphoreType.DMA((6,)),
             pltpu.VMEM((4096, 128), F32),
-            pltpu.VMEM((3, 128, 128), F32),
-            [pltpu.VMEM((256, 1024), BF16)] * 2,
+            pltpu.VMEM((2, 128, 128), F32),
+            [pltpu.VMEM((1024, 256), BF16)] * 2,
             [pltpu.VMEM((512, 1024), BF16)] * 2,
             pltpu.VMEM((512, 256), F32),
         ]
@@ -783,12 +797,13 @@
     return pl.pallas_call(
         outer_kernel,
         out_shape=jax.ShapeDtypeStruct((1024, 128), F32),
-        in_specs=vmem(1) + far(1) + vmem(1) + far(1),
+        in_specs=vmem(1) + far(3),
         out_specs=vmem(1)[0],
         scratch_shapes=[
             pltpu.VMEM((240, 2, 16, 256), F32),
+            pltpu.VMEM((3072, 256), BF16),
             pltpu.VMEM((1536, 256), BF16),
-            pltpu.SemaphoreType.DMA((5,)),
+            pltpu.SemaphoreType.DMA((6,)),
         ]
         + LEVEL_SCRATCH,
         name="outer",

time: 101 us -> 109 us (1.079)
  Pallas kernels: 44 us -> 52.1 us
    pallas_call x1, Pallas kernels: 17.6 us -> 21.3 us  [inner_levels(): pl.pallas_call(inner_kernel, out_shape=jax.ShapeDtypeStruct((1024, 128),...]
    pallas_call x1, Pallas kernels: 7.73 us -> 10.3 us  [outer_levels(): pl.pallas_call(outer_kernel, out_shape=jax.ShapeDtypeStruct((1024, 128),...]
    pallas_call x1, Pallas kernels: 12.6 us -> 14.5 us  [inner_turns(): pl.pallas_call(inner_turns_kernel, out_shape=[jax.ShapeDtypeStruct((128,...]
where the time goes in v1:
time: 109 us
  Pallas kernels  52.1 us (48%)
  starting transfers between devices  21.3 us (20%)
  blocking collectives  17.8 us (16%)
  local copies, waits for them, and re-layouts  9.44 us (9%)
  waiting for transfers between devices  6.13 us (6%)
  other arithmetic  1.89 us (2%)
    pallas_call x1, Pallas kernels, inner_levels(): pl.pallas_call(inner_kernel, out_shape=jax.ShapeDtypeStruct((1024, 128),...  21.3 us
    all_to_all x2, starting transfers between devices, exchange(): lax.all_to_all(array, ('bx', 'by'), split_axis=0, concat_axis=0, tiled=True)  21.3 us
    all_to_all x1, blocking collectives, exchange(): lax.all_to_all(array, ('bx', 'by'), split_axis=0, concat_axis=0, tiled=True)  17.8 us
    pallas_call x1, Pallas kernels, inner_turns(): pl.pallas_call(inner_turns_kernel, out_shape=[jax.ShapeDtypeStruct((128,...  14.5 us
    pallas_call x1, Pallas kernels, outer_levels(): pl.pallas_call(outer_kernel, out_shape=jax.ShapeDtypeStruct((1024, 128),...  10.3 us
    all_to_all x2, waiting for transfers between devices, exchange(): lax.all_to_all(array, ('bx', 'by'), split_axis=0, concat_axis=0, tiled=True)  6.13 us
    pallas_call x1, Pallas kernels, outer_turns(): pl.pallas_call(outer_turns_kernel, out_shape=jax.ShapeDtypeStruct((240, 2...  6.11 us
    unnamed x15, local copies, waits for them, and re-layouts  5.52 us
  transfers between devices with their start and end apart: 2, of which 1 were waited for; matrix products, arithmetic and copies ran while one was open for 2% of the time, Pallas kernels for 19%

profile of v1, /device:TPU:1, one launch (start us, length us, event | category | flops | bytes accessed | tf_op | source)
XLA Modules:
  0.0 108.9 jit_solution(16769131921030164946)
XLA Ops:
  0.0 1.0 convert_element_type.7
  1.0 0.1 copy.12
  1.1 1.0 copy.13
  2.1 0.8 maximum_bitcast_fusion
  2.9 0.0 copy-start.6
  2.9 11.5 %all-to-all-start = ((f32[128,4,128]{2,1,0:T(4,128)}), f32[128,4,128]{2,1,0:T(4,128)S(1)}, u32[]{:S(2)}, u32[]{:S(2)}) async-start(f32[128,4,128]{2,1,0:T(4,128)} %maximum_bitcast_fusion), calls=%async_computation | async-start | bytes 524288 | tf_op jit(solution)/shard_map/all_to_all | solution.py:829
  14.5 0.9 copy.14
  15.4 0.1 pad_add_fusion.block
  15.5 0.0 copy-start.4
  15.5 1.0 copy-done.4
  16.5 0.0 copy-start.5
  16.5 0.7 copy-done.5
  17.3 14.5 %inner_turns.1 = (f32[128,128]{1,0:T(8,128)S(1)}, f32[256,2,16,256]{3,2,1,0:T(8,128)}) custom-call(s32[2]{0:T(128)S(1)} %pad_add_fusion.block, s32[256,64]{1,0:T(8,128)S(1)} %bitcast.18, f32[16,256]{1,0:T(8,128)S(1)} %copy-done.5, f32[1024,128]{1,0:T(8,128)S(1)} %copy-done.4), custom_call_target="tpu_custom_call" | custom-call | tf_op jit(solution)/shard_map/inner_turns/pallas_call | solution.py:717
  31.8 0.0 all-to-all-done
  31.8 0.0 copy-start
  31.8 1.4 %copy-done = bf16[3072,256]{1,0:T(8,128)(2,1)S(1)} copy-done((bf16[3072,256]{1,0:T(8,128)(2,1)S(1)}, bf16[3072,256]{1,0:T(8,128)(2,1)}, u32[]{:S(2)}) %copy-start) | copy-done | bytes 1572888
  33.2 0.0 copy-start.2
  33.2 1.4 %copy-done.2 = bf16[1536,512]{1,0:T(8,128)(2,1)S(1)} copy-done((bf16[1536,512]{1,0:T(8,128)(2,1)S(1)}, bf16[1536,512]{1,0:T(8,128)(2,1)}, u32[]{:S(2)}) %copy-start.2) | copy-done | bytes 1572888
  34.6 21.3 %inner.1 = f32[1024,128]{1,0:T(8,128)} custom-call(f32[512,128]{1,0:T(8,128)S(1)} %bitcast.17, f32[128,128]{1,0:T(8,128)S(1)} %get-tuple-element.13.mask, bf16[1536,512]{1,0:T(8,128)(2,1)S(1)} %copy-done.2, f32[256,2,16,256]{3,2,1,0:T(8,128)} %get-tuple-element.14.table_far, bf16[3072,256]{1,0:T(8,128)(2,1)S(1)} %copy-done), custom_call_target="tpu_custom_call" | custom-call | tf_op jit(solution)/shard_map/inner/pallas_call | solution.py:768
  55.9 0.0 copy-start.1
  55.9 0.0 copy-start.3
  55.9 9.8 %all-to-all-start.1 = ((f32[128,8,128]{2,1,0:T(8,128)}), f32[128,8,128]{2,1,0:T(8,128)S(1)}, u32[]{:S(2)}, u32[]{:S(2)}) async-start(f32[128,8,128]{2,1,0:T(8,128)} %bitcast.7), calls=%async_computation.1 | async-start | bytes 1048576 | tf_op jit(solution)/shard_map/all_to_all | solution.py:829
  65.7 0.9 dynamic-slice_reduce_fusion
  66.6 0.3 broadcast_in_dim.9.speeds
  66.9 0.0 copy-done.6
  66.9 6.1 %outer_turns.1.table_far = f32[240,2,16,256]{3,2,1,0:T(8,128)} custom-call(f32[16,256]{1,0:T(8,128)S(1)} %copy-done.6, f32[1792,128]{1,0:T(8,128)S(1)} %broadcast_in_dim.9.speeds), custom_call_target="tpu_custom_call" | custom-call | tf_op jit(solution)/shard_map/outer_turns/pallas_call | solution.py:743
  73.0 6.1 %all-to-all-done.1 = f32[128,8,128]{2,1,0:T(8,128)S(1)} async-done(((f32[128,8,128]{2,1,0:T(8,128)}), f32[128,8,128]{2,1,0:T(8,128)S(1)}, u32[]{:S(2)}, u32[]{:S(2)}) %all-to-all-start.1) | async-done | bytes 524320 | tf_op jit(solution)/shard_map/all_to_all | solution.py:829
  79.1 0.0 copy-done.1
  79.1 0.0 copy-done.3
  79.1 10.3 %outer.1 = f32[1024,128]{1,0:T(8,128)S(1)} custom-call(f32[1024,128]{1,0:T(8,128)S(1)} %bitcast.15, f32[240,2,16,256]{3,2,1,0:T(8,128)} %outer_turns.1.table_far, bf16[3072,256]{1,0:T(8,128)(2,1)S(1)} %copy-done.1, bf16[1536,256]{1,0:T(8,128)(2,1)S(1)} %copy-done.3), custom_call_target="tpu_custom_call" | custom-call | tf_op jit(solution)/shard_map/outer/pallas_call | solution.py:797
  89.4 17.8 %all_to_all.15 = f32[128,8,128]{2,1,0:T(8,128)S(1)} all-to-all(f32[128,8,128]{2,1,0:T(8,128)S(1)} %bitcast.16), channel_id=1, replica_groups=mesh['bx'=8,'by'=16] {'bx','by'}, dimensions={0} | all-to-all | bytes 1048576 | tf_op jit(solution)/shard_map/all_to_all | solution.py:829
  107.2 0.3 copy.17
  107.5 1.4 %reshape.31 = f32[16,1,16,1,2,256]{5,4,3,2,1,0:T(2,128)} reshape(f32[16,16,2,2,128]{4,3,2,1,0:T(2,128)S(1)} %bitcast.20) | data formatting | bytes 1048576 | tf_op jit(solution)/shard_map/reshape | solution.py:849
Async XLA Ops:
  2.9 63.9 %copy-start.6 = (f32[16,256]{1,0:T(8,128)S(1)}, f32[16,256]{1,0:T(8,128)}, u32[]{:S(2)}) copy-start(f32[16,256]{1,0:T(8,128)} %constant.36.clone.node_far.node) | copy-start | bytes 49156
  2.9 28.8 %all-to-all-start = ((f32[128,4,128]{2,1,0:T(4,128)}), f32[128,4,128]{2,1,0:T(4,128)S(1)}, u32[]{:S(2)}, u32[]{:S(2)}) async-start(f32[128,4,128]{2,1,0:T(4,128)} %maximum_bitcast_fusion), calls=%async_computation | async-start | bytes 524288 | tf_op jit(solution)/shard_map/all_to_all | solution.py:829
  15.5 1.0 copy-start.4
  16.5 0.7 copy-start.5
  31.8 1.4 %copy-start = (bf16[3072,256]{1,0:T(8,128)(2,1)S(1)}, bf16[3072,256]{1,0:T(8,128)(2,1)}, u32[]{:S(2)}) copy-start(bf16[3072,256]{1,0:T(8,128)(2,1)} %constant.39.clone.matrix_far) | copy-start | bytes 4718596
  33.2 1.4 %copy-start.2 = (bf16[1536,512]{1,0:T(8,128)(2,1)S(1)}, bf16[1536,512]{1,0:T(8,128)(2,1)}, u32[]{:S(2)}) copy-start(bf16[1536,512]{1,0:T(8,128)(2,1)} %constant.38.clone.second_far) | copy-start | bytes 4718596
  55.9 23.2 %copy-start.1 = (bf16[3072,256]{1,0:T(8,128)(2,1)S(1)}, bf16[3072,256]{1,0:T(8,128)(2,1)}, u32[]{:S(2)}) copy-start(bf16[3072,256]{1,0:T(8,128)(2,1)} %constant.39.clone.matrix_far) | copy-start | bytes 4718596
  55.9 23.2 %copy-start.3 = (bf16[1536,256]{1,0:T(8,128)(2,1)S(1)}, bf16[1536,256]{1,0:T(8,128)(2,1)}, u32[]{:S(2)}) copy-start(bf16[1536,256]{1,0:T(8,128)(2,1)} %constant.41.clone.last_far) | copy-start | bytes 2359300
  55.9 23.2 %all-to-all-start.1 = ((f32[128,8,128]{2,1,0:T(8,128)}), f32[128,8,128]{2,1,0:T(8,128)S(1)}, u32[]{:S(2)}, u32[]{:S(2)}) async-start(f32[128,8,128]{2,1,0:T(8,128)} %bitcast.7), calls=%async_computation.1 | async-start | bytes 1048576 | tf_op jit(solution)/shard_map/all_to_all | solution.py:829

commit v2 on v0

--- a/solution.py
+++ b/solution.py
@@ -220,11 +220,13 @@
     lax.fori_loop(0, (4 if children == 4 else 2) * pairs, step, 0)
 
 
-def level(read, table, first_line, high, low, matrix, children, rows):
+def level(read, table, first_line, high, low, matrix, children, rows, ready, matrix_ready=None):
     sources = 4 if children == 4 else 2
     pairs = rows // 2
     for source in range(sources):
         lanes = slice(source * BOX_NODES, (source + 1) * BOX_NODES)
+        if source < len(ready):
+            ready[source].wait()
         for pair in range(pairs):
             group = source * rows + 2 * pair
             real, imaginary = (
@@ -241,11 +243,13 @@
                     value_high, value_low = split(value)
                     high[place : place + 16, lanes] = value_high
                     low[place : place + 16, lanes] = value_low
-        operand = jnp.concatenate([high[:, lanes], low[:, lanes], high[:, lanes]], axis=1)
-        weights = matrix[source * 768 : (source + 1) * 768, :]
-        part = jnp.dot(operand, weights, preferred_element_type=F32)
-        total = part if source == 0 else total + part
-    return total
+    pieces = []
+    for source in range(sources):
+        lanes = slice(source * BOX_NODES, (source + 1) * BOX_NODES)
+        pieces += [high[:, lanes], low[:, lanes], high[:, lanes]]
+    if matrix_ready is not None:
+        matrix_ready.wait()
+    return jnp.dot(jnp.concatenate(pieces, axis=1), matrix[...], preferred_element_type=F32)
 
 
 def three_parts(matrix):
@@ -255,36 +259,48 @@
     return np.stack([high, high, low], axis=1).reshape(-1, BOX_NODES)
 
 
+def matrices():
+    return np.concatenate([three_parts(stacked_matrix(2, 2)), three_parts(stacked_matrix(1, 2))])
+
+
 def sub_bits():
     row = lax.broadcasted_iota(jnp.int32, (8, BOX_NODES), 0)
     return [bit(row, 2 - k).astype(F32) for k in range(3)]
 
 
-def find_mask(slots, mask, high_hot, low_hot, total):
+def find_mask(slots, mask, entries, high_hot, low_hot, total):
     iota = lax.broadcasted_iota(jnp.int32, (16, 128), 0).astype(F32)
-    rows = [(iota + 16.0 * k).astype(BF16) for k in range(8)]
-    one = jnp.ones((16, 128), BF16)
-    zero = jnp.zeros((16, 128), BF16)
+    rows = [iota + 16.0 * k for k in range(8)]
+    block = jnp.concatenate([slots[:, :128], slots[:, 128:]], axis=0)
+    entries[0] = (block >> 7).astype(F32)
+    entries[1] = (block & 127).astype(F32)
+
+    def step(index, carry):
+        for source, hot in enumerate((high_hot, low_hot)):
+            block = entries[source, pl.ds(pl.multiple_of(index * 8, 8), 8), :]
+            for k in range(8):
+                value = jnp.broadcast_to(block[k : k + 1], (16, 128))
+                lanes = pl.ds(pl.multiple_of(index * 1024 + 128 * k, 128), 128)
+                for place in range(8):
+                    hot[16 * place : 16 * (place + 1), lanes] = jnp.where(
+                        value == rows[place], 1.0, 0.0
+                    ).astype(BF16)
+        return carry
+
+    lax.fori_loop(0, 16, step, 0)
     total[...] = jnp.zeros_like(total)
 
-    def step(index, carry):
-        block = slots[pl.ds(pl.multiple_of(index * 16, 16), 16), :]
-        block = jnp.concatenate([block[:8], block[8:]], axis=1)
-        high = (block >> 7).astype(F32)
-        low = (block & 127).astype(F32)
-        for k in range(8):
-            for source, hot in ((high, high_hot), (low, low_hot)):
-                value = jnp.broadcast_to(source[k : k + 1], (16, 128)).astype(BF16)
-                for place in range(8):
-                    hot[16 * place : 16 * (place + 1), 128 * k : 128 * (k + 1)] = jnp.where(
-                        value == rows[place], one, zero
-                    )
+    def add(index, carry):
+        lanes = pl.ds(pl.multiple_of(index * 4096, 4096), 4096)
         total[...] += lax.dot_general(
-            high_hot[...], low_hot[...], (((1,), (1,)), ((), ())), preferred_element_type=F32
+            high_hot[:, lanes],
+            low_hot[:, lanes],
+            (((1,), (1,)), ((), ())),
+            preferred_element_type=F32,
         )
         return carry
 
-    lax.fori_loop(0, 16, step, 0)
+    lax.fori_loop(0, 4, add, 0)
     mask[...] = jnp.where(total[...] > 0.5, 1.0, 0.0)
 
 
@@ -309,6 +325,7 @@
     node,
     speeds,
     table,
+    entries,
     high_hot,
     low_hot,
     total,
@@ -324,7 +341,7 @@
     for fetch in fetches:
         fetch.start()
     fetches[0].wait()
-    find_mask(slots, mask, high_hot, low_hot, total)
+    find_mask(slots, mask, entries, high_hot, low_hot, total)
     for fetch in fetches[1:]:
         fetch.wait()
     stores = [store_level(table, table_far, leave, k) for k in range(4)]
@@ -481,32 +498,27 @@
 
     lax.fori_loop(0, 8, source_step, 0)
 
-    iota = lax.broadcasted_iota(jnp.int32, (16, 128), 0).astype(F32).astype(BF16)
-    one = jnp.ones((16, 128), BF16)
-    zero = jnp.zeros((16, 128), BF16)
-    both = jnp.zeros((32, 128), BF16)
+    iota = lax.broadcasted_iota(jnp.int32, (16, 128), 0).astype(F32)
 
     def build(chunk, hot, spread):
-        for k in range(8):
-            sender = chunk * 8 + k
+        for k in range(16):
+            sender = chunk * 16 + k
             lanes = slice(128 * k, 128 * (k + 1))
 
-            def row(number, height):
-                value = cells[number, pl.ds(sender, 1), :]
-                return jnp.broadcast_to(value, (height, 128)).astype(BF16)
-
-            value = wide[pl.ds(pl.multiple_of(sender * 32, 32), 32), :].astype(BF16)
-            cell = row(0, 32)
+            def row(number):
+                return jnp.broadcast_to(cells[number, pl.ds(sender, 1), :], (8, 128))
+
+            values = wide[pl.ds(pl.multiple_of(sender * 32, 32), 32), :]
+            cell = row(0)
             for c in range(16):
-                spread[32 * c : 32 * (c + 1), lanes] = jnp.where(
-                    cell == jnp.full((32, 128), c, BF16), value, both
-                )
-            inside = jnp.where(row(2, 16) == iota, one, zero)
-            above = row(1, 16)
+                chosen = jnp.concatenate([cell == float(c)] * 4)
+                spread[32 * c : 32 * (c + 1), lanes] = jnp.where(chosen, values, 0.0).astype(BF16)
+            low = row(2)
+            inside = jnp.where(jnp.concatenate([low, low]) == iota, 1.0, 0.0)
+            above = row(1)
             for c in range(16):
-                hot[16 * c : 16 * (c + 1), lanes] = jnp.where(
-                    above == jnp.full((16, 128), c, BF16), inside, zero
-                )
+                chosen = jnp.concatenate([above == float(c)] * 2)
+                hot[16 * c : 16 * (c + 1), lanes] = jnp.where(chosen, inside, 0.0).astype(BF16)
 
     def add(hot, spread):
         grid[...] += lax.dot_general(
@@ -517,13 +529,13 @@
     build(0, hots[0], spreads[0])
 
     def spread_step(index, carry):
+        add(hots[0], spreads[0])
         build(2 * index + 1, hots[1], spreads[1])
-        add(hots[0], spreads[0])
-        build(jnp.minimum(2 * index + 2, 15), hots[0], spreads[0])
         add(hots[1], spreads[1])
+        build(jnp.minimum(2 * index + 2, 7), hots[0], spreads[0])
         return carry
 
-    lax.fori_loop(0, 8, spread_step, 0)
+    lax.fori_loop(0, 4, spread_step, 0)
 
     grid_high, grid_low = split(grid[...].T)
     fetch_second.wait()
@@ -557,9 +569,10 @@
     mask,
     second_far,
     table_far,
-    matrix,
+    matrix_far,
     out,
     second,
+    matrix,
     table,
     arrive,
     wide,
@@ -577,11 +590,23 @@
     fetches = [fetch_level(table_far, table, arrive, k) for k in range(4)]
     for fetch in fetches:
         fetch.start()
+    fetch_matrix = pltpu.make_async_copy(matrix_far.at[pl.ds(0, 3072)], matrix, arrive.at[5])
+    fetch_matrix.start()
     deposit(arrived, mask, second, fetch_second, state, wide, cells, hots, spreads, grid)
 
     def run(number, read):
-        fetches[number - 1].wait()
-        return level(read, table, 64 * (number - 1), high, low, matrix, 4, 8)
+        return level(
+            read,
+            table,
+            64 * (number - 1),
+            high,
+            low,
+            matrix,
+            4,
+            8,
+            fetches[number - 1 : number],
+            fetch_matrix if number == 1 else None,
+        )
 
     def read(group, part):
         return state[group, part]
@@ -617,15 +642,21 @@
 
 
 def outer_kernel(
-    arrived, table_far, matrix, last_far, out, table, last, arrive, state, turned, high, low
+    arrived, table_far, matrix_far, out, table, matrix, last, arrive, state, turned, high, low
 ):
+    first = [
+        pltpu.make_async_copy(
+            table_far.at[pl.ds(16 * k, 16)], table.at[pl.ds(16 * k, 16)], arrive.at[6 + k]
+        )
+        for k in range(4)
+    ]
     fetches = [
-        fetch_level(table_far, table, arrive, k, 64 if k < 3 else 48) for k in range(4)
+        fetch_level(table_far, table, arrive, k, 64 if k < 3 else 48) for k in range(1, 4)
     ]
-    fetch_last = pltpu.make_async_copy(last_far, last, arrive.at[4])
-    for fetch in fetches:
+    fetch_matrix = pltpu.make_async_copy(matrix_far.at[pl.ds(0, 3072)], matrix, arrive.at[5])
+    fetch_last = pltpu.make_async_copy(matrix_far.at[pl.ds(3072, 1536)], last, arrive.at[4])
+    for fetch in first + [fetch_matrix] + fetches + [fetch_last]:
         fetch.start()
-    fetch_last.start()
 
     def first_read(group, part):
         i2, j3, i1, i0, j2 = bits(group, 5)
@@ -639,8 +670,18 @@
         )
 
     def run(number, read):
-        fetches[number - 5].wait()
-        return level(read, table, 64 * (number - 5), high, low, matrix, 4, 8)
+        return level(
+            read,
+            table,
+            64 * (number - 5),
+            high,
+            low,
+            matrix,
+            4,
+            8,
+            first if number == 5 else fetches[number - 6 : number - 5],
+            fetch_matrix if number == 5 else None,
+        )
 
     def read(group, part):
         return state[group, part]
@@ -666,9 +707,7 @@
         for part in range(2):
             state[j0 * 16 + x * 8 + y * 4 + t6x * 2 + pair, part] = values[part]
 
-    fetches[3].wait()
-    fetch_last.wait()
-    result = level(read, table, 192, high, low, last, 2, 16)
+    result = level(read, table, 192, high, low, last, 2, 16, fetches[2:], fetch_last)
     for child in range(2):
         for row in range(16):
             t7x, t7y, t6x, pair = bits(row, 4)
@@ -697,7 +736,42 @@
 
 
 def far(count):
-    return [pl.BlockSpec(memory_space=pl.ANY)] * count
+    return [pl.BlockSpec(memory_space=pltpu.HBM)] * count
+
+
+def payload_kernel(place_far, amp_far, out_far, place, amp, out, arrive, leave):
+    fetches = [
+        pltpu.make_async_copy(place_far, place, arrive.at[0]),
+        pltpu.make_async_copy(amp_far, amp, arrive.at[1]),
+    ]
+    for fetch in fetches:
+        fetch.start()
+    for fetch in fetches:
+        fetch.wait()
+    for k in range(2):
+        out[pl.ds(k, DEVICES, stride=4), :] = place[k].astype(F32)
+        out[pl.ds(2 + k, DEVICES, stride=4), :] = amp[k]
+    store = pltpu.make_async_copy(out, out_far, leave)
+    store.start()
+    store.wait()
+
+
+def make_payload(place, amp):
+    return pl.pallas_call(
+        payload_kernel,
+        out_shape=jax.ShapeDtypeStruct((4 * DEVICES, 128), F32),
+        in_specs=far(2),
+        out_specs=far(1)[0],
+        scratch_shapes=[
+            pltpu.VMEM((2, DEVICES, 128), jnp.int32),
+            pltpu.VMEM((2, DEVICES, 128), F32),
+            pltpu.VMEM((4 * DEVICES, 128), F32),
+            pltpu.SemaphoreType.DMA((2,)),
+            pltpu.SemaphoreType.DMA,
+        ],
+        name="payload",
+        compiler_params=pltpu.CompilerParams(vmem_limit_bytes=60 << 20),
+    )(place, amp)
 
 
 def inner_turns(block, slots):
@@ -711,18 +785,19 @@
         in_specs=smem(1) + far(3),
         out_specs=vmem(1) + far(1),
         scratch_shapes=[
-            pltpu.VMEM((256, 64), jnp.int32),
+            pltpu.VMEM((64, 256), jnp.int32),
             pltpu.VMEM((16, 256), F32),
             pltpu.VMEM((1024, 128), F32),
             pltpu.VMEM((256, 2, 16, 256), F32),
-            pltpu.VMEM((128, 1024), BF16),
-            pltpu.VMEM((128, 1024), BF16),
+            pltpu.VMEM((2, 128, 128), F32),
+            pltpu.VMEM((128, 16384), BF16),
+            pltpu.VMEM((128, 16384), BF16),
             pltpu.VMEM((128, 128), F32),
             pltpu.SemaphoreType.DMA((3,)),
             pltpu.SemaphoreType.DMA((4,)),
         ],
         name="inner_turns",
-        compiler_params=pltpu.CompilerParams(vmem_limit_bytes=48 << 20),
+        compiler_params=pltpu.CompilerParams(vmem_limit_bytes=60 << 20),
     )(block, slots, jnp.asarray(node_tables()), jnp.asarray(speeds))
 
 
@@ -737,7 +812,7 @@
             pltpu.SemaphoreType.DMA((4,)),
         ],
         name="outer_turns",
-        compiler_params=pltpu.CompilerParams(vmem_limit_bytes=48 << 20),
+        compiler_params=pltpu.CompilerParams(vmem_limit_bytes=59 << 20),
     )(jnp.asarray(node_tables()), speeds)
 
 
@@ -755,27 +830,28 @@
     return pl.pallas_call(
         inner_kernel,
         out_shape=jax.ShapeDtypeStruct((1024, 128), F32),
-        in_specs=vmem(2) + far(2) + vmem(1),
+        in_specs=vmem(2) + far(3),
         out_specs=vmem(1)[0],
         scratch_shapes=[
             pltpu.VMEM((1536, 512), BF16),
+            pltpu.VMEM((3072, 256), BF16),
             pltpu.VMEM((256, 2, 16, 256), F32),
-            pltpu.SemaphoreType.DMA((5,)),
+            pltpu.SemaphoreType.DMA((6,)),
             pltpu.VMEM((4096, 128), F32),
             pltpu.VMEM((3, 128, 128), F32),
-            [pltpu.VMEM((256, 1024), BF16)] * 2,
-            [pltpu.VMEM((512, 1024), BF16)] * 2,
+            [pltpu.VMEM((256, 2048), BF16)] * 2,
+            [pltpu.VMEM((512, 2048), BF16)] * 2,
             pltpu.VMEM((512, 256), F32),
         ]
         + LEVEL_SCRATCH,
         name="inner",
-        compiler_params=pltpu.CompilerParams(vmem_limit_bytes=48 << 20),
+        compiler_params=pltpu.CompilerParams(vmem_limit_bytes=59 << 20),
     )(
         arrived,
         mask,
         jnp.asarray(second),
         table,
-        jnp.asarray(three_parts(stacked_matrix(2, 2))),
+        jnp.asarray(matrices()),
     )
 
 
@@ -783,21 +859,21 @@
     return pl.pallas_call(
         outer_kernel,
         out_shape=jax.ShapeDtypeStruct((1024, 128), F32),
-        in_specs=vmem(1) + far(1) + vmem(1) + far(1),
+        in_specs=vmem(1) + far(2),
         out_specs=vmem(1)[0],
         scratch_shapes=[
             pltpu.VMEM((240, 2, 16, 256), F32),
+            pltpu.VMEM((3072, 256), BF16),
             pltpu.VMEM((1536, 256), BF16),
-            pltpu.SemaphoreType.DMA((5,)),
+            pltpu.SemaphoreType.DMA((10,)),
         ]
         + LEVEL_SCRATCH,
         name="outer",
-        compiler_params=pltpu.CompilerParams(vmem_limit_bytes=48 << 20),
+        compiler_params=pltpu.CompilerParams(vmem_limit_bytes=59 << 20),
     )(
         arrived,
         table,
-        jnp.asarray(three_parts(stacked_matrix(2, 2))),
-        jnp.asarray(three_parts(stacked_matrix(1, 2))),
+        jnp.asarray(matrices()),
     )
 
 
@@ -819,10 +895,9 @@
     row = lax.axis_index("by")
     device = column * BY + row
     block = jnp.stack([reverse_bits(column, 3), reverse_bits(row, 4)]).astype(jnp.int32)
-    payload = jnp.concatenate([src_pos[:, 0, :].astype(F32), src_amp[:, 0, :]], axis=0)
-    payload = payload.reshape(4, DEVICES, 128).transpose(1, 0, 2)
-    arrived = exchange(payload).reshape(512, 128)
-    mask, table = inner_turns(block, box_slots[0])
+    payload = make_payload(src_pos.reshape(2, DEVICES, 128), src_amp.reshape(2, DEVICES, 128))
+    arrived = exchange(payload.reshape(DEVICES, 4, 128)).reshape(512, 128)
+    mask, table = inner_turns(block, box_slots[0].T)
     arrived, mask, table = lax.optimization_barrier((arrived, mask, table))
     weights = inner_levels(arrived, mask, table)
     weights = exchange(weights.reshape(DEVICES, 8, 128)).reshape(1024, 128)
@@ -830,7 +905,8 @@
     speeds = jnp.broadcast_to(speeds[:, None], (7 * 256, 128))
     weights = outer_levels(weights, outer_turns(speeds))
     weights = exchange(weights.reshape(DEVICES, 8, 128))
-    weights = weights.reshape(LEAVES, LEAVES, 2, 2, 128).transpose(0, 1, 3, 2, 4)
+    weights = weights.reshape(LEAVES, LEAVES, 2, 2, 128)
+    weights = jnp.concatenate([weights[:, :, 0], weights[:, :, 1]], axis=-1)
     return weights.reshape(LEAVES, 1, LEAVES, 1, 2, BOX_NODES)
 
 

time: 101 us -> 103 us (1.020)
  Pallas kernels: 44 us -> 52.2 us
  local copies, waits for them, and re-layouts: 9.44 us -> 3.99 us
  waiting for transfers between devices: 6.12 us -> 3.89 us
  blocking collectives: 17.8 us -> 19.3 us
    unnamed x15 -> x4, local copies, waits for them, and re-layouts: 5.52 us -> 1.51 us
    pallas_call x1, Pallas kernels: 7.73 us -> 10.3 us  [outer_levels(): pl.pallas_call(outer_kernel, out_shape=jax.ShapeDtypeStruct((1024, 128),...]
    all_to_all x2, waiting for transfers between devices: 6.12 us -> 3.89 us  [exchange(): lax.all_to_all(array, ('bx', 'by'), split_axis=0, concat_axis=0, tiled=True)]
    pallas_call x1, Pallas kernels: 17.6 us -> 19.8 us  [inner_levels(): pl.pallas_call(inner_kernel, out_shape=jax.ShapeDtypeStruct((1024, 128),...]
    pallas_call x0 -> x1, Pallas kernels: none -> 1.72 us  [make_payload(): pl.pallas_call(payload_kernel, out_shape=jax.ShapeDtypeStruct((4 * DEVICE...]
    reshape x2 -> x0, local copies, waits for them, and re-layouts: 1.66 us -> none  [the longest x1 1.39 us: shards(): return weights.reshape(LEAVES, 1, LEAVES, 1, 2, BOX_NODES)]
    all_to_all x1, blocking collectives: 17.8 us -> 19.3 us  [exchange(): lax.all_to_all(array, ('bx', 'by'), split_axis=0, concat_axis=0, tiled=True)]
    pallas_call x1, Pallas kernels: 6.11 us -> 7.3 us  [outer_turns(): pl.pallas_call(outer_turns_kernel, out_shape=jax.ShapeDtypeStruct((240, 2...]
  transfers between devices with their start and end apart: 2 -> 2, of which waited for: 1 -> 1; matrix products, arithmetic and copies ran while one was open for 2% -> 3% of each run, Pallas kernels for 19% -> 20%
where the time goes in v2:
time: 103 us
  Pallas kernels  52.2 us (51%)
  starting transfers between devices  21.3 us (21%)
  blocking collectives  19.3 us (19%)
  local copies, waits for them, and re-layouts  3.99 us (4%)
  waiting for transfers between devices  3.89 us (4%)
  other arithmetic  1.69 us (2%)
    all_to_all x2, starting transfers between devices, exchange(): lax.all_to_all(array, ('bx', 'by'), split_axis=0, concat_axis=0, tiled=True)  21.3 us
    pallas_call x1, Pallas kernels, inner_levels(): pl.pallas_call(inner_kernel, out_shape=jax.ShapeDtypeStruct((1024, 128),...  19.8 us
    all_to_all x1, blocking collectives, exchange(): lax.all_to_all(array, ('bx', 'by'), split_axis=0, concat_axis=0, tiled=True)  19.3 us
    pallas_call x1, Pallas kernels, inner_turns(): pl.pallas_call(inner_turns_kernel, out_shape=[jax.ShapeDtypeStruct((128,...  13.1 us
    pallas_call x1, Pallas kernels, outer_levels(): pl.pallas_call(outer_kernel, out_shape=jax.ShapeDtypeStruct((1024, 128),...  10.3 us
    pallas_call x1, Pallas kernels, outer_turns(): pl.pallas_call(outer_turns_kernel, out_shape=jax.ShapeDtypeStruct((240, 2...  7.3 us
    all_to_all x2, waiting for transfers between devices, exchange(): lax.all_to_all(array, ('bx', 'by'), split_axis=0, concat_axis=0, tiled=True)  3.89 us
  transfers between devices with their start and end apart: 2, of which 1 were waited for; matrix products, arithmetic and copies ran while one was open for 3% of the time, Pallas kernels for 20%

profile of v2, /device:TPU:1, one launch (start us, length us, event | category | flops | bytes accessed | tf_op | source)
XLA Modules:
  0.0 102.5 jit_solution(8836655814023468003)
XLA Ops:
  0.0 1.7 %payload.1 = f32[512,128]{1,0:T(8,128)} custom-call(s32[2,128,128]{2,1,0:T(8,128)} %bitcast.29, f32[2,128,128]{2,1,0:T(8,128)} %bitcast.30), custom_call_target="tpu_custom_call" | custom-call | tf_op jit(solution)/shard_map/payload/pallas_call | solution.py:760
  1.7 11.5 %all-to-all-start = ((f32[128,4,128]{2,1,0:T(4,128)}), f32[128,4,128]{2,1,0:T(4,128)S(1)}, u32[]{:S(2)}, u32[]{:S(2)}) async-start(f32[128,4,128]{2,1,0:T(4,128)} %bitcast.28), calls=%async_computation | async-start | bytes 524288 | tf_op jit(solution)/shard_map/all_to_all | solution.py:890
  13.3 0.6 pad_add_fusion.block
  13.9 13.1 %inner_turns.1 = (f32[128,128]{1,0:T(8,128)}, f32[256,2,16,256]{3,2,1,0:T(8,128)}) custom-call(s32[2]{0:T(128)} %pad_add_fusion.block, s32[64,256]{1,0:T(8,128)} %bitcast.31, f32[16,256]{1,0:T(8,128)} %constant.34.clone.node_far.node, f32[1024,128]{1,0:T(8,128)} %constant.35.clone.speeds_far), custom_call_target="tpu_custom_call" | custom-call | tf_op jit(solution)/shard_map/inner_turns/pallas_call | solution.py:779
  27.1 0.0 all-to-all-done
  27.1 0.0 copy-start.1
  27.1 0.7 copy-done.1
  27.8 19.8 %inner.1 = f32[1024,128]{1,0:T(8,128)} custom-call(f32[512,128]{1,0:T(8,128)} %bitcast.27, f32[128,128]{1,0:T(8,128)} %get-tuple-element.13.mask, bf16[1536,512]{1,0:T(8,128)(2,1)} %constant.36.clone.second_far, f32[256,2,16,256]{3,2,1,0:T(8,128)} %get-tuple-element.14.table_far, bf16[4608,256]{1,0:T(8,128)(2,1)} %constant.37.clone.matrix_far), custom_call_target="tpu_custom_call" | custom-call | tf_op jit(solution)/shard_map/inner/pallas_call | solution.py:830
  47.6 9.8 %all-to-all-start.1 = ((f32[128,8,128]{2,1,0:T(8,128)}), f32[128,8,128]{2,1,0:T(8,128)S(1)}, u32[]{:S(2)}, u32[]{:S(2)}) async-start(f32[128,8,128]{2,1,0:T(8,128)} %bitcast.24), calls=%async_computation.1 | async-start | bytes 1048576 | tf_op jit(solution)/shard_map/all_to_all | solution.py:890
  57.4 0.9 dynamic-slice_reduce_fusion
  58.2 1.3 %broadcast_in_dim.9.speeds = f32[1792,128]{1,0:T(8,128)} broadcast(f32[1792]{0:T(1024)S(1)} %dynamic-slice_reduce_fusion), dimensions={0} | broadcast | bytes 924672 | tf_op jit(solution)/shard_map/broadcast_in_dim | solution.py:905
  59.6 7.3 %outer_turns.1.table_far = f32[240,2,16,256]{3,2,1,0:T(8,128)} custom-call(f32[16,256]{1,0:T(8,128)} %constant.34.clone.node_far.node, f32[1792,128]{1,0:T(8,128)} %broadcast_in_dim.9.speeds), custom_call_target="tpu_custom_call" | custom-call | tf_op jit(solution)/shard_map/outer_turns/pallas_call | solution.py:805
  66.9 3.9 %all-to-all-done.1 = f32[128,8,128]{2,1,0:T(8,128)S(1)} async-done(((f32[128,8,128]{2,1,0:T(8,128)}), f32[128,8,128]{2,1,0:T(8,128)S(1)}, u32[]{:S(2)}, u32[]{:S(2)}) %all-to-all-start.1) | async-done | bytes 524320 | tf_op jit(solution)/shard_map/all_to_all | solution.py:890
  70.8 0.0 copy-start
  70.8 0.8 copy-done
  71.6 10.3 %outer.1 = f32[1024,128]{1,0:T(8,128)} custom-call(f32[1024,128]{1,0:T(8,128)} %bitcast.23, f32[240,2,16,256]{3,2,1,0:T(8,128)} %outer_turns.1.table_far, bf16[4608,256]{1,0:T(8,128)(2,1)} %constant.37.clone.matrix_far), custom_call_target="tpu_custom_call" | custom-call | tf_op jit(solution)/shard_map/outer/pallas_call | solution.py:859
  81.9 19.3 %all_to_all.15 = f32[128,8,128]{2,1,0:T(8,128)S(1)} all-to-all(f32[128,8,128]{2,1,0:T(8,128)} %bitcast.25), channel_id=1, replica_groups=mesh['bx'=8,'by'=16] {'bx','by'}, dimensions={0} | all-to-all | bytes 1048576 | tf_op jit(solution)/shard_map/all_to_all | solution.py:890
  101.2 0.3 slice_bitcast_fusion.1
  101.5 1.0 %maximum_bitcast_fusion = f32[16,1,16,1,2,256]{5,4,3,2,1,0:T(2,128)} fusion(f32[16,16,2,128]{3,2,1,0:T(2,128)S(1)} %get-tuple-element.16, f32[16,16,2,128]{3,2,1,0:T(2,128)S(1)} %get-tuple-element.15), kind=kLoop, calls=%fused_computation | loop fusion | flops 131072 | bytes 1048576 | tf_op jit(solution)/shard_map/reshape | solution.py:910
Async XLA Ops:
  1.7 25.3 %all-to-all-start = ((f32[128,4,128]{2,1,0:T(4,128)}), f32[128,4,128]{2,1,0:T(4,128)S(1)}, u32[]{:S(2)}, u32[]{:S(2)}) async-start(f32[128,4,128]{2,1,0:T(4,128)} %bitcast.28), calls=%async_computation | async-start | bytes 524288 | tf_op jit(solution)/shard_map/all_to_all | solution.py:890
  27.1 0.7 copy-start.1
  47.6 23.2 %all-to-all-start.1 = ((f32[128,8,128]{2,1,0:T(8,128)}), f32[128,8,128]{2,1,0:T(8,128)S(1)}, u32[]{:S(2)}, u32[]{:S(2)}) async-start(f32[128,8,128]{2,1,0:T(8,128)} %bitcast.24), calls=%async_computation.1 | async-start | bytes 1048576 | tf_op jit(solution)/shard_map/all_to_all | solution.py:890
  70.8 0.8 copy-start

commit v3 on v2

--- a/solution.py
+++ b/solution.py
@@ -243,24 +243,23 @@
                     value_high, value_low = split(value)
                     high[place : place + 16, lanes] = value_high
                     low[place : place + 16, lanes] = value_low
-    pieces = []
-    for source in range(sources):
-        lanes = slice(source * BOX_NODES, (source + 1) * BOX_NODES)
-        pieces += [high[:, lanes], low[:, lanes], high[:, lanes]]
     if matrix_ready is not None:
         matrix_ready.wait()
-    return jnp.dot(jnp.concatenate(pieces, axis=1), matrix[...], preferred_element_type=F32)
-
-
-def three_parts(matrix):
-    high, low = two_parts(matrix)
-    high = high.reshape(-1, BOX_NODES, BOX_NODES)
-    low = low.reshape(-1, BOX_NODES, BOX_NODES)
-    return np.stack([high, high, low], axis=1).reshape(-1, BOX_NODES)
+    columns = sources * BOX_NODES
+    both = jnp.dot(high[:, :columns], matrix[...], preferred_element_type=F32)
+    rest = jnp.dot(low[:, :columns], matrix[:, :BOX_NODES], preferred_element_type=F32)
+    return both[:, :BOX_NODES] + (both[:, BOX_NODES:] + rest)
 
 
 def matrices():
-    return np.concatenate([three_parts(stacked_matrix(2, 2)), three_parts(stacked_matrix(1, 2))])
+    basis = second_basis()
+    rows = [
+        stacked_matrix(2, 2),
+        stacked_matrix(1, 2),
+        basis[:, :256],
+        basis[:, 256:],
+    ]
+    return np.concatenate(two_parts(np.concatenate(rows)), axis=1)
 
 
 def sub_bits():
@@ -270,7 +269,9 @@
 
 def find_mask(slots, mask, entries, high_hot, low_hot, total):
     iota = lax.broadcasted_iota(jnp.int32, (16, 128), 0).astype(F32)
-    rows = [iota + 16.0 * k for k in range(8)]
+    rows = [(iota + 16.0 * k).astype(BF16) for k in range(8)]
+    one = jnp.ones((16, 128), BF16)
+    zero = jnp.zeros((16, 128), BF16)
     block = jnp.concatenate([slots[:, :128], slots[:, 128:]], axis=0)
     entries[0] = (block >> 7).astype(F32)
     entries[1] = (block & 127).astype(F32)
@@ -279,12 +280,12 @@
         for source, hot in enumerate((high_hot, low_hot)):
             block = entries[source, pl.ds(pl.multiple_of(index * 8, 8), 8), :]
             for k in range(8):
-                value = jnp.broadcast_to(block[k : k + 1], (16, 128))
+                value = jnp.broadcast_to(block[k : k + 1], (16, 128)).astype(BF16)
                 lanes = pl.ds(pl.multiple_of(index * 1024 + 128 * k, 128), 128)
                 for place in range(8):
                     hot[16 * place : 16 * (place + 1), lanes] = jnp.where(
-                        value == rows[place], 1.0, 0.0
-                    ).astype(BF16)
+                        value == rows[place], one, zero
+                    )
         return carry
 
     lax.fori_loop(0, 16, step, 0)
@@ -498,31 +499,36 @@
 
     lax.fori_loop(0, 8, source_step, 0)
 
-    iota = lax.broadcasted_iota(jnp.int32, (16, 128), 0).astype(F32)
+    iota = lax.broadcasted_iota(jnp.int32, (16, 128), 0).astype(F32).astype(BF16)
+    one = jnp.ones((16, 128), BF16)
+    zero = jnp.zeros((16, 128), BF16)
+    both = jnp.zeros((32, 128), BF16)
 
     def build(chunk, hot, spread):
         for k in range(16):
             sender = chunk * 16 + k
             lanes = slice(128 * k, 128 * (k + 1))
 
-            def row(number):
-                return jnp.broadcast_to(cells[number, pl.ds(sender, 1), :], (8, 128))
-
-            values = wide[pl.ds(pl.multiple_of(sender * 32, 32), 32), :]
-            cell = row(0)
+            def row(number, height):
+                value = cells[number, pl.ds(sender, 1), :]
+                return jnp.broadcast_to(value, (height, 128)).astype(BF16)
+
+            value = wide[pl.ds(pl.multiple_of(sender * 32, 32), 32), :].astype(BF16)
+            cell = row(0, 32)
             for c in range(16):
-                chosen = jnp.concatenate([cell == float(c)] * 4)
-                spread[32 * c : 32 * (c + 1), lanes] = jnp.where(chosen, values, 0.0).astype(BF16)
-            low = row(2)
-            inside = jnp.where(jnp.concatenate([low, low]) == iota, 1.0, 0.0)
-            above = row(1)
+                spread[32 * c : 32 * (c + 1), lanes] = jnp.where(
+                    cell == jnp.full((32, 128), c, BF16), value, both
+                )
+            inside = jnp.where(row(2, 16) == iota, one, zero)
+            above = row(1, 16)
             for c in range(16):
-                chosen = jnp.concatenate([above == float(c)] * 2)
-                hot[16 * c : 16 * (c + 1), lanes] = jnp.where(chosen, inside, 0.0).astype(BF16)
+                hot[16 * c : 16 * (c + 1), lanes] = jnp.where(
+                    above == jnp.full((16, 128), c, BF16), inside, zero
+                )
 
     def add(hot, spread):
         grid[...] += lax.dot_general(
-            spread[...], hot[...], (((1,), (1,)), ((), ())), preferred_element_type=F32
+            hot[...], spread[...], (((1,), (1,)), ((), ())), preferred_element_type=F32
         )
 
     grid[...] = jnp.zeros_like(grid)
@@ -537,18 +543,15 @@
 
     lax.fori_loop(0, 4, spread_step, 0)
 
-    grid_high, grid_low = split(grid[...].T)
+    grid_high, grid_low = split(grid[...])
     fetch_second.wait()
-    result = jnp.dot(
-        jnp.concatenate([grid_high, grid_low, grid_high], axis=1),
-        second[...],
-        preferred_element_type=F32,
-    )
-    for group in range(32):
-        for part in range(2):
-            state[group, part] = result[
-                8 * group : 8 * group + 8, BOX_NODES * part : BOX_NODES * (part + 1)
-            ]
+    for part in range(2):
+        basis = second[512 * part : 512 * (part + 1), :]
+        result = jnp.dot(grid_high, basis, preferred_element_type=F32)
+        rest = jnp.dot(grid_low, basis[:, :BOX_NODES], preferred_element_type=F32)
+        result = result[:, :BOX_NODES] + (result[:, BOX_NODES:] + rest)
+        for group in range(32):
+            state[group, part] = result[8 * group : 8 * group + 8, :]
 
 
 def pieces(result):
@@ -567,7 +570,6 @@
 def inner_kernel(
     arrived,
     mask,
-    second_far,
     table_far,
     matrix_far,
     out,
@@ -585,12 +587,12 @@
     high,
     low,
 ):
-    fetch_second = pltpu.make_async_copy(second_far, second, arrive.at[4])
+    fetch_second = pltpu.make_async_copy(matrix_far.at[pl.ds(1536, 1024)], second, arrive.at[4])
     fetch_second.start()
     fetches = [fetch_level(table_far, table, arrive, k) for k in range(4)]
     for fetch in fetches:
         fetch.start()
-    fetch_matrix = pltpu.make_async_copy(matrix_far.at[pl.ds(0, 3072)], matrix, arrive.at[5])
+    fetch_matrix = pltpu.make_async_copy(matrix_far.at[pl.ds(0, 1024)], matrix, arrive.at[5])
     fetch_matrix.start()
     deposit(arrived, mask, second, fetch_second, state, wide, cells, hots, spreads, grid)
 
@@ -653,8 +655,8 @@
     fetches = [
         fetch_level(table_far, table, arrive, k, 64 if k < 3 else 48) for k in range(1, 4)
     ]
-    fetch_matrix = pltpu.make_async_copy(matrix_far.at[pl.ds(0, 3072)], matrix, arrive.at[5])
-    fetch_last = pltpu.make_async_copy(matrix_far.at[pl.ds(3072, 1536)], last, arrive.at[4])
+    fetch_matrix = pltpu.make_async_copy(matrix_far.at[pl.ds(0, 1024)], matrix, arrive.at[5])
+    fetch_last = pltpu.make_async_copy(matrix_far.at[pl.ds(1024, 512)], last, arrive.at[4])
     for fetch in first + [fetch_matrix] + fetches + [fetch_last]:
         fetch.start()
 
@@ -812,7 +814,7 @@
             pltpu.SemaphoreType.DMA((4,)),
         ],
         name="outer_turns",
-        compiler_params=pltpu.CompilerParams(vmem_limit_bytes=59 << 20),
+        compiler_params=pltpu.CompilerParams(vmem_limit_bytes=52 << 20),
     )(jnp.asarray(node_tables()), speeds)
 
 
@@ -825,31 +827,28 @@
 
 
 def inner_levels(arrived, mask, table):
-    second_high, second_low = two_parts(second_basis())
-    second = np.concatenate([second_high, second_high, second_low], axis=0)
     return pl.pallas_call(
         inner_kernel,
         out_shape=jax.ShapeDtypeStruct((1024, 128), F32),
-        in_specs=vmem(2) + far(3),
+        in_specs=vmem(2) + far(2),
         out_specs=vmem(1)[0],
         scratch_shapes=[
-            pltpu.VMEM((1536, 512), BF16),
-            pltpu.VMEM((3072, 256), BF16),
+            pltpu.VMEM((1024, 512), BF16),
+            pltpu.VMEM((1024, 512), BF16),
             pltpu.VMEM((256, 2, 16, 256), F32),
             pltpu.SemaphoreType.DMA((6,)),
             pltpu.VMEM((4096, 128), F32),
             pltpu.VMEM((3, 128, 128), F32),
             [pltpu.VMEM((256, 2048), BF16)] * 2,
             [pltpu.VMEM((512, 2048), BF16)] * 2,
-            pltpu.VMEM((512, 256), F32),
+            pltpu.VMEM((256, 512), F32),
         ]
         + LEVEL_SCRATCH,
         name="inner",
-        compiler_params=pltpu.CompilerParams(vmem_limit_bytes=59 << 20),
+        compiler_params=pltpu.CompilerParams(vmem_limit_bytes=52 << 20),
     )(
         arrived,
         mask,
-        jnp.asarray(second),
         table,
         jnp.asarray(matrices()),
     )
@@ -863,13 +862,13 @@
         out_specs=vmem(1)[0],
         scratch_shapes=[
             pltpu.VMEM((240, 2, 16, 256), F32),
-            pltpu.VMEM((3072, 256), BF16),
-            pltpu.VMEM((1536, 256), BF16),
+            pltpu.VMEM((1024, 512), BF16),
+            pltpu.VMEM((512, 512), BF16),
             pltpu.SemaphoreType.DMA((10,)),
         ]
         + LEVEL_SCRATCH,
         name="outer",
-        compiler_params=pltpu.CompilerParams(vmem_limit_bytes=59 << 20),
+        compiler_params=pltpu.CompilerParams(vmem_limit_bytes=52 << 20),
     )(
         arrived,
         table,

time: 103 us -> 95.3 us (0.925)
  Pallas kernels: 52.2 us -> 45.7 us
  waiting for transfers between devices: 3.89 us -> 6.12 us
  local copies, waits for them, and re-layouts: 3.99 us -> 2.26 us
  blocking collectives: 19.3 us -> 17.8 us
    pallas_call x1, Pallas kernels: 19.8 us -> 17.3 us  [inner_levels(): pl.pallas_call(inner_kernel, out_shape=jax.ShapeDtypeStruct((1024, 128),...]
    all_to_all x2, waiting for transfers between devices: 3.89 us -> 6.12 us  [exchange(): lax.all_to_all(array, ('bx', 'by'), split_axis=0, concat_axis=0, tiled=True)]
    pallas_call x1, Pallas kernels: 10.3 us -> 8.24 us  [outer_levels(): pl.pallas_call(outer_kernel, out_shape=jax.ShapeDtypeStruct((1024, 128),...]
    all_to_all x1, blocking collectives: 19.3 us -> 17.8 us  [exchange(): lax.all_to_all(array, ('bx', 'by'), split_axis=0, concat_axis=0, tiled=True)]
    pallas_call x1, Pallas kernels: 7.3 us -> 6.11 us  [outer_turns(): pl.pallas_call(outer_turns_kernel, out_shape=jax.ShapeDtypeStruct((240, 2...]
    broadcast_in_dim x1, local copies, waits for them, and re-layouts: 1.35 us -> 0.29 us  [shards(): speeds = jnp.broadcast_to(speeds[:, None], (7 * 256, 128))]
  transfers between devices with their start and end apart: 2 -> 2, of which waited for: 1 -> 1; matrix products, arithmetic and copies ran while one was open for 3% -> 2% of each run, Pallas kernels for 20% -> 19%
where the time goes in v3:
time: 95.3 us; the launch traced here: 95 us
  Pallas kernels  45.7 us (48%)
  starting transfers between devices  21.3 us (22%)
  blocking collectives  17.8 us (19%)
  waiting for transfers between devices  6.12 us (6%)
  local copies, waits for them, and re-layouts  2.26 us (2%)
  other arithmetic  1.7 us (2%)
    all_to_all x2, starting transfers between devices, exchange(): lax.all_to_all(array, ('bx', 'by'), split_axis=0, concat_axis=0, tiled=True)  21.3 us
    all_to_all x1, blocking collectives, exchange(): lax.all_to_all(array, ('bx', 'by'), split_axis=0, concat_axis=0, tiled=True)  17.8 us
    pallas_call x1, Pallas kernels, inner_levels(): pl.pallas_call(inner_kernel, out_shape=jax.ShapeDtypeStruct((1024, 128),...  17.3 us
    pallas_call x1, Pallas kernels, inner_turns(): pl.pallas_call(inner_turns_kernel, out_shape=[jax.ShapeDtypeStruct((128,...  12.3 us
    pallas_call x1, Pallas kernels, outer_levels(): pl.pallas_call(outer_kernel, out_shape=jax.ShapeDtypeStruct((1024, 128),...  8.24 us
    all_to_all x2, waiting for transfers between devices, exchange(): lax.all_to_all(array, ('bx', 'by'), split_axis=0, concat_axis=0, tiled=True)  6.12 us
    pallas_call x1, Pallas kernels, outer_turns(): pl.pallas_call(outer_turns_kernel, out_shape=jax.ShapeDtypeStruct((240, 2...  6.11 us
  transfers between devices with their start and end apart: 2, of which 1 were waited for; matrix products, arithmetic and copies ran while one was open for 2% of the time, Pallas kernels for 19%

profile of v3, /device:TPU:1, one launch (start us, length us, event | category | flops | bytes accessed | tf_op | source)
XLA Modules:
  0.0 95.0 jit_solution(3152141365078013118)
XLA Ops:
  0.0 0.0 copy-start.1
  0.0 1.7 %payload.1 = f32[512,128]{1,0:T(8,128)} custom-call(s32[2,128,128]{2,1,0:T(8,128)} %bitcast.28, f32[2,128,128]{2,1,0:T(8,128)} %bitcast.29), custom_call_target="tpu_custom_call" | custom-call | tf_op jit(solution)/shard_map/payload/pallas_call | solution.py:762
  1.7 11.5 %all-to-all-start = ((f32[128,4,128]{2,1,0:T(4,128)}), f32[128,4,128]{2,1,0:T(4,128)S(1)}, u32[]{:S(2)}, u32[]{:S(2)}) async-start(f32[128,4,128]{2,1,0:T(4,128)} %bitcast.27), calls=%async_computation | async-start | bytes 524288 | tf_op jit(solution)/shard_map/all_to_all | solution.py:889
  13.3 0.7 pad_add_fusion.block
  13.9 12.3 %inner_turns.1 = (f32[128,128]{1,0:T(8,128)}, f32[256,2,16,256]{3,2,1,0:T(8,128)}) custom-call(s32[2]{0:T(128)} %pad_add_fusion.block, s32[64,256]{1,0:T(8,128)} %bitcast.30, f32[16,256]{1,0:T(8,128)} %constant.32.clone.node_far.node, f32[1024,128]{1,0:T(8,128)} %constant.33.clone.speeds_far), custom_call_target="tpu_custom_call" | custom-call | tf_op jit(solution)/shard_map/inner_turns/pallas_call | solution.py:781
  26.2 0.0 all-to-all-done
  26.2 0.0 copy-start
  26.2 0.8 copy-done
  27.1 17.3 %inner.1 = f32[1024,128]{1,0:T(8,128)} custom-call(f32[512,128]{1,0:T(8,128)S(1)} %bitcast.25, f32[128,128]{1,0:T(8,128)S(1)} %copy-done, f32[256,2,16,256]{3,2,1,0:T(8,128)} %get-tuple-element.14.table_far, bf16[2560,512]{1,0:T(8,128)(2,1)} %constant.34.clone.matrix_far), custom_call_target="tpu_custom_call" | custom-call | tf_op jit(solution)/shard_map/inner/pallas_call | solution.py:830
  44.4 9.8 %all-to-all-start.1 = ((f32[128,8,128]{2,1,0:T(8,128)}), f32[128,8,128]{2,1,0:T(8,128)S(1)}, u32[]{:S(2)}, u32[]{:S(2)}) async-start(f32[128,8,128]{2,1,0:T(8,128)} %bitcast.8), calls=%async_computation.1 | async-start | bytes 1048576 | tf_op jit(solution)/shard_map/all_to_all | solution.py:889
  54.2 0.9 dynamic-slice_reduce_fusion
  55.0 0.3 broadcast_in_dim.9.speeds
  55.3 0.0 copy-done.1
  55.3 6.1 %outer_turns.1.table_far = f32[240,2,16,256]{3,2,1,0:T(8,128)} custom-call(f32[16,256]{1,0:T(8,128)S(1)} %copy-done.1, f32[1792,128]{1,0:T(8,128)S(1)} %broadcast_in_dim.9.speeds), custom_call_target="tpu_custom_call" | custom-call | tf_op jit(solution)/shard_map/outer_turns/pallas_call | solution.py:807
  61.4 6.1 %all-to-all-done.1 = f32[128,8,128]{2,1,0:T(8,128)S(1)} async-done(((f32[128,8,128]{2,1,0:T(8,128)}), f32[128,8,128]{2,1,0:T(8,128)S(1)}, u32[]{:S(2)}, u32[]{:S(2)}) %all-to-all-start.1) | async-done | bytes 524320 | tf_op jit(solution)/shard_map/all_to_all | solution.py:889
  67.6 8.2 %outer.1 = f32[1024,128]{1,0:T(8,128)S(1)} custom-call(f32[1024,128]{1,0:T(8,128)S(1)} %bitcast.23, f32[240,2,16,256]{3,2,1,0:T(8,128)} %outer_turns.1.table_far, bf16[2560,512]{1,0:T(8,128)(2,1)} %constant.34.clone.matrix_far), custom_call_target="tpu_custom_call" | custom-call | tf_op jit(solution)/shard_map/outer/pallas_call | solution.py:858
  75.8 17.8 %all_to_all.15 = f32[128,8,128]{2,1,0:T(8,128)S(1)} all-to-all(f32[128,8,128]{2,1,0:T(8,128)S(1)} %bitcast.24), channel_id=1, replica_groups=mesh['bx'=8,'by'=16] {'bx','by'}, dimensions={0} | all-to-all | bytes 1048576 | tf_op jit(solution)/shard_map/all_to_all | solution.py:889
  93.6 0.3 slice_bitcast_fusion.1
  93.9 1.0 %maximum_bitcast_fusion = f32[16,1,16,1,2,256]{5,4,3,2,1,0:T(2,128)} fusion(f32[16,16,2,128]{3,2,1,0:T(2,128)S(1)} %get-tuple-element.16, f32[16,16,2,128]{3,2,1,0:T(2,128)S(1)} %get-tuple-element.15), kind=kLoop, calls=%fused_computation | loop fusion | flops 131072 | bytes 1048576 | tf_op jit(solution)/shard_map/reshape | solution.py:909
Async XLA Ops:
  0.0 55.3 %copy-start.1 = (f32[16,256]{1,0:T(8,128)S(1)}, f32[16,256]{1,0:T(8,128)}, u32[]{:S(2)}) copy-start(f32[16,256]{1,0:T(8,128)} %constant.32.clone.node_far.node) | copy-start | bytes 49156
  1.7 24.5 %all-to-all-start = ((f32[128,4,128]{2,1,0:T(4,128)}), f32[128,4,128]{2,1,0:T(4,128)S(1)}, u32[]{:S(2)}, u32[]{:S(2)}) async-start(f32[128,4,128]{2,1,0:T(4,128)} %bitcast.27), calls=%async_computation | async-start | bytes 524288 | tf_op jit(solution)/shard_map/all_to_all | solution.py:889
  26.2 0.8 copy-start
  44.4 23.2 %all-to-all-start.1 = ((f32[128,8,128]{2,1,0:T(8,128)}), f32[128,8,128]{2,1,0:T(8,128)S(1)}, u32[]{:S(2)}, u32[]{:S(2)}) async-start(f32[128,8,128]{2,1,0:T(8,128)} %bitcast.8), calls=%async_computation.1 | async-start | bytes 1048576 | tf_op jit(solution)/shard_map/all_to_all | solution.py:889

commit v4 on v3

--- a/solution.py
+++ b/solution.py
@@ -140,7 +140,7 @@
     points = chebyshev_points(NODES).astype(np.float32).astype(np.float64)
     first = np.repeat(points, NODES)
     second = np.tile(points, NODES)
-    rows = np.zeros((16, BOX_NODES))
+    rows = np.zeros((24, BOX_NODES))
     for child in range(4):
         x, y = bits(child, 2)
         turns = (2 * x - 1) * 2 * first + (2 * y - 1) * second
@@ -153,6 +153,9 @@
     rows[9] = first - rows[8]
     rows[10] = np.round(second * 8192) / 8192
     rows[11] = second - rows[10]
+    for child in range(2):
+        rows[16 + 2 * child] = np.cos(2 * np.pi * rows[child])
+        rows[17 + 2 * child] = np.sin(2 * np.pi * rows[child])
     rows[12] = BAND * np.sqrt(first * first + second * second)
     return rows.astype(np.float32)
 
@@ -193,7 +196,9 @@
     return (value >> place) & 1
 
 
-def make_turns(table, first_line, box, level_number, speeds, speed_row, node, base_row, children, rows):
+def make_turns(
+    table, first_line, box, level_number, speeds, speed_row, node, base_row, children, rows, stores=()
+):
     scale = 4.0 * 2.0 ** (level_number - 1)
     pairs = rows // 2
 
@@ -217,38 +222,83 @@
             table[line, 1] = sine
         return carry
 
-    lax.fori_loop(0, (4 if children == 4 else 2) * pairs, step, 0)
+    if not stores:
+        lax.fori_loop(0, (4 if children == 4 else 2) * pairs, step, 0)
+    for source, store in enumerate(stores):
+        lax.fori_loop(source * pairs, (source + 1) * pairs, step, 0)
+        store.start()
+
+
+def make_first_turns(table, box, node):
+    def step(index, carry):
+        radius = []
+        for k in range(2):
+            first, second = box(index // 4, 2 * (index % 4) + k)
+            along = first + node[6:7, :]
+            across = second + node[7:8, :]
+            radius.append(0.5 * jnp.sqrt(along * along + across * across))
+        cosine, sine = turn(jnp.concatenate(radius))
+        for kind in range(2):
+            base_cosine = node[16 + 2 * kind : 17 + 2 * kind, :]
+            base_sine = node[17 + 2 * kind : 18 + 2 * kind, :]
+            cosines = base_cosine * cosine
+            sines = base_sine * sine
+            mixed = base_sine * cosine
+            other = base_cosine * sine
+            line = 4 * index + kind
+            mirror = 4 * index + 3 - kind
+            if kind == 0:
+                table[line, 0] = cosines - sines
+                table[line, 1] = mixed + other
+                table[mirror, 0] = cosines + sines
+                table[mirror, 1] = other - mixed
+            else:
+                table[line, 0] = cosines + sines
+                table[line, 1] = mixed - other
+                table[mirror, 0] = cosines - sines
+                table[mirror, 1] = -mixed - other
+        return carry
+
+    lax.fori_loop(0, 16, step, 0)
 
 
 def level(read, table, first_line, high, low, matrix, children, rows, ready, matrix_ready=None):
     sources = 4 if children == 4 else 2
     pairs = rows // 2
-    for source in range(sources):
-        lanes = slice(source * BOX_NODES, (source + 1) * BOX_NODES)
-        if source < len(ready):
-            ready[source].wait()
-        for pair in range(pairs):
-            group = source * rows + 2 * pair
-            real, imaginary = (
-                jnp.concatenate([read(group, part), read(group + 1, part)]) for part in range(2)
-            )
-            for child in range(children):
-                line = first_line + (source * pairs + pair) * children + child
-                cosine = table[line, 0]
-                sine = table[line, 1]
-                for part, value in enumerate(
-                    (real * cosine - imaginary * sine, real * sine + imaginary * cosine)
-                ):
-                    place = (child * 2 + part) * rows * 8 + pair * 16
-                    value_high, value_low = split(value)
-                    high[place : place + 16, lanes] = value_high
-                    low[place : place + 16, lanes] = value_low
-    if matrix_ready is not None:
-        matrix_ready.wait()
     columns = sources * BOX_NODES
-    both = jnp.dot(high[:, :columns], matrix[...], preferred_element_type=F32)
-    rest = jnp.dot(low[:, :columns], matrix[:, :BOX_NODES], preferred_element_type=F32)
-    return both[:, :BOX_NODES] + (both[:, BOX_NODES:] + rest)
+    results = []
+    for first in range(0, children, children // 2):
+        chosen = range(first, first + children // 2)
+        for source in range(sources):
+            lanes = slice(source * BOX_NODES, (source + 1) * BOX_NODES)
+            if first == 0 and source < len(ready):
+                ready[source].wait()
+            for pair in range(pairs):
+                group = source * rows + 2 * pair
+                real, imaginary = (
+                    jnp.concatenate([read(group, part), read(group + 1, part)])
+                    for part in range(2)
+                )
+                for child in chosen:
+                    line = first_line + (source * pairs + pair) * children + child
+                    cosine = table[line, 0]
+                    sine = table[line, 1]
+                    for part, value in enumerate(
+                        (real * cosine - imaginary * sine, real * sine + imaginary * cosine)
+                    ):
+                        place = (child * 2 + part) * rows * 8 + pair * 16
+                        value_high, value_low = split(value)
+                        high[place : place + 16, lanes] = value_high
+                        low[place : place + 16, lanes] = value_low
+        if first == 0 and matrix_ready is not None:
+            matrix_ready.wait()
+        places = slice(first * 2 * rows * 8, (first + children // 2) * 2 * rows * 8)
+        both = jnp.dot(high[places, :columns], matrix[...], preferred_element_type=F32)
+        rest = jnp.dot(
+            low[places, :columns], matrix[:, :BOX_NODES], preferred_element_type=F32
+        )
+        results.append(both[:, :BOX_NODES] + (both[:, BOX_NODES:] + rest))
+    return jnp.concatenate(results)
 
 
 def matrices():
@@ -267,7 +317,7 @@
     return [bit(row, 2 - k).astype(F32) for k in range(3)]
 
 
-def find_mask(slots, mask, entries, high_hot, low_hot, total):
+def find_mask(slots, table, entries, high_hot, low_hot, total):
     iota = lax.broadcasted_iota(jnp.int32, (16, 128), 0).astype(F32)
     rows = [(iota + 16.0 * k).astype(BF16) for k in range(8)]
     one = jnp.ones((16, 128), BF16)
@@ -278,17 +328,18 @@
 
     def step(index, carry):
         for source, hot in enumerate((high_hot, low_hot)):
-            block = entries[source, pl.ds(pl.multiple_of(index * 8, 8), 8), :]
-            for k in range(8):
-                value = jnp.broadcast_to(block[k : k + 1], (16, 128)).astype(BF16)
-                lanes = pl.ds(pl.multiple_of(index * 1024 + 128 * k, 128), 128)
-                for place in range(8):
-                    hot[16 * place : 16 * (place + 1), lanes] = jnp.where(
-                        value == rows[place], one, zero
-                    )
+            for side in range(2):
+                start = pl.multiple_of(index * 8 + 64 * side, 8)
+                block = entries[source, pl.ds(start, 8), :]
+                for k in range(8):
+                    value = jnp.broadcast_to(block[k : k + 1], (16, 128)).astype(BF16)
+                    lanes = pl.ds(pl.multiple_of(index * 1024 + 128 * k, 128), 128)
+                    for place in range(8):
+                        line = 128 * side + 16 * place
+                        hot[line : line + 16, lanes] = jnp.where(value == rows[place], one, zero)
         return carry
 
-    lax.fori_loop(0, 16, step, 0)
+    lax.fori_loop(0, 8, step, 0)
     total[...] = jnp.zeros_like(total)
 
     def add(index, carry):
@@ -301,13 +352,17 @@
         )
         return carry
 
-    lax.fori_loop(0, 4, add, 0)
-    mask[...] = jnp.where(total[...] > 0.5, 1.0, 0.0)
-
-
-def store_level(table, table_far, leave, index, size=64):
-    lines = pl.ds(64 * index, size)
-    return pltpu.make_async_copy(table.at[lines], table_far.at[lines], leave.at[index])
+    lax.fori_loop(0, 2, add, 0)
+    mask = jnp.where(total[:128, :128] + total[128:, 128:] > 0.5, 1.0, 0.0)
+    for k in range(8):
+        lanes = slice(128 * (k % 2), 128 * (k % 2 + 1))
+        table[256 + k // 4, k // 2 % 2, :, lanes] = mask[16 * k : 16 * (k + 1)]
+
+
+def store_level(table, table_far, leave, index, size=64, first=0):
+    lines = pl.ds(size * index, size)
+    place = leave.at[index if first == 0 else first + index % 4]
+    return pltpu.make_async_copy(table.at[lines], table_far.at[lines], place)
 
 
 def fetch_level(table_far, table, arrive, index, size=64):
@@ -315,12 +370,17 @@
     return pltpu.make_async_copy(table_far.at[lines], table.at[lines], arrive.at[index])
 
 
+def fetch_mask_lines(table_far, table, place):
+    lines = pl.ds(256, 2)
+    return pltpu.make_async_copy(table_far.at[lines], table.at[lines], place)
+
+
 def inner_turns_kernel(
-    block,
+    block_first_ref,
+    block_second_ref,
     slots_far,
     node_far,
     speeds_far,
-    mask,
     table_far,
     slots,
     node,
@@ -342,13 +402,16 @@
     for fetch in fetches:
         fetch.start()
     fetches[0].wait()
-    find_mask(slots, mask, entries, high_hot, low_hot, total)
+    find_mask(slots, table, entries, high_hot, low_hot, total)
     for fetch in fetches[1:]:
         fetch.wait()
-    stores = [store_level(table, table_far, leave, k) for k in range(4)]
+    stores = [store_level(table, table_far, leave, k) for k in range(3)]
+    stores += [store_level(table, table_far, leave, 12 + k, 16, 3) for k in range(4)]
+    store_mask = store_level(table, table_far, leave, 128, 2, 7)
+    store_mask.start()
     sub = sub_bits()
-    block_first = block[0]
-    block_second = block[1]
+    block_first = block_first_ref[0]
+    block_second = block_second_ref[0]
 
     def box(source, row):
         first = block_first * 16 + bit(source, 1) + 2 * bit(row, 2)
@@ -358,7 +421,7 @@
             second.astype(F32) + 4.0 * sub[1],
         )
 
-    make_turns(table, 0, box, 1, speeds, 0, node, 0, 4, 8)
+    make_first_turns(table, box, node)
     stores[0].start()
 
     def box(source, row):
@@ -385,14 +448,14 @@
         second = block_second * 2 + bit(source, 0)
         return 2.0 * first.astype(F32), second.astype(F32)
 
-    make_turns(table, 192, box, 4, speeds, 768, node, 0, 4, 8)
-    stores[3].start()
-    for store in stores:
+    make_turns(table, 192, box, 4, speeds, 768, node, 0, 4, 8, stores[3:])
+    for store in stores + [store_mask]:
         store.wait()
 
 
 def outer_turns_kernel(node, speeds, table_far, table, leave):
-    stores = [store_level(table, table_far, leave, k, 64 if k < 3 else 48) for k in range(4)]
+    stores = [store_level(table, table_far, leave, k) for k in range(3)]
+    stores += [store_level(table, table_far, leave, 12 + k, 16, 3) for k in range(3)]
     sub = sub_bits()
 
     def box(source, row):
@@ -422,7 +485,7 @@
     def box(source, row):
         return jnp.float32(0.0), source.astype(F32)
 
-    make_turns(table, 192, box, 8, speeds, 768, node, 4, 2, 16)
+    make_turns(table, 192, box, 8, speeds, 768, node, 4, 2, 16, stores[3:5])
 
     def last(index, carry):
         def column(table):
@@ -444,13 +507,13 @@
         return carry
 
     lax.fori_loop(0, 16, last, 0)
-    stores[3].start()
+    stores[5].start()
     for store in stores:
         store.wait()
 
 
 def deposit(
-    arrived, mask, second, fetch_second, state, wide, cells, hots, spreads, grid
+    arrived, table, second, fetch_second, state, wide, cells, hots, spreads, grid
 ):
     points = [float(value) for value in chebyshev_points(NODES).astype(np.float32)]
     factors = basis_factors()
@@ -468,7 +531,8 @@
         cosine, sine = turn(
             0.125 * eighths + 0.0625 * jnp.sqrt(along * along + across * across)
         )
-        live = mask[rows, :]
+        lanes = pl.ds(pl.multiple_of(index % 2 * 128, 128), 128)
+        live = table[256 + index // 4, index // 2 % 2, :, lanes]
         real = real * live
         imaginary = imaginary * live
         turned = (real * cosine - imaginary * sine, real * sine + imaginary * cosine)
@@ -502,7 +566,6 @@
     iota = lax.broadcasted_iota(jnp.int32, (16, 128), 0).astype(F32).astype(BF16)
     one = jnp.ones((16, 128), BF16)
     zero = jnp.zeros((16, 128), BF16)
-    both = jnp.zeros((32, 128), BF16)
 
     def build(chunk, hot, spread):
         for k in range(16):
@@ -514,11 +577,13 @@
                 return jnp.broadcast_to(value, (height, 128)).astype(BF16)
 
             value = wide[pl.ds(pl.multiple_of(sender * 32, 32), 32), :].astype(BF16)
-            cell = row(0, 32)
+            cell = row(0, 16)
             for c in range(16):
-                spread[32 * c : 32 * (c + 1), lanes] = jnp.where(
-                    cell == jnp.full((32, 128), c, BF16), value, both
-                )
+                chosen = cell == jnp.full((16, 128), c, BF16)
+                for part in range(2):
+                    spread[32 * c + 16 * part : 32 * c + 16 * (part + 1), lanes] = jnp.where(
+                        chosen, value[16 * part : 16 * (part + 1)], zero
+                    )
             inside = jnp.where(row(2, 16) == iota, one, zero)
             above = row(1, 16)
             for c in range(16):
@@ -526,19 +591,18 @@
                     above == jnp.full((16, 128), c, BF16), inside, zero
                 )
 
-    def add(hot, spread):
-        grid[...] += lax.dot_general(
+    def product(hot, spread):
+        return lax.dot_general(
             hot[...], spread[...], (((1,), (1,)), ((), ())), preferred_element_type=F32
         )
 
     grid[...] = jnp.zeros_like(grid)
-    build(0, hots[0], spreads[0])
 
     def spread_step(index, carry):
-        add(hots[0], spreads[0])
-        build(2 * index + 1, hots[1], spreads[1])
-        add(hots[1], spreads[1])
-        build(jnp.minimum(2 * index + 2, 7), hots[0], spreads[0])
+        for k in range(2):
+            build(2 * index + k, hots[k], spreads[k])
+        parts = [product(hots[k], spreads[k]) for k in range(2)]
+        grid[...] += parts[0] + parts[1]
         return carry
 
     lax.fori_loop(0, 4, spread_step, 0)
@@ -569,7 +633,6 @@
 
 def inner_kernel(
     arrived,
-    mask,
     table_far,
     matrix_far,
     out,
@@ -587,6 +650,8 @@
     high,
     low,
 ):
+    fetch_mask = fetch_mask_lines(table_far, table, arrive.at[6])
+    fetch_mask.start()
     fetch_second = pltpu.make_async_copy(matrix_far.at[pl.ds(1536, 1024)], second, arrive.at[4])
     fetch_second.start()
     fetches = [fetch_level(table_far, table, arrive, k) for k in range(4)]
@@ -594,7 +659,8 @@
         fetch.start()
     fetch_matrix = pltpu.make_async_copy(matrix_far.at[pl.ds(0, 1024)], matrix, arrive.at[5])
     fetch_matrix.start()
-    deposit(arrived, mask, second, fetch_second, state, wide, cells, hots, spreads, grid)
+    fetch_mask.wait()
+    deposit(arrived, table, second, fetch_second, state, wide, cells, hots, spreads, grid)
 
     def run(number, read):
         return level(
@@ -776,31 +842,28 @@
     )(place, amp)
 
 
-def inner_turns(block, slots):
+def inner_turns(block_first, block_second, slots):
     speeds = np.repeat(inner_speeds()[:, None], 128, axis=1)
     return pl.pallas_call(
         inner_turns_kernel,
-        out_shape=[
-            jax.ShapeDtypeStruct((128, 128), F32),
-            jax.ShapeDtypeStruct((256, 2, 16, 256), F32),
-        ],
-        in_specs=smem(1) + far(3),
-        out_specs=vmem(1) + far(1),
+        out_shape=jax.ShapeDtypeStruct((258, 2, 16, 256), F32),
+        in_specs=smem(2) + far(3),
+        out_specs=far(1)[0],
         scratch_shapes=[
             pltpu.VMEM((64, 256), jnp.int32),
-            pltpu.VMEM((16, 256), F32),
+            pltpu.VMEM((24, 256), F32),
             pltpu.VMEM((1024, 128), F32),
-            pltpu.VMEM((256, 2, 16, 256), F32),
+            pltpu.VMEM((258, 2, 16, 256), F32),
             pltpu.VMEM((2, 128, 128), F32),
-            pltpu.VMEM((128, 16384), BF16),
-            pltpu.VMEM((128, 16384), BF16),
-            pltpu.VMEM((128, 128), F32),
+            pltpu.VMEM((256, 8192), BF16),
+            pltpu.VMEM((256, 8192), BF16),
+            pltpu.VMEM((256, 256), F32),
             pltpu.SemaphoreType.DMA((3,)),
-            pltpu.SemaphoreType.DMA((4,)),
+            pltpu.SemaphoreType.DMA((8,)),
         ],
         name="inner_turns",
         compiler_params=pltpu.CompilerParams(vmem_limit_bytes=60 << 20),
-    )(block, slots, jnp.asarray(node_tables()), jnp.asarray(speeds))
+    )(block_first, block_second, slots, jnp.asarray(node_tables()), jnp.asarray(speeds))
 
 
 def outer_turns(speeds):
@@ -811,7 +874,7 @@
         out_specs=far(1)[0],
         scratch_shapes=[
             pltpu.VMEM((240, 2, 16, 256), F32),
-            pltpu.SemaphoreType.DMA((4,)),
+            pltpu.SemaphoreType.DMA((7,)),
         ],
         name="outer_turns",
         compiler_params=pltpu.CompilerParams(vmem_limit_bytes=52 << 20),
@@ -826,17 +889,17 @@
 ]
 
 
-def inner_levels(arrived, mask, table):
+def inner_levels(arrived, table):
     return pl.pallas_call(
         inner_kernel,
         out_shape=jax.ShapeDtypeStruct((1024, 128), F32),
-        in_specs=vmem(2) + far(2),
+        in_specs=vmem(1) + far(2),
         out_specs=vmem(1)[0],
         scratch_shapes=[
             pltpu.VMEM((1024, 512), BF16),
             pltpu.VMEM((1024, 512), BF16),
-            pltpu.VMEM((256, 2, 16, 256), F32),
-            pltpu.SemaphoreType.DMA((6,)),
+            pltpu.VMEM((258, 2, 16, 256), F32),
+            pltpu.SemaphoreType.DMA((7,)),
             pltpu.VMEM((4096, 128), F32),
             pltpu.VMEM((3, 128, 128), F32),
             [pltpu.VMEM((256, 2048), BF16)] * 2,
@@ -848,7 +911,6 @@
         compiler_params=pltpu.CompilerParams(vmem_limit_bytes=52 << 20),
     )(
         arrived,
-        mask,
         table,
         jnp.asarray(matrices()),
     )
@@ -893,12 +955,13 @@
     column = lax.axis_index("bx")
     row = lax.axis_index("by")
     device = column * BY + row
-    block = jnp.stack([reverse_bits(column, 3), reverse_bits(row, 4)]).astype(jnp.int32)
+    block_first = reverse_bits(column, 3).astype(jnp.int32).reshape(1)
+    block_second = reverse_bits(row, 4).astype(jnp.int32).reshape(1)
     payload = make_payload(src_pos.reshape(2, DEVICES, 128), src_amp.reshape(2, DEVICES, 128))
     arrived = exchange(payload.reshape(DEVICES, 4, 128)).reshape(512, 128)
-    mask, table = inner_turns(block, box_slots[0].T)
-    arrived, mask, table = lax.optimization_barrier((arrived, mask, table))
-    weights = inner_levels(arrived, mask, table)
+    table = inner_turns(block_first, block_second, box_slots[0].T)
+    arrived, table = lax.optimization_barrier((arrived, table))
+    weights = inner_levels(arrived, table)
     weights = exchange(weights.reshape(DEVICES, 8, 128)).reshape(1024, 128)
     speeds = lax.dynamic_index_in_dim(jnp.asarray(outer_speeds()), device, 0, keepdims=False)
     speeds = jnp.broadcast_to(speeds[:, None], (7 * 256, 128))

time: 95.3 us -> 85.9 us (0.901)
  Pallas kernels: 45.7 us -> 37.5 us
  waiting for transfers between devices: 6.12 us -> 7.33 us
    pallas_call x1, Pallas kernels: 17.3 us -> 14 us  [inner_levels(): pl.pallas_call(inner_kernel, out_shape=jax.ShapeDtypeStruct((1024, 128),...]
    pallas_call x1, Pallas kernels: 12.3 us -> 9.93 us  [inner_turns(): pl.pallas_call(inner_turns_kernel, out_shape=jax.ShapeDtypeStruct((258, 2...]
    pallas_call x1, Pallas kernels: 8.24 us -> 5.99 us  [outer_levels(): pl.pallas_call(outer_kernel, out_shape=jax.ShapeDtypeStruct((1024, 128),...]
    all_to_all x2, waiting for transfers between devices: 6.12 us -> 7.33 us  [exchange(): lax.all_to_all(array, ('bx', 'by'), split_axis=0, concat_axis=0, tiled=True)]
  transfers between devices with their start and end apart: 2 -> 2, of which waited for: 1 -> 2; matrix products, arithmetic and copies ran while one was open for 2% -> 1% of each run, Pallas kernels for 19% -> 18%
where the time goes in v4:
time: 85.9 us; the launch traced here: 85.6 us
  Pallas kernels  37.5 us (44%)
  starting transfers between devices  20.4 us (24%)
  blocking collectives  17.8 us (21%)
  waiting for transfers between devices  7.33 us (9%)
  local copies, waits for them, and re-layouts  1.43 us (2%)
  other arithmetic  1.04 us (1%)
    all_to_all x2, starting transfers between devices, exchange(): lax.all_to_all(array, ('bx', 'by'), split_axis=0, concat_axis=0, tiled=True)  20.4 us
    all_to_all x1, blocking collectives, exchange(): lax.all_to_all(array, ('bx', 'by'), split_axis=0, concat_axis=0, tiled=True)  17.8 us
    pallas_call x1, Pallas kernels, inner_levels(): pl.pallas_call(inner_kernel, out_shape=jax.ShapeDtypeStruct((1024, 128),...  14 us
    pallas_call x1, Pallas kernels, inner_turns(): pl.pallas_call(inner_turns_kernel, out_shape=jax.ShapeDtypeStruct((258, 2...  9.93 us
    all_to_all x2, waiting for transfers between devices, exchange(): lax.all_to_all(array, ('bx', 'by'), split_axis=0, concat_axis=0, tiled=True)  7.33 us
    pallas_call x1, Pallas kernels, outer_levels(): pl.pallas_call(outer_kernel, out_shape=jax.ShapeDtypeStruct((1024, 128),...  5.99 us
    pallas_call x1, Pallas kernels, outer_turns(): pl.pallas_call(outer_turns_kernel, out_shape=jax.ShapeDtypeStruct((240, 2...  5.77 us
    pallas_call x1, Pallas kernels, make_payload(): pl.pallas_call(payload_kernel, out_shape=jax.ShapeDtypeStruct((4 * DEVICE...  1.72 us
  transfers between devices with their start and end apart: 2, of which 2 were waited for; matrix products, arithmetic and copies ran while one was open for 1% of the time, Pallas kernels for 18%

profile of v4, /device:TPU:1, one launch (start us, length us, event | category | flops | bytes accessed | tf_op | source)
XLA Modules:
  0.0 85.6 jit_solution(3004470440560277433)
XLA Ops:
  0.0 1.7 %payload.1 = f32[512,128]{1,0:T(8,128)} custom-call(s32[2,128,128]{2,1,0:T(8,128)} %bitcast.28, f32[2,128,128]{2,1,0:T(8,128)} %bitcast.29), custom_call_target="tpu_custom_call" | custom-call | tf_op jit(solution)/shard_map/payload/pallas_call | solution.py:828
  1.7 11.5 %all-to-all-start = ((f32[128,4,128]{2,1,0:T(4,128)}), f32[128,4,128]{2,1,0:T(4,128)S(1)}, u32[]{:S(2)}, u32[]{:S(2)}) async-start(f32[128,4,128]{2,1,0:T(4,128)} %bitcast.27), calls=%async_computation | async-start | bytes 524288 | tf_op jit(solution)/shard_map/all_to_all | solution.py:951
  13.3 9.9 %inner_turns.1.table_far = f32[258,2,16,256]{3,2,1,0:T(8,128)} custom-call(s32[1]{0:T(128)} %bitcast.4.block_first_ref, s32[1]{0:T(128)} %bitcast.5.block_second_ref, s32[64,256]{1,0:T(8,128)} %bitcast.30, f32[24,256]{1,0:T(8,128)} %constant.32.clone.node_far.node, f32[1024,128]{1,0:T(8,128)} %constant.33.clone.speeds_far), custom_call_target="tpu_custom_call" | custom-call | tf_op jit(solution)/shard_map/inner_turns/pallas_call | solution.py:847
  23.2 0.0 copy-start
  23.2 0.9 %all-to-all-done = f32[128,4,128]{2,1,0:T(4,128)S(1)} async-done(((f32[128,4,128]{2,1,0:T(4,128)}), f32[128,4,128]{2,1,0:T(4,128)S(1)}, u32[]{:S(2)}, u32[]{:S(2)}) %all-to-all-start) | async-done | bytes 262176 | tf_op jit(solution)/shard_map/all_to_all | solution.py:951
  24.1 14.0 %inner.1 = f32[1024,128]{1,0:T(8,128)} custom-call(f32[512,128]{1,0:T(8,128)S(1)} %bitcast.25, f32[258,2,16,256]{3,2,1,0:T(8,128)} %inner_turns.1.table_far, bf16[2560,512]{1,0:T(8,128)(2,1)} %constant.34.clone.matrix_far), custom_call_target="tpu_custom_call" | custom-call | tf_op jit(solution)/shard_map/inner/pallas_call | solution.py:893
  38.1 8.9 %all-to-all-start.1 = ((f32[128,8,128]{2,1,0:T(8,128)}), f32[128,8,128]{2,1,0:T(8,128)S(1)}, u32[]{:S(2)}, u32[]{:S(2)}) async-start(f32[128,8,128]{2,1,0:T(8,128)} %bitcast.8), calls=%async_computation.1 | async-start | bytes 1048576 | tf_op jit(solution)/shard_map/all_to_all | solution.py:951
  47.1 0.9 dynamic-slice_reduce_fusion
  47.9 0.3 broadcast_in_dim.9.speeds
  48.2 0.0 copy-done
  48.2 5.8 %outer_turns.1.table_far = f32[240,2,16,256]{3,2,1,0:T(8,128)} custom-call(f32[24,256]{1,0:T(8,128)S(1)} %copy-done, f32[1792,128]{1,0:T(8,128)S(1)} %broadcast_in_dim.9.speeds), custom_call_target="tpu_custom_call" | custom-call | tf_op jit(solution)/shard_map/outer_turns/pallas_call | solution.py:870
  54.0 6.4 %all-to-all-done.1 = f32[128,8,128]{2,1,0:T(8,128)S(1)} async-done(((f32[128,8,128]{2,1,0:T(8,128)}), f32[128,8,128]{2,1,0:T(8,128)S(1)}, u32[]{:S(2)}, u32[]{:S(2)}) %all-to-all-start.1) | async-done | bytes 524320 | tf_op jit(solution)/shard_map/all_to_all | solution.py:951
  60.5 6.0 %outer.1 = f32[1024,128]{1,0:T(8,128)S(1)} custom-call(f32[1024,128]{1,0:T(8,128)S(1)} %bitcast.23, f32[240,2,16,256]{3,2,1,0:T(8,128)} %outer_turns.1.table_far, bf16[2560,512]{1,0:T(8,128)(2,1)} %constant.34.clone.matrix_far), custom_call_target="tpu_custom_call" | custom-call | tf_op jit(solution)/shard_map/outer/pallas_call | solution.py:920
  66.5 17.8 %all_to_all.15 = f32[128,8,128]{2,1,0:T(8,128)S(1)} all-to-all(f32[128,8,128]{2,1,0:T(8,128)S(1)} %bitcast.24), channel_id=1, replica_groups=mesh['bx'=8,'by'=16] {'bx','by'}, dimensions={0} | all-to-all | bytes 1048576 | tf_op jit(solution)/shard_map/all_to_all | solution.py:951
  84.3 0.3 slice_bitcast_fusion.1
  84.6 1.0 %maximum_bitcast_fusion = f32[16,1,16,1,2,256]{5,4,3,2,1,0:T(2,128)} fusion(f32[16,16,2,128]{3,2,1,0:T(2,128)S(1)} %get-tuple-element.10, f32[16,16,2,128]{3,2,1,0:T(2,128)S(1)} %get-tuple-element.9), kind=kLoop, calls=%fused_computation | loop fusion | flops 131072 | bytes 1048576 | tf_op jit(solution)/shard_map/reshape | solution.py:972
Async XLA Ops:
  1.7 22.4 %all-to-all-start = ((f32[128,4,128]{2,1,0:T(4,128)}), f32[128,4,128]{2,1,0:T(4,128)S(1)}, u32[]{:S(2)}, u32[]{:S(2)}) async-start(f32[128,4,128]{2,1,0:T(4,128)} %bitcast.27), calls=%async_computation | async-start | bytes 524288 | tf_op jit(solution)/shard_map/all_to_all | solution.py:951
  23.2 25.0 %copy-start = (f32[24,256]{1,0:T(8,128)S(1)}, f32[24,256]{1,0:T(8,128)}, u32[]{:S(2)}) copy-start(f32[24,256]{1,0:T(8,128)} %constant.32.clone.node_far.node) | copy-start | bytes 73732
  38.1 22.3 %all-to-all-start.1 = ((f32[128,8,128]{2,1,0:T(8,128)}), f32[128,8,128]{2,1,0:T(8,128)S(1)}, u32[]{:S(2)}, u32[]{:S(2)}) async-start(f32[128,8,128]{2,1,0:T(8,128)} %bitcast.8), calls=%async_computation.1 | async-start | bytes 1048576 | tf_op jit(solution)/shard_map/all_to_all | solution.py:951

commit v5 on v4

--- a/solution.py
+++ b/solution.py
@@ -262,43 +262,56 @@
     lax.fori_loop(0, 16, step, 0)
 
 
-def level(read, table, first_line, high, low, matrix, children, rows, ready, matrix_ready=None):
+def level(
+    read, table, first_line, highs, lows, matrix, children, rows, by_rows, ready, emit, matrix_ready=None
+):
     sources = 4 if children == 4 else 2
     pairs = rows // 2
     columns = sources * BOX_NODES
-    results = []
-    for first in range(0, children, children // 2):
-        chosen = range(first, first + children // 2)
+    for half in range(2):
+        high, low = highs[half], lows[half]
+        if by_rows:
+            chosen = list(range(children))
+            near = list(range(half * pairs // 2, (half + 1) * pairs // 2))
+        else:
+            chosen = list(range(half * children // 2, (half + 1) * children // 2))
+            near = list(range(pairs))
+        height = 16 * len(near)
         for source in range(sources):
             lanes = slice(source * BOX_NODES, (source + 1) * BOX_NODES)
-            if first == 0 and source < len(ready):
+            if half == 0 and source < len(ready):
                 ready[source].wait()
-            for pair in range(pairs):
+            for spot, pair in enumerate(near):
                 group = source * rows + 2 * pair
                 real, imaginary = (
                     jnp.concatenate([read(group, part), read(group + 1, part)])
                     for part in range(2)
                 )
-                for child in chosen:
+                for number, child in enumerate(chosen):
                     line = first_line + (source * pairs + pair) * children + child
                     cosine = table[line, 0]
                     sine = table[line, 1]
                     for part, value in enumerate(
                         (real * cosine - imaginary * sine, real * sine + imaginary * cosine)
                     ):
-                        place = (child * 2 + part) * rows * 8 + pair * 16
+                        place = (number * 2 + part) * height + spot * 16
                         value_high, value_low = split(value)
                         high[place : place + 16, lanes] = value_high
                         low[place : place + 16, lanes] = value_low
-        if first == 0 and matrix_ready is not None:
+        if half == 0 and matrix_ready is not None:
             matrix_ready.wait()
-        places = slice(first * 2 * rows * 8, (first + children // 2) * 2 * rows * 8)
-        both = jnp.dot(high[places, :columns], matrix[...], preferred_element_type=F32)
-        rest = jnp.dot(
-            low[places, :columns], matrix[:, :BOX_NODES], preferred_element_type=F32
-        )
-        results.append(both[:, :BOX_NODES] + (both[:, BOX_NODES:] + rest))
-    return jnp.concatenate(results)
+        both = jnp.dot(high[:, :columns], matrix[...], preferred_element_type=F32)
+        rest = jnp.dot(low[:, :columns], matrix[:, :BOX_NODES], preferred_element_type=F32)
+        result = both[:, :BOX_NODES] + (both[:, BOX_NODES:] + rest)
+        for number, child in enumerate(chosen):
+            for spot, pair in enumerate(near):
+                for k in range(2):
+                    start = number * 2 * height + spot * 16 + 8 * k
+                    emit(
+                        child,
+                        2 * pair + k,
+                        [result[start + height * part : start + height * part + 8] for part in range(2)],
+                    )
 
 
 def matrices():
@@ -317,7 +330,7 @@
     return [bit(row, 2 - k).astype(F32) for k in range(3)]
 
 
-def find_mask(slots, table, entries, high_hot, low_hot, total):
+def find_mask(slots, table, entries, high_hot, low_hot):
     iota = lax.broadcasted_iota(jnp.int32, (16, 128), 0).astype(F32)
     rows = [(iota + 16.0 * k).astype(BF16) for k in range(8)]
     one = jnp.ones((16, 128), BF16)
@@ -340,19 +353,16 @@
         return carry
 
     lax.fori_loop(0, 8, step, 0)
-    total[...] = jnp.zeros_like(total)
-
-    def add(index, carry):
-        lanes = pl.ds(pl.multiple_of(index * 4096, 4096), 4096)
-        total[...] += lax.dot_general(
-            high_hot[:, lanes],
-            low_hot[:, lanes],
+    parts = [
+        lax.dot_general(
+            high_hot[:, 4096 * k : 4096 * (k + 1)],
+            low_hot[:, 4096 * k : 4096 * (k + 1)],
             (((1,), (1,)), ((), ())),
             preferred_element_type=F32,
         )
-        return carry
-
-    lax.fori_loop(0, 2, add, 0)
+        for k in range(2)
+    ]
+    total = parts[0] + parts[1]
     mask = jnp.where(total[:128, :128] + total[128:, 128:] > 0.5, 1.0, 0.0)
     for k in range(8):
         lanes = slice(128 * (k % 2), 128 * (k % 2 + 1))
@@ -389,7 +399,6 @@
     entries,
     high_hot,
     low_hot,
-    total,
     arrive,
     leave,
 ):
@@ -402,7 +411,7 @@
     for fetch in fetches:
         fetch.start()
     fetches[0].wait()
-    find_mask(slots, table, entries, high_hot, low_hot, total)
+    find_mask(slots, table, entries, high_hot, low_hot)
     for fetch in fetches[1:]:
         fetch.wait()
     stores = [store_level(table, table_far, leave, k) for k in range(3)]
@@ -568,8 +577,8 @@
     zero = jnp.zeros((16, 128), BF16)
 
     def build(chunk, hot, spread):
-        for k in range(16):
-            sender = chunk * 16 + k
+        for k in range(8):
+            sender = chunk * 8 + k
             lanes = slice(128 * k, 128 * (k + 1))
 
             def row(number, height):
@@ -597,12 +606,17 @@
         )
 
     grid[...] = jnp.zeros_like(grid)
+    for k in range(2):
+        build(k, hots[k], spreads[k])
 
     def spread_step(index, carry):
-        for k in range(2):
-            build(2 * index + k, hots[k], spreads[k])
-        parts = [product(hots[k], spreads[k]) for k in range(2)]
-        grid[...] += parts[0] + parts[1]
+        for side in range(2):
+            here, there = 2 * side, 2 - 2 * side
+            parts = [product(hots[here + k], spreads[here + k]) for k in range(2)]
+            for k in range(2):
+                chunk = jnp.minimum(4 * index + 2 * side + 2 + k, 15)
+                build(chunk, hots[there + k], spreads[there + k])
+            grid[...] += parts[0] + parts[1]
         return carry
 
     lax.fori_loop(0, 4, spread_step, 0)
@@ -616,15 +630,6 @@
         result = result[:, :BOX_NODES] + (result[:, BOX_NODES:] + rest)
         for group in range(32):
             state[group, part] = result[8 * group : 8 * group + 8, :]
-
-
-def pieces(result):
-    for child in range(4):
-        for row in range(8):
-            start = child * 128 + row * 8
-            yield bits(child, 2), bits(row, 3), [
-                result[start + 64 * part : start + 64 * part + 8, :] for part in range(2)
-            ]
 
 
 def halves(value):
@@ -645,10 +650,11 @@
     hots,
     spreads,
     grid,
+    other,
+    turned,
+    highs,
+    lows,
     state,
-    turned,
-    high,
-    low,
 ):
     fetch_mask = fetch_mask_lines(table_far, table, arrive.at[6])
     fetch_mask.start()
@@ -662,32 +668,41 @@
     fetch_mask.wait()
     deposit(arrived, table, second, fetch_second, state, wide, cells, hots, spreads, grid)
 
-    def run(number, read):
-        return level(
+    def run(number, read, emit):
+        level(
             read,
             table,
             64 * (number - 1),
-            high,
-            low,
+            highs,
+            lows,
             matrix,
             4,
             8,
+            number % 2 == 0,
             fetches[number - 1 : number],
+            emit,
             fetch_matrix if number == 1 else None,
         )
 
+    def leaf(group, part):
+        return state[group, part]
+
     def read(group, part):
-        return state[group, part]
-
-    for (x, y), (r0, r1, r2), values in pieces(run(1, read)):
+        return other[group, part]
+
+    def keep(child, row, values):
         for part in range(2):
-            state[(2 * r0 + r1) * 8 + x * 4 + y * 2 + r2, part] = values[part]
-
-    for (x, y), (r0, r1, r2), values in pieces(run(2, read)):
-        start = ((r2 * 2 + x) * 8 + r0 * 4 + r1 * 2 + y) * 8
+            other[(row // 2) * 8 + child * 2 + row % 2, part] = values[part]
+
+    run(1, leaf, keep)
+
+    def turn_over(child, row, values):
+        start = ((row % 2 * 2 + child // 2) * 8 + row // 2 * 2 + child % 2) * 8
         for part in range(2):
             for half, value in enumerate(halves(values[part])):
                 turned[2 * part + half, start : start + 8, :] = value
+
+    run(2, read, turn_over)
 
     def across(group, part):
         b2x, b2y, b3x, b3y, t2x = bits(group, 5)
@@ -696,11 +711,11 @@
             [turned.at[2 * part + half][pl.ds(start, 8, stride=8), :] for half in range(2)], axis=1
         )
 
-    for (x, y), (r0, r1, r2), values in pieces(run(3, across)):
-        for part in range(2):
-            state[(2 * r0 + r1) * 8 + x * 4 + y * 2 + r2, part] = values[part]
-
-    for (x, y), (r0, r1, r2), values in pieces(run(4, read)):
+    run(3, across, keep)
+
+    def send(child, row, values):
+        x, y = bits(child, 2)
+        r0, r1, r2 = bits(row, 3)
         device = r2 * 32 + r0 * 16 + x * 8 + r1
         for upper in range(2):
             for part in range(2):
@@ -708,9 +723,11 @@
                     start = (device + 64 * upper) * 8 + y * 4 + half * 2 + part
                     out[pl.ds(start, 4, stride=16), :] = value[4 * upper : 4 * upper + 4]
 
+    run(4, read, send)
+
 
 def outer_kernel(
-    arrived, table_far, matrix_far, out, table, matrix, last, arrive, state, turned, high, low
+    arrived, table_far, matrix_far, out, table, matrix, last, arrive, state, turned, highs, lows
 ):
     first = [
         pltpu.make_async_copy(
@@ -737,32 +754,39 @@
             axis=1,
         )
 
-    def run(number, read):
-        return level(
+    def run(number, read, emit):
+        level(
             read,
             table,
             64 * (number - 5),
-            high,
-            low,
+            highs,
+            lows,
             matrix,
             4,
             8,
+            number % 2 == 0,
             first if number == 5 else fetches[number - 6 : number - 5],
+            emit,
             fetch_matrix if number == 5 else None,
         )
 
     def read(group, part):
         return state[group, part]
 
-    for (x, y), (i1, i0, j2), values in pieces(run(5, first_read)):
+    def keep(child, row, values):
+        i1, i0, j2 = bits(row, 3)
         for part in range(2):
-            state[(2 * i1 + j2) * 8 + x * 4 + y * 2 + i0, part] = values[part]
-
-    for (x, y), (r0, r1, i0), values in pieces(run(6, read)):
-        start = ((i0 * 2 + x) * 8 + r0 * 4 + r1 * 2 + y) * 8
+            state[(2 * i1 + j2) * 8 + child * 2 + i0, part] = values[part]
+
+    run(5, first_read, keep)
+
+    def turn_over(child, row, values):
+        start = ((row % 2 * 2 + child // 2) * 8 + row // 2 * 2 + child % 2) * 8
         for part in range(2):
             for half, value in enumerate(halves(values[part])):
                 turned[2 * part + half, start : start + 8, :] = value
+
+    run(6, read, turn_over)
 
     def across(group, part):
         i0, j1, t6x, j0, pair = bits(group, 5)
@@ -771,28 +795,31 @@
             [turned.at[2 * part + half][pl.ds(start, 8, stride=8), :] for half in range(2)], axis=1
         )
 
-    for (x, y), (t6x, j0, pair), values in pieces(run(7, across)):
+    def keep_last(child, row, values):
+        t6x, j0, pair = bits(row, 3)
         for part in range(2):
-            state[j0 * 16 + x * 8 + y * 4 + t6x * 2 + pair, part] = values[part]
-
-    result = level(read, table, 192, high, low, last, 2, 16, fetches[2:], fetch_last)
-    for child in range(2):
-        for row in range(16):
-            t7x, t7y, t6x, pair = bits(row, 4)
-            start = child * 256 + row * 8
-            line = 224 + child * 8 + row // 2
-            cosine = table[line, 0, 8 * (row % 2) : 8 * (row % 2) + 8, :]
-            sine = table[line, 1, 8 * (row % 2) : 8 * (row % 2) + 8, :]
-            real = result[start : start + 8, :]
-            imaginary = result[start + 128 : start + 136, :]
-            device = t6x * 32 + t7x * 16 + t7y * 2 + child
-            for part, whole in enumerate(
-                (real * cosine + imaginary * sine, imaginary * cosine - real * sine)
-            ):
-                for half, value in enumerate(halves(whole)):
-                    for upper in range(2):
-                        place = (device + 64 * upper) * 8 + pair * 4 + half * 2 + part
-                        out[pl.ds(place, 4, stride=32), :] = value[4 * upper : 4 * upper + 4]
+            state[j0 * 16 + child * 4 + t6x * 2 + pair, part] = values[part]
+
+    run(7, across, keep_last)
+
+    def send(child, row, values):
+        t7x, t7y, t6x, pair = bits(row, 4)
+        line = 224 + child * 8 + row // 2
+        cosine = table[line, 0, 8 * (row % 2) : 8 * (row % 2) + 8, :]
+        sine = table[line, 1, 8 * (row % 2) : 8 * (row % 2) + 8, :]
+        real, imaginary = values
+        device = t6x * 32 + t7x * 16 + t7y * 2 + child
+        for part, whole in enumerate(
+            (real * cosine + imaginary * sine, imaginary * cosine - real * sine)
+        ):
+            for half, value in enumerate(halves(whole)):
+                for upper in range(2):
+                    place = (device + 64 * upper) * 8 + pair * 4 + half * 2 + part
+                    out[pl.ds(place, 4, stride=32), :] = value[4 * upper : 4 * upper + 4]
+
+    level(
+        read, table, 192, highs, lows, last, 2, 16, True, fetches[2:], send, fetch_last
+    )
 
 
 def vmem(count):
@@ -857,7 +884,6 @@
             pltpu.VMEM((2, 128, 128), F32),
             pltpu.VMEM((256, 8192), BF16),
             pltpu.VMEM((256, 8192), BF16),
-            pltpu.VMEM((256, 256), F32),
             pltpu.SemaphoreType.DMA((3,)),
             pltpu.SemaphoreType.DMA((8,)),
         ],
@@ -884,8 +910,8 @@
 LEVEL_SCRATCH = [
     pltpu.VMEM((32, 2, 8, 256), F32),
     pltpu.VMEM((4, 256, 128), F32),
-    pltpu.VMEM((512, 1024), BF16),
-    pltpu.VMEM((512, 1024), BF16),
+    [pltpu.VMEM((256, 1024), BF16)] * 2,
+    [pltpu.VMEM((256, 1024), BF16)] * 2,
 ]
 
 
@@ -902,11 +928,12 @@
             pltpu.SemaphoreType.DMA((7,)),
             pltpu.VMEM((4096, 128), F32),
             pltpu.VMEM((3, 128, 128), F32),
-            [pltpu.VMEM((256, 2048), BF16)] * 2,
-            [pltpu.VMEM((512, 2048), BF16)] * 2,
+            [pltpu.VMEM((256, 1024), BF16)] * 4,
+            [pltpu.VMEM((512, 1024), BF16)] * 4,
             pltpu.VMEM((256, 512), F32),
         ]
-        + LEVEL_SCRATCH,
+        + LEVEL_SCRATCH
+        + LEVEL_SCRATCH[:1],
         name="inner",
         compiler_params=pltpu.CompilerParams(vmem_limit_bytes=52 << 20),
     )(

time: 85.9 us -> 86.9 us (1.012)
  Pallas kernels: 37.5 us -> 38.5 us
    pallas_call x1, Pallas kernels: 14 us -> 15.2 us  [inner_levels(): pl.pallas_call(inner_kernel, out_shape=jax.ShapeDtypeStruct((1024, 128),...]
where the time goes in v5:
time: 86.9 us; the launch traced here: 86.6 us
  Pallas kernels  38.5 us (44%)
  starting transfers between devices  20.1 us (23%)
  blocking collectives  17.8 us (20%)
  waiting for transfers between devices  7.56 us (9%)
  local copies, waits for them, and re-layouts  1.43 us (2%)
  other arithmetic  1.04 us (1%)
    all_to_all x2, starting transfers between devices, exchange(): lax.all_to_all(array, ('bx', 'by'), split_axis=0, concat_axis=0, tiled=True)  20.1 us
    all_to_all x1, blocking collectives, exchange(): lax.all_to_all(array, ('bx', 'by'), split_axis=0, concat_axis=0, tiled=True)  17.8 us
    pallas_call x1, Pallas kernels, inner_levels(): pl.pallas_call(inner_kernel, out_shape=jax.ShapeDtypeStruct((1024, 128),...  15.2 us
    pallas_call x1, Pallas kernels, inner_turns(): pl.pallas_call(inner_turns_kernel, out_shape=jax.ShapeDtypeStruct((258, 2...  9.7 us
    all_to_all x2, waiting for transfers between devices, exchange(): lax.all_to_all(array, ('bx', 'by'), split_axis=0, concat_axis=0, tiled=True)  7.56 us
    pallas_call x1, Pallas kernels, outer_levels(): pl.pallas_call(outer_kernel, out_shape=jax.ShapeDtypeStruct((1024, 128),...  6.03 us
    pallas_call x1, Pallas kernels, outer_turns(): pl.pallas_call(outer_turns_kernel, out_shape=jax.ShapeDtypeStruct((240, 2...  5.77 us
  transfers between devices with their start and end apart: 2, of which 2 were waited for; matrix products, arithmetic and copies ran while one was open for 1% of the time, Pallas kernels for 18%

profile of v5, /device:TPU:1, one launch (start us, length us, event | category | flops | bytes accessed | tf_op | source)
XLA Modules:
  0.0 86.6 jit_solution(11752889681076133711)
XLA Ops:
  0.0 1.7 %payload.1 = f32[512,128]{1,0:T(8,128)} custom-call(s32[2,128,128]{2,1,0:T(8,128)} %bitcast.28, f32[2,128,128]{2,1,0:T(8,128)} %bitcast.29), custom_call_target="tpu_custom_call" | custom-call | tf_op jit(solution)/shard_map/payload/pallas_call | solution.py:855
  1.7 11.5 %all-to-all-start = ((f32[128,4,128]{2,1,0:T(4,128)}), f32[128,4,128]{2,1,0:T(4,128)S(1)}, u32[]{:S(2)}, u32[]{:S(2)}) async-start(f32[128,4,128]{2,1,0:T(4,128)} %bitcast.27), calls=%async_computation | async-start | bytes 524288 | tf_op jit(solution)/shard_map/all_to_all | solution.py:978
  13.3 9.7 %inner_turns.1.table_far = f32[258,2,16,256]{3,2,1,0:T(8,128)} custom-call(s32[1]{0:T(128)} %bitcast.4.block_first_ref, s32[1]{0:T(128)} %bitcast.5.block_second_ref, s32[64,256]{1,0:T(8,128)} %bitcast.30, f32[24,256]{1,0:T(8,128)} %constant.32.clone.node_far.node, f32[1024,128]{1,0:T(8,128)} %constant.33.clone.speeds_far), custom_call_target="tpu_custom_call" | custom-call | tf_op jit(solution)/shard_map/inner_turns/pallas_call | solution.py:874
  23.0 0.0 copy-start
  23.0 1.1 %all-to-all-done = f32[128,4,128]{2,1,0:T(4,128)S(1)} async-done(((f32[128,4,128]{2,1,0:T(4,128)}), f32[128,4,128]{2,1,0:T(4,128)S(1)}, u32[]{:S(2)}, u32[]{:S(2)}) %all-to-all-start) | async-done | bytes 262176 | tf_op jit(solution)/shard_map/all_to_all | solution.py:978
  24.1 15.2 %inner.1 = f32[1024,128]{1,0:T(8,128)} custom-call(f32[512,128]{1,0:T(8,128)S(1)} %bitcast.25, f32[258,2,16,256]{3,2,1,0:T(8,128)} %inner_turns.1.table_far, bf16[2560,512]{1,0:T(8,128)(2,1)} %constant.34.clone.matrix_far), custom_call_target="tpu_custom_call" | custom-call | tf_op jit(solution)/shard_map/inner/pallas_call | solution.py:919
  39.3 8.6 %all-to-all-start.1 = ((f32[128,8,128]{2,1,0:T(8,128)}), f32[128,8,128]{2,1,0:T(8,128)S(1)}, u32[]{:S(2)}, u32[]{:S(2)}) async-start(f32[128,8,128]{2,1,0:T(8,128)} %bitcast.8), calls=%async_computation.1 | async-start | bytes 1048576 | tf_op jit(solution)/shard_map/all_to_all | solution.py:978
  48.0 0.9 dynamic-slice_reduce_fusion
  48.8 0.3 broadcast_in_dim.9.speeds
  49.1 0.0 copy-done
  49.1 5.8 %outer_turns.1.table_far = f32[240,2,16,256]{3,2,1,0:T(8,128)} custom-call(f32[24,256]{1,0:T(8,128)S(1)} %copy-done, f32[1792,128]{1,0:T(8,128)S(1)} %broadcast_in_dim.9.speeds), custom_call_target="tpu_custom_call" | custom-call | tf_op jit(solution)/shard_map/outer_turns/pallas_call | solution.py:896
  54.9 6.4 %all-to-all-done.1 = f32[128,8,128]{2,1,0:T(8,128)S(1)} async-done(((f32[128,8,128]{2,1,0:T(8,128)}), f32[128,8,128]{2,1,0:T(8,128)S(1)}, u32[]{:S(2)}, u32[]{:S(2)}) %all-to-all-start.1) | async-done | bytes 524320 | tf_op jit(solution)/shard_map/all_to_all | solution.py:978
  61.4 6.0 %outer.1 = f32[1024,128]{1,0:T(8,128)S(1)} custom-call(f32[1024,128]{1,0:T(8,128)S(1)} %bitcast.23, f32[240,2,16,256]{3,2,1,0:T(8,128)} %outer_turns.1.table_far, bf16[2560,512]{1,0:T(8,128)(2,1)} %constant.34.clone.matrix_far), custom_call_target="tpu_custom_call" | custom-call | tf_op jit(solution)/shard_map/outer/pallas_call | solution.py:947
  67.4 17.8 %all_to_all.15 = f32[128,8,128]{2,1,0:T(8,128)S(1)} all-to-all(f32[128,8,128]{2,1,0:T(8,128)S(1)} %bitcast.24), channel_id=1, replica_groups=mesh['bx'=8,'by'=16] {'bx','by'}, dimensions={0} | all-to-all | bytes 1048576 | tf_op jit(solution)/shard_map/all_to_all | solution.py:978
  85.2 0.3 slice_bitcast_fusion.1
  85.5 1.0 %maximum_bitcast_fusion = f32[16,1,16,1,2,256]{5,4,3,2,1,0:T(2,128)} fusion(f32[16,16,2,128]{3,2,1,0:T(2,128)S(1)} %get-tuple-element.10, f32[16,16,2,128]{3,2,1,0:T(2,128)S(1)} %get-tuple-element.9), kind=kLoop, calls=%fused_computation | loop fusion | flops 131072 | bytes 1048576 | tf_op jit(solution)/shard_map/reshape | solution.py:999
Async XLA Ops:
  1.7 22.4 %all-to-all-start = ((f32[128,4,128]{2,1,0:T(4,128)}), f32[128,4,128]{2,1,0:T(4,128)S(1)}, u32[]{:S(2)}, u32[]{:S(2)}) async-start(f32[128,4,128]{2,1,0:T(4,128)} %bitcast.27), calls=%async_computation | async-start | bytes 524288 | tf_op jit(solution)/shard_map/all_to_all | solution.py:978
  23.0 26.2 %copy-start = (f32[24,256]{1,0:T(8,128)S(1)}, f32[24,256]{1,0:T(8,128)}, u32[]{:S(2)}) copy-start(f32[24,256]{1,0:T(8,128)} %constant.32.clone.node_far.node) | copy-start | bytes 73732
  39.3 22.1 %all-to-all-start.1 = ((f32[128,8,128]{2,1,0:T(8,128)}), f32[128,8,128]{2,1,0:T(8,128)S(1)}, u32[]{:S(2)}, u32[]{:S(2)}) async-start(f32[128,8,128]{2,1,0:T(8,128)} %bitcast.8), calls=%async_computation.1 | async-start | bytes 1048576 | tf_op jit(solution)/shard_map/all_to_all | solution.py:978

commit v6 on v5

--- a/solution.py
+++ b/solution.py
@@ -263,66 +263,75 @@
 
 
 def level(
-    read, table, first_line, highs, lows, matrix, children, rows, by_rows, ready, emit, matrix_ready=None
+    read, table, first_line, highs, lows, matrix, children, rows, ready, emit, matrix_ready=None
 ):
     sources = 4 if children == 4 else 2
     pairs = rows // 2
-    columns = sources * BOX_NODES
+    parts = []
     for half in range(2):
-        high, low = highs[half], lows[half]
-        if by_rows:
-            chosen = list(range(children))
-            near = list(range(half * pairs // 2, (half + 1) * pairs // 2))
-        else:
-            chosen = list(range(half * children // 2, (half + 1) * children // 2))
-            near = list(range(pairs))
-        height = 16 * len(near)
-        for source in range(sources):
-            lanes = slice(source * BOX_NODES, (source + 1) * BOX_NODES)
-            if half == 0 and source < len(ready):
+        pieces = []
+        for source in range(half * sources // 2, (half + 1) * sources // 2):
+            lanes = slice(BOX_NODES * (source % 2), BOX_NODES * (source % 2 + 1))
+            high, low = highs[half], lows[half]
+            if source < len(ready):
                 ready[source].wait()
-            for spot, pair in enumerate(near):
+            for pair in range(pairs):
                 group = source * rows + 2 * pair
                 real, imaginary = (
                     jnp.concatenate([read(group, part), read(group + 1, part)])
                     for part in range(2)
                 )
-                for number, child in enumerate(chosen):
+                for child in range(children):
                     line = first_line + (source * pairs + pair) * children + child
                     cosine = table[line, 0]
                     sine = table[line, 1]
                     for part, value in enumerate(
                         (real * cosine - imaginary * sine, real * sine + imaginary * cosine)
                     ):
-                        place = (number * 2 + part) * height + spot * 16
+                        place = (child * 2 + part) * rows * 8 + pair * 16
                         value_high, value_low = split(value)
                         high[place : place + 16, lanes] = value_high
                         low[place : place + 16, lanes] = value_low
+            pieces += [high[:, lanes], low[:, lanes], high[:, lanes]]
         if half == 0 and matrix_ready is not None:
             matrix_ready.wait()
-        both = jnp.dot(high[:, :columns], matrix[...], preferred_element_type=F32)
-        rest = jnp.dot(low[:, :columns], matrix[:, :BOX_NODES], preferred_element_type=F32)
-        result = both[:, :BOX_NODES] + (both[:, BOX_NODES:] + rest)
-        for number, child in enumerate(chosen):
-            for spot, pair in enumerate(near):
-                for k in range(2):
-                    start = number * 2 * height + spot * 16 + 8 * k
-                    emit(
-                        child,
-                        2 * pair + k,
-                        [result[start + height * part : start + height * part + 8] for part in range(2)],
-                    )
+        depth = 384 * sources
+        parts.append(
+            jnp.dot(
+                jnp.concatenate(pieces, axis=1),
+                matrix[depth * half : depth * (half + 1), :],
+                preferred_element_type=F32,
+            )
+        )
+    result = parts[0] + parts[1]
+    for child in range(children):
+        for row in range(rows):
+            start = child * 2 * rows * 8 + row * 8
+            emit(
+                child,
+                row,
+                [result[start + rows * 8 * part : start + rows * 8 * part + 8] for part in range(2)],
+            )
+
+
+def three_parts(matrix):
+    high, low = two_parts(matrix)
+    high = high.reshape(-1, BOX_NODES, BOX_NODES)
+    low = low.reshape(-1, BOX_NODES, BOX_NODES)
+    return np.stack([high, high, low], axis=1).reshape(-1, BOX_NODES)
 
 
 def matrices():
-    basis = second_basis()
-    rows = [
-        stacked_matrix(2, 2),
-        stacked_matrix(1, 2),
-        basis[:, :256],
-        basis[:, 256:],
-    ]
-    return np.concatenate(two_parts(np.concatenate(rows)), axis=1)
+    high, low = two_parts(second_basis())
+    basis = np.concatenate([high, high, low], axis=0)
+    return np.concatenate(
+        [
+            three_parts(stacked_matrix(2, 2)),
+            three_parts(stacked_matrix(1, 2)),
+            basis[:, :256],
+            basis[:, 256:],
+        ]
+    )
 
 
 def sub_bits():
@@ -577,8 +586,8 @@
     zero = jnp.zeros((16, 128), BF16)
 
     def build(chunk, hot, spread):
-        for k in range(8):
-            sender = chunk * 8 + k
+        for k in range(16):
+            sender = chunk * 16 + k
             lanes = slice(128 * k, 128 * (k + 1))
 
             def row(number, height):
@@ -602,32 +611,27 @@
 
     def product(hot, spread):
         return lax.dot_general(
-            hot[...], spread[...], (((1,), (1,)), ((), ())), preferred_element_type=F32
+            spread[...], hot[...], (((1,), (1,)), ((), ())), preferred_element_type=F32
         )
 
     grid[...] = jnp.zeros_like(grid)
-    for k in range(2):
-        build(k, hots[k], spreads[k])
 
     def spread_step(index, carry):
-        for side in range(2):
-            here, there = 2 * side, 2 - 2 * side
-            parts = [product(hots[here + k], spreads[here + k]) for k in range(2)]
-            for k in range(2):
-                chunk = jnp.minimum(4 * index + 2 * side + 2 + k, 15)
-                build(chunk, hots[there + k], spreads[there + k])
-            grid[...] += parts[0] + parts[1]
+        for k in range(2):
+            build(2 * index + k, hots[k], spreads[k])
+        parts = [product(hots[k], spreads[k]) for k in range(2)]
+        grid[...] += parts[0] + parts[1]
         return carry
 
     lax.fori_loop(0, 4, spread_step, 0)
 
-    grid_high, grid_low = split(grid[...])
+    grid_high, grid_low = split(grid[...].T)
     fetch_second.wait()
+    operand = jnp.concatenate([grid_high, grid_low, grid_high], axis=1)
     for part in range(2):
-        basis = second[512 * part : 512 * (part + 1), :]
-        result = jnp.dot(grid_high, basis, preferred_element_type=F32)
-        rest = jnp.dot(grid_low, basis[:, :BOX_NODES], preferred_element_type=F32)
-        result = result[:, :BOX_NODES] + (result[:, BOX_NODES:] + rest)
+        result = jnp.dot(
+            operand, second[1536 * part : 1536 * (part + 1), :], preferred_element_type=F32
+        )
         for group in range(32):
             state[group, part] = result[8 * group : 8 * group + 8, :]
 
@@ -658,12 +662,12 @@
 ):
     fetch_mask = fetch_mask_lines(table_far, table, arrive.at[6])
     fetch_mask.start()
-    fetch_second = pltpu.make_async_copy(matrix_far.at[pl.ds(1536, 1024)], second, arrive.at[4])
+    fetch_second = pltpu.make_async_copy(matrix_far.at[pl.ds(4608, 3072)], second, arrive.at[4])
     fetch_second.start()
     fetches = [fetch_level(table_far, table, arrive, k) for k in range(4)]
     for fetch in fetches:
         fetch.start()
-    fetch_matrix = pltpu.make_async_copy(matrix_far.at[pl.ds(0, 1024)], matrix, arrive.at[5])
+    fetch_matrix = pltpu.make_async_copy(matrix_far.at[pl.ds(0, 3072)], matrix, arrive.at[5])
     fetch_matrix.start()
     fetch_mask.wait()
     deposit(arrived, table, second, fetch_second, state, wide, cells, hots, spreads, grid)
@@ -678,7 +682,6 @@
             matrix,
             4,
             8,
-            number % 2 == 0,
             fetches[number - 1 : number],
             emit,
             fetch_matrix if number == 1 else None,
@@ -738,8 +741,8 @@
     fetches = [
         fetch_level(table_far, table, arrive, k, 64 if k < 3 else 48) for k in range(1, 4)
     ]
-    fetch_matrix = pltpu.make_async_copy(matrix_far.at[pl.ds(0, 1024)], matrix, arrive.at[5])
-    fetch_last = pltpu.make_async_copy(matrix_far.at[pl.ds(1024, 512)], last, arrive.at[4])
+    fetch_matrix = pltpu.make_async_copy(matrix_far.at[pl.ds(0, 3072)], matrix, arrive.at[5])
+    fetch_last = pltpu.make_async_copy(matrix_far.at[pl.ds(3072, 1536)], last, arrive.at[4])
     for fetch in first + [fetch_matrix] + fetches + [fetch_last]:
         fetch.start()
 
@@ -764,7 +767,6 @@
             matrix,
             4,
             8,
-            number % 2 == 0,
             first if number == 5 else fetches[number - 6 : number - 5],
             emit,
             fetch_matrix if number == 5 else None,
@@ -818,7 +820,7 @@
                     out[pl.ds(place, 4, stride=32), :] = value[4 * upper : 4 * upper + 4]
 
     level(
-        read, table, 192, highs, lows, last, 2, 16, True, fetches[2:], send, fetch_last
+        read, table, 192, highs, lows, last, 2, 16, fetches[2:], send, fetch_last
     )
 
 
@@ -910,8 +912,8 @@
 LEVEL_SCRATCH = [
     pltpu.VMEM((32, 2, 8, 256), F32),
     pltpu.VMEM((4, 256, 128), F32),
-    [pltpu.VMEM((256, 1024), BF16)] * 2,
-    [pltpu.VMEM((256, 1024), BF16)] * 2,
+    [pltpu.VMEM((512, 512), BF16)] * 2,
+    [pltpu.VMEM((512, 512), BF16)] * 2,
 ]
 
 
@@ -922,15 +924,15 @@
         in_specs=vmem(1) + far(2),
         out_specs=vmem(1)[0],
         scratch_shapes=[
-            pltpu.VMEM((1024, 512), BF16),
-            pltpu.VMEM((1024, 512), BF16),
+            pltpu.VMEM((3072, 256), BF16),
+            pltpu.VMEM((3072, 256), BF16),
             pltpu.VMEM((258, 2, 16, 256), F32),
             pltpu.SemaphoreType.DMA((7,)),
             pltpu.VMEM((4096, 128), F32),
             pltpu.VMEM((3, 128, 128), F32),
-            [pltpu.VMEM((256, 1024), BF16)] * 4,
-            [pltpu.VMEM((512, 1024), BF16)] * 4,
-            pltpu.VMEM((256, 512), F32),
+            [pltpu.VMEM((256, 2048), BF16)] * 2,
+            [pltpu.VMEM((512, 2048), BF16)] * 2,
+            pltpu.VMEM((512, 256), F32),
         ]
         + LEVEL_SCRATCH
         + LEVEL_SCRATCH[:1],
@@ -951,8 +953,8 @@
         out_specs=vmem(1)[0],
         scratch_shapes=[
             pltpu.VMEM((240, 2, 16, 256), F32),
-            pltpu.VMEM((1024, 512), BF16),
-            pltpu.VMEM((512, 512), BF16),
+            pltpu.VMEM((3072, 256), BF16),
+            pltpu.VMEM((1536, 256), BF16),
             pltpu.SemaphoreType.DMA((10,)),
         ]
         + LEVEL_SCRATCH,

time: 86.9 us -> 91.5 us (1.053)
  Pallas kernels: 38.5 us -> 43.1 us
    pallas_call x1, Pallas kernels: 6.03 us -> 8.49 us  [outer_levels(): pl.pallas_call(outer_kernel, out_shape=jax.ShapeDtypeStruct((1024, 128),...]
    pallas_call x1, Pallas kernels: 15.2 us -> 17.4 us  [inner_levels(): pl.pallas_call(inner_kernel, out_shape=jax.ShapeDtypeStruct((1024, 128),...]
  transfers between devices with their start and end apart: 2 -> 2, of which waited for: 2 -> 2; matrix products, arithmetic and copies ran while one was open for 1% -> 1% of each run, Pallas kernels for 18% -> 17%
where the time goes in v6:
time: 91.5 us; the launch traced here: 91.2 us
  Pallas kernels  43.1 us (47%)
  starting transfers between devices  20.2 us (22%)
  blocking collectives  17.8 us (19%)
  waiting for transfers between devices  7.56 us (8%)
  local copies, waits for them, and re-layouts  1.43 us (2%)
  other arithmetic  1.04 us (1%)
    all_to_all x2, starting transfers between devices, exchange(): lax.all_to_all(array, ('bx', 'by'), split_axis=0, concat_axis=0, tiled=True)  20.2 us
    all_to_all x1, blocking collectives, exchange(): lax.all_to_all(array, ('bx', 'by'), split_axis=0, concat_axis=0, tiled=True)  17.8 us
    pallas_call x1, Pallas kernels, inner_levels(): pl.pallas_call(inner_kernel, out_shape=jax.ShapeDtypeStruct((1024, 128),...  17.4 us
    pallas_call x1, Pallas kernels, inner_turns(): pl.pallas_call(inner_turns_kernel, out_shape=jax.ShapeDtypeStruct((258, 2...  9.7 us
    pallas_call x1, Pallas kernels, outer_levels(): pl.pallas_call(outer_kernel, out_shape=jax.ShapeDtypeStruct((1024, 128),...  8.49 us
    all_to_all x2, waiting for transfers between devices, exchange(): lax.all_to_all(array, ('bx', 'by'), split_axis=0, concat_axis=0, tiled=True)  7.56 us
    pallas_call x1, Pallas kernels, outer_turns(): pl.pallas_call(outer_turns_kernel, out_shape=jax.ShapeDtypeStruct((240, 2...  5.77 us
  transfers between devices with their start and end apart: 2, of which 2 were waited for; matrix products, arithmetic and copies ran while one was open for 1% of the time, Pallas kernels for 17%

profile of v6, /device:TPU:1, one launch (start us, length us, event | category | flops | bytes accessed | tf_op | source)
XLA Modules:
  0.0 91.2 jit_solution(10766435731178335556)
XLA Ops:
  0.0 1.7 %payload.1 = f32[512,128]{1,0:T(8,128)} custom-call(s32[2,128,128]{2,1,0:T(8,128)} %bitcast.28, f32[2,128,128]{2,1,0:T(8,128)} %bitcast.29), custom_call_target="tpu_custom_call" | custom-call | tf_op jit(solution)/shard_map/payload/pallas_call | solution.py:857
  1.7 11.5 %all-to-all-start = ((f32[128,4,128]{2,1,0:T(4,128)}), f32[128,4,128]{2,1,0:T(4,128)S(1)}, u32[]{:S(2)}, u32[]{:S(2)}) async-start(f32[128,4,128]{2,1,0:T(4,128)} %bitcast.27), calls=%async_computation | async-start | bytes 524288 | tf_op jit(solution)/shard_map/all_to_all | solution.py:980
  13.3 9.7 %inner_turns.1.table_far = f32[258,2,16,256]{3,2,1,0:T(8,128)} custom-call(s32[1]{0:T(128)} %bitcast.4.block_first_ref, s32[1]{0:T(128)} %bitcast.5.block_second_ref, s32[64,256]{1,0:T(8,128)} %bitcast.30, f32[24,256]{1,0:T(8,128)} %constant.32.clone.node_far.node, f32[1024,128]{1,0:T(8,128)} %constant.33.clone.speeds_far), custom_call_target="tpu_custom_call" | custom-call | tf_op jit(solution)/shard_map/inner_turns/pallas_call | solution.py:876
  23.0 0.0 copy-start
  23.0 1.1 %all-to-all-done = f32[128,4,128]{2,1,0:T(4,128)S(1)} async-done(((f32[128,4,128]{2,1,0:T(4,128)}), f32[128,4,128]{2,1,0:T(4,128)S(1)}, u32[]{:S(2)}, u32[]{:S(2)}) %all-to-all-start) | async-done | bytes 262176 | tf_op jit(solution)/shard_map/all_to_all | solution.py:980
  24.1 17.4 %inner.1 = f32[1024,128]{1,0:T(8,128)} custom-call(f32[512,128]{1,0:T(8,128)S(1)} %bitcast.25, f32[258,2,16,256]{3,2,1,0:T(8,128)} %inner_turns.1.table_far, bf16[7680,256]{1,0:T(8,128)(2,1)} %constant.34.clone.matrix_far), custom_call_target="tpu_custom_call" | custom-call | tf_op jit(solution)/shard_map/inner/pallas_call | solution.py:921
  41.5 8.7 %all-to-all-start.1 = ((f32[128,8,128]{2,1,0:T(8,128)}), f32[128,8,128]{2,1,0:T(8,128)S(1)}, u32[]{:S(2)}, u32[]{:S(2)}) async-start(f32[128,8,128]{2,1,0:T(8,128)} %bitcast.8), calls=%async_computation.1 | async-start | bytes 1048576 | tf_op jit(solution)/shard_map/all_to_all | solution.py:980
  50.2 0.9 dynamic-slice_reduce_fusion
  51.1 0.3 broadcast_in_dim.9.speeds
  51.4 0.0 copy-done
  51.4 5.8 %outer_turns.1.table_far = f32[240,2,16,256]{3,2,1,0:T(8,128)} custom-call(f32[24,256]{1,0:T(8,128)S(1)} %copy-done, f32[1792,128]{1,0:T(8,128)S(1)} %broadcast_in_dim.9.speeds), custom_call_target="tpu_custom_call" | custom-call | tf_op jit(solution)/shard_map/outer_turns/pallas_call | solution.py:898
  57.1 6.4 %all-to-all-done.1 = f32[128,8,128]{2,1,0:T(8,128)S(1)} async-done(((f32[128,8,128]{2,1,0:T(8,128)}), f32[128,8,128]{2,1,0:T(8,128)S(1)}, u32[]{:S(2)}, u32[]{:S(2)}) %all-to-all-start.1) | async-done | bytes 524320 | tf_op jit(solution)/shard_map/all_to_all | solution.py:980
  63.6 8.5 %outer.1 = f32[1024,128]{1,0:T(8,128)S(1)} custom-call(f32[1024,128]{1,0:T(8,128)S(1)} %bitcast.23, f32[240,2,16,256]{3,2,1,0:T(8,128)} %outer_turns.1.table_far, bf16[7680,256]{1,0:T(8,128)(2,1)} %constant.34.clone.matrix_far), custom_call_target="tpu_custom_call" | custom-call | tf_op jit(solution)/shard_map/outer/pallas_call | solution.py:949
  72.1 17.8 %all_to_all.15 = f32[128,8,128]{2,1,0:T(8,128)S(1)} all-to-all(f32[128,8,128]{2,1,0:T(8,128)S(1)} %bitcast.24), channel_id=1, replica_groups=mesh['bx'=8,'by'=16] {'bx','by'}, dimensions={0} | all-to-all | bytes 1048576 | tf_op jit(solution)/shard_map/all_to_all | solution.py:980
  89.9 0.3 slice_bitcast_fusion.1
  90.2 1.0 %maximum_bitcast_fusion = f32[16,1,16,1,2,256]{5,4,3,2,1,0:T(2,128)} fusion(f32[16,16,2,128]{3,2,1,0:T(2,128)S(1)} %get-tuple-element.10, f32[16,16,2,128]{3,2,1,0:T(2,128)S(1)} %get-tuple-element.9), kind=kLoop, calls=%fused_computation | loop fusion | flops 131072 | bytes 1048576 | tf_op jit(solution)/shard_map/reshape | solution.py:1001
Async XLA Ops:
  1.7 22.4 %all-to-all-start = ((f32[128,4,128]{2,1,0:T(4,128)}), f32[128,4,128]{2,1,0:T(4,128)S(1)}, u32[]{:S(2)}, u32[]{:S(2)}) async-start(f32[128,4,128]{2,1,0:T(4,128)} %bitcast.27), calls=%async_computation | async-start | bytes 524288 | tf_op jit(solution)/shard_map/all_to_all | solution.py:980
  23.0 28.4 %copy-start = (f32[24,256]{1,0:T(8,128)S(1)}, f32[24,256]{1,0:T(8,128)}, u32[]{:S(2)}) copy-start(f32[24,256]{1,0:T(8,128)} %constant.32.clone.node_far.node) | copy-start | bytes 73732
  41.5 22.1 %all-to-all-start.1 = ((f32[128,8,128]{2,1,0:T(8,128)}), f32[128,8,128]{2,1,0:T(8,128)S(1)}, u32[]{:S(2)}, u32[]{:S(2)}) async-start(f32[128,8,128]{2,1,0:T(8,128)} %bitcast.8), calls=%async_computation.1 | async-start | bytes 1048576 | tf_op jit(solution)/shard_map/all_to_all | solution.py:980

commit v7 on v5

--- a/solution.py
+++ b/solution.py
@@ -577,8 +577,8 @@
     zero = jnp.zeros((16, 128), BF16)
 
     def build(chunk, hot, spread):
-        for k in range(8):
-            sender = chunk * 8 + k
+        for k in range(16):
+            sender = chunk * 16 + k
             lanes = slice(128 * k, 128 * (k + 1))
 
             def row(number, height):
@@ -600,23 +600,17 @@
                     above == jnp.full((16, 128), c, BF16), inside, zero
                 )
 
-    def product(hot, spread):
-        return lax.dot_general(
-            hot[...], spread[...], (((1,), (1,)), ((), ())), preferred_element_type=F32
-        )
-
     grid[...] = jnp.zeros_like(grid)
-    for k in range(2):
-        build(k, hots[k], spreads[k])
 
     def spread_step(index, carry):
-        for side in range(2):
-            here, there = 2 * side, 2 - 2 * side
-            parts = [product(hots[here + k], spreads[here + k]) for k in range(2)]
-            for k in range(2):
-                chunk = jnp.minimum(4 * index + 2 * side + 2 + k, 15)
-                build(chunk, hots[there + k], spreads[there + k])
-            grid[...] += parts[0] + parts[1]
+        for k in range(2):
+            build(2 * index + k, hots[k], spreads[k])
+        grid[...] += lax.dot_general(
+            jnp.concatenate([hots[0][...], hots[1][...]], axis=1),
+            jnp.concatenate([spreads[0][...], spreads[1][...]], axis=1),
+            (((1,), (1,)), ((), ())),
+            preferred_element_type=F32,
+        )
         return carry
 
     lax.fori_loop(0, 4, spread_step, 0)
@@ -928,8 +922,8 @@
             pltpu.SemaphoreType.DMA((7,)),
             pltpu.VMEM((4096, 128), F32),
             pltpu.VMEM((3, 128, 128), F32),
-            [pltpu.VMEM((256, 1024), BF16)] * 4,
-            [pltpu.VMEM((512, 1024), BF16)] * 4,
+            [pltpu.VMEM((256, 2048), BF16)] * 2,
+            [pltpu.VMEM((512, 2048), BF16)] * 2,
             pltpu.VMEM((256, 512), F32),
         ]
         + LEVEL_SCRATCH

time: 86.9 us -> 85.7 us (0.986)
  Pallas kernels: 38.5 us -> 37.3 us
    pallas_call x1, Pallas kernels: 15.2 us -> 14.1 us  [inner_levels(): pl.pallas_call(inner_kernel, out_shape=jax.ShapeDtypeStruct((1024, 128),...]
where the time goes in v7:
time: 85.7 us; the launch traced here: 85.4 us
  Pallas kernels  37.3 us (44%)
  starting transfers between devices  20.2 us (24%)
  blocking collectives  17.8 us (21%)
  waiting for transfers between devices  7.56 us (9%)
  local copies, waits for them, and re-layouts  1.43 us (2%)
  other arithmetic  1.04 us (1%)
    all_to_all x2, starting transfers between devices, exchange(): lax.all_to_all(array, ('bx', 'by'), split_axis=0, concat_axis=0, tiled=True)  20.2 us
    all_to_all x1, blocking collectives, exchange(): lax.all_to_all(array, ('bx', 'by'), split_axis=0, concat_axis=0, tiled=True)  17.8 us
    pallas_call x1, Pallas kernels, inner_levels(): pl.pallas_call(inner_kernel, out_shape=jax.ShapeDtypeStruct((1024, 128),...  14.1 us
    pallas_call x1, Pallas kernels, inner_turns(): pl.pallas_call(inner_turns_kernel, out_shape=jax.ShapeDtypeStruct((258, 2...  9.7 us
    all_to_all x2, waiting for transfers between devices, exchange(): lax.all_to_all(array, ('bx', 'by'), split_axis=0, concat_axis=0, tiled=True)  7.56 us
    pallas_call x1, Pallas kernels, outer_levels(): pl.pallas_call(outer_kernel, out_shape=jax.ShapeDtypeStruct((1024, 128),...  6.03 us
    pallas_call x1, Pallas kernels, outer_turns(): pl.pallas_call(outer_turns_kernel, out_shape=jax.ShapeDtypeStruct((240, 2...  5.77 us
    pallas_call x1, Pallas kernels, make_payload(): pl.pallas_call(payload_kernel, out_shape=jax.ShapeDtypeStruct((4 * DEVICE...  1.72 us
  transfers between devices with their start and end apart: 2, of which 2 were waited for; matrix products, arithmetic and copies ran while one was open for 1% of the time, Pallas kernels for 18%

profile of v7, /device:TPU:1, one launch (start us, length us, event | category | flops | bytes accessed | tf_op | source)
XLA Modules:
  0.0 85.4 jit_solution(15119007790379030127)
XLA Ops:
  0.0 1.7 %payload.1 = f32[512,128]{1,0:T(8,128)} custom-call(s32[2,128,128]{2,1,0:T(8,128)} %bitcast.28, f32[2,128,128]{2,1,0:T(8,128)} %bitcast.29), custom_call_target="tpu_custom_call" | custom-call | tf_op jit(solution)/shard_map/payload/pallas_call | solution.py:849
  1.7 11.5 %all-to-all-start = ((f32[128,4,128]{2,1,0:T(4,128)}), f32[128,4,128]{2,1,0:T(4,128)S(1)}, u32[]{:S(2)}, u32[]{:S(2)}) async-start(f32[128,4,128]{2,1,0:T(4,128)} %bitcast.27), calls=%async_computation | async-start | bytes 524288 | tf_op jit(solution)/shard_map/all_to_all | solution.py:972
  13.3 9.7 %inner_turns.1.table_far = f32[258,2,16,256]{3,2,1,0:T(8,128)} custom-call(s32[1]{0:T(128)} %bitcast.4.block_first_ref, s32[1]{0:T(128)} %bitcast.5.block_second_ref, s32[64,256]{1,0:T(8,128)} %bitcast.30, f32[24,256]{1,0:T(8,128)} %constant.32.clone.node_far.node, f32[1024,128]{1,0:T(8,128)} %constant.33.clone.speeds_far), custom_call_target="tpu_custom_call" | custom-call | tf_op jit(solution)/shard_map/inner_turns/pallas_call | solution.py:868
  23.0 0.0 copy-start
  23.0 1.1 %all-to-all-done = f32[128,4,128]{2,1,0:T(4,128)S(1)} async-done(((f32[128,4,128]{2,1,0:T(4,128)}), f32[128,4,128]{2,1,0:T(4,128)S(1)}, u32[]{:S(2)}, u32[]{:S(2)}) %all-to-all-start) | async-done | bytes 262176 | tf_op jit(solution)/shard_map/all_to_all | solution.py:972
  24.1 14.1 %inner.1 = f32[1024,128]{1,0:T(8,128)} custom-call(f32[512,128]{1,0:T(8,128)S(1)} %bitcast.25, f32[258,2,16,256]{3,2,1,0:T(8,128)} %inner_turns.1.table_far, bf16[2560,512]{1,0:T(8,128)(2,1)} %constant.34.clone.matrix_far), custom_call_target="tpu_custom_call" | custom-call | tf_op jit(solution)/shard_map/inner/pallas_call | solution.py:913
  38.2 8.7 %all-to-all-start.1 = ((f32[128,8,128]{2,1,0:T(8,128)}), f32[128,8,128]{2,1,0:T(8,128)S(1)}, u32[]{:S(2)}, u32[]{:S(2)}) async-start(f32[128,8,128]{2,1,0:T(8,128)} %bitcast.8), calls=%async_computation.1 | async-start | bytes 1048576 | tf_op jit(solution)/shard_map/all_to_all | solution.py:972
  46.9 0.9 dynamic-slice_reduce_fusion
  47.7 0.3 broadcast_in_dim.9.speeds
  48.0 0.0 copy-done
  48.0 5.8 %outer_turns.1.table_far = f32[240,2,16,256]{3,2,1,0:T(8,128)} custom-call(f32[24,256]{1,0:T(8,128)S(1)} %copy-done, f32[1792,128]{1,0:T(8,128)S(1)} %broadcast_in_dim.9.speeds), custom_call_target="tpu_custom_call" | custom-call | tf_op jit(solution)/shard_map/outer_turns/pallas_call | solution.py:890
  53.8 6.4 %all-to-all-done.1 = f32[128,8,128]{2,1,0:T(8,128)S(1)} async-done(((f32[128,8,128]{2,1,0:T(8,128)}), f32[128,8,128]{2,1,0:T(8,128)S(1)}, u32[]{:S(2)}, u32[]{:S(2)}) %all-to-all-start.1) | async-done | bytes 524320 | tf_op jit(solution)/shard_map/all_to_all | solution.py:972
  60.2 6.0 %outer.1 = f32[1024,128]{1,0:T(8,128)S(1)} custom-call(f32[1024,128]{1,0:T(8,128)S(1)} %bitcast.23, f32[240,2,16,256]{3,2,1,0:T(8,128)} %outer_turns.1.table_far, bf16[2560,512]{1,0:T(8,128)(2,1)} %constant.34.clone.matrix_far), custom_call_target="tpu_custom_call" | custom-call | tf_op jit(solution)/shard_map/outer/pallas_call | solution.py:941
  66.3 17.8 %all_to_all.15 = f32[128,8,128]{2,1,0:T(8,128)S(1)} all-to-all(f32[128,8,128]{2,1,0:T(8,128)S(1)} %bitcast.24), channel_id=1, replica_groups=mesh['bx'=8,'by'=16] {'bx','by'}, dimensions={0} | all-to-all | bytes 1048576 | tf_op jit(solution)/shard_map/all_to_all | solution.py:972
  84.1 0.3 slice_bitcast_fusion.1
  84.4 1.0 %maximum_bitcast_fusion = f32[16,1,16,1,2,256]{5,4,3,2,1,0:T(2,128)} fusion(f32[16,16,2,128]{3,2,1,0:T(2,128)S(1)} %get-tuple-element.10, f32[16,16,2,128]{3,2,1,0:T(2,128)S(1)} %get-tuple-element.9), kind=kLoop, calls=%fused_computation | loop fusion | flops 131072 | bytes 1048576 | tf_op jit(solution)/shard_map/reshape | solution.py:993
Async XLA Ops:
  1.7 22.4 %all-to-all-start = ((f32[128,4,128]{2,1,0:T(4,128)}), f32[128,4,128]{2,1,0:T(4,128)S(1)}, u32[]{:S(2)}, u32[]{:S(2)}) async-start(f32[128,4,128]{2,1,0:T(4,128)} %bitcast.27), calls=%async_computation | async-start | bytes 524288 | tf_op jit(solution)/shard_map/all_to_all | solution.py:972
  23.0 25.0 %copy-start = (f32[24,256]{1,0:T(8,128)S(1)}, f32[24,256]{1,0:T(8,128)}, u32[]{:S(2)}) copy-start(f32[24,256]{1,0:T(8,128)} %constant.32.clone.node_far.node) | copy-start | bytes 73732
  38.2 22.1 %all-to-all-start.1 = ((f32[128,8,128]{2,1,0:T(8,128)}), f32[128,8,128]{2,1,0:T(8,128)S(1)}, u32[]{:S(2)}, u32[]{:S(2)}) async-start(f32[128,8,128]{2,1,0:T(8,128)} %bitcast.8), calls=%async_computation.1 | async-start | bytes 1048576 | tf_op jit(solution)/shard_map/all_to_all | solution.py:972

commit v8 on v7

--- a/solution.py
+++ b/solution.py
@@ -262,6 +262,15 @@
     lax.fori_loop(0, 16, step, 0)
 
 
+def whole_product(high, low, matrix):
+    result = jnp.dot(
+        jnp.concatenate([high, low], axis=1),
+        jnp.concatenate([matrix, matrix], axis=0),
+        preferred_element_type=F32,
+    )
+    return result[:, :BOX_NODES] + result[:, BOX_NODES:]
+
+
 def level(
     read, table, first_line, highs, lows, matrix, children, rows, by_rows, ready, emit, matrix_ready=None
 ):
@@ -300,9 +309,7 @@
                         low[place : place + 16, lanes] = value_low
         if half == 0 and matrix_ready is not None:
             matrix_ready.wait()
-        both = jnp.dot(high[:, :columns], matrix[...], preferred_element_type=F32)
-        rest = jnp.dot(low[:, :columns], matrix[:, :BOX_NODES], preferred_element_type=F32)
-        result = both[:, :BOX_NODES] + (both[:, BOX_NODES:] + rest)
+        result = whole_product(high[:, :columns], low[:, :columns], matrix[...])
         for number, child in enumerate(chosen):
             for spot, pair in enumerate(near):
                 for k in range(2):
@@ -618,10 +625,7 @@
     grid_high, grid_low = split(grid[...])
     fetch_second.wait()
     for part in range(2):
-        basis = second[512 * part : 512 * (part + 1), :]
-        result = jnp.dot(grid_high, basis, preferred_element_type=F32)
-        rest = jnp.dot(grid_low, basis[:, :BOX_NODES], preferred_element_type=F32)
-        result = result[:, :BOX_NODES] + (result[:, BOX_NODES:] + rest)
+        result = whole_product(grid_high, grid_low, second[512 * part : 512 * (part + 1), :])
         for group in range(32):
             state[group, part] = result[8 * group : 8 * group + 8, :]
 

time: 85.7 us -> 87.9 us (1.026)
  Pallas kernels: 37.3 us -> 39.5 us
    pallas_call x1, Pallas kernels: 14.1 us -> 15.3 us  [inner_levels(): pl.pallas_call(inner_kernel, out_shape=jax.ShapeDtypeStruct((1024, 128),...]
    pallas_call x1, Pallas kernels: 6.03 us -> 6.99 us  [outer_levels(): pl.pallas_call(outer_kernel, out_shape=jax.ShapeDtypeStruct((1024, 128),...]
where the time goes in v8:
time: 87.9 us; the launch traced here: 87.6 us
  Pallas kernels  39.5 us (45%)
  starting transfers between devices  20.2 us (23%)
  blocking collectives  17.8 us (20%)
  waiting for transfers between devices  7.56 us (9%)
  local copies, waits for them, and re-layouts  1.43 us (2%)
  other arithmetic  1.04 us (1%)
    all_to_all x2, starting transfers between devices, exchange(): lax.all_to_all(array, ('bx', 'by'), split_axis=0, concat_axis=0, tiled=True)  20.2 us
    all_to_all x1, blocking collectives, exchange(): lax.all_to_all(array, ('bx', 'by'), split_axis=0, concat_axis=0, tiled=True)  17.8 us
    pallas_call x1, Pallas kernels, inner_levels(): pl.pallas_call(inner_kernel, out_shape=jax.ShapeDtypeStruct((1024, 128),...  15.3 us
    pallas_call x1, Pallas kernels, inner_turns(): pl.pallas_call(inner_turns_kernel, out_shape=jax.ShapeDtypeStruct((258, 2...  9.7 us
    all_to_all x2, waiting for transfers between devices, exchange(): lax.all_to_all(array, ('bx', 'by'), split_axis=0, concat_axis=0, tiled=True)  7.56 us
    pallas_call x1, Pallas kernels, outer_levels(): pl.pallas_call(outer_kernel, out_shape=jax.ShapeDtypeStruct((1024, 128),...  6.99 us
    pallas_call x1, Pallas kernels, outer_turns(): pl.pallas_call(outer_turns_kernel, out_shape=jax.ShapeDtypeStruct((240, 2...  5.77 us
  transfers between devices with their start and end apart: 2, of which 2 were waited for; matrix products, arithmetic and copies ran while one was open for 1% of the time, Pallas kernels for 18%

profile of v8, /device:TPU:1, one launch (start us, length us, event | category | flops | bytes accessed | tf_op | source)
XLA Modules:
  0.0 87.6 jit_solution(9705214589413757119)
XLA Ops:
  0.0 1.7 %payload.1 = f32[512,128]{1,0:T(8,128)} custom-call(s32[2,128,128]{2,1,0:T(8,128)} %bitcast.28, f32[2,128,128]{2,1,0:T(8,128)} %bitcast.29), custom_call_target="tpu_custom_call" | custom-call | tf_op jit(solution)/shard_map/payload/pallas_call | solution.py:853
  1.7 11.5 %all-to-all-start = ((f32[128,4,128]{2,1,0:T(4,128)}), f32[128,4,128]{2,1,0:T(4,128)S(1)}, u32[]{:S(2)}, u32[]{:S(2)}) async-start(f32[128,4,128]{2,1,0:T(4,128)} %bitcast.27), calls=%async_computation | async-start | bytes 524288 | tf_op jit(solution)/shard_map/all_to_all | solution.py:976
  13.3 9.7 %inner_turns.1.table_far = f32[258,2,16,256]{3,2,1,0:T(8,128)} custom-call(s32[1]{0:T(128)} %bitcast.4.block_first_ref, s32[1]{0:T(128)} %bitcast.5.block_second_ref, s32[64,256]{1,0:T(8,128)} %bitcast.30, f32[24,256]{1,0:T(8,128)} %constant.32.clone.node_far.node, f32[1024,128]{1,0:T(8,128)} %constant.33.clone.speeds_far), custom_call_target="tpu_custom_call" | custom-call | tf_op jit(solution)/shard_map/inner_turns/pallas_call | solution.py:872
  23.0 0.0 copy-start
  23.0 1.1 %all-to-all-done = f32[128,4,128]{2,1,0:T(4,128)S(1)} async-done(((f32[128,4,128]{2,1,0:T(4,128)}), f32[128,4,128]{2,1,0:T(4,128)S(1)}, u32[]{:S(2)}, u32[]{:S(2)}) %all-to-all-start) | async-done | bytes 262176 | tf_op jit(solution)/shard_map/all_to_all | solution.py:976
  24.1 15.3 %inner.1 = f32[1024,128]{1,0:T(8,128)} custom-call(f32[512,128]{1,0:T(8,128)S(1)} %bitcast.25, f32[258,2,16,256]{3,2,1,0:T(8,128)} %inner_turns.1.table_far, bf16[2560,512]{1,0:T(8,128)(2,1)} %constant.34.clone.matrix_far), custom_call_target="tpu_custom_call" | custom-call | tf_op jit(solution)/shard_map/inner/pallas_call | solution.py:917
  39.4 8.7 %all-to-all-start.1 = ((f32[128,8,128]{2,1,0:T(8,128)}), f32[128,8,128]{2,1,0:T(8,128)S(1)}, u32[]{:S(2)}, u32[]{:S(2)}) async-start(f32[128,8,128]{2,1,0:T(8,128)} %bitcast.8), calls=%async_computation.1 | async-start | bytes 1048576 | tf_op jit(solution)/shard_map/all_to_all | solution.py:976
  48.1 0.9 dynamic-slice_reduce_fusion
  48.9 0.3 broadcast_in_dim.9.speeds
  49.2 0.0 copy-done
  49.2 5.8 %outer_turns.1.table_far = f32[240,2,16,256]{3,2,1,0:T(8,128)} custom-call(f32[24,256]{1,0:T(8,128)S(1)} %copy-done, f32[1792,128]{1,0:T(8,128)S(1)} %broadcast_in_dim.9.speeds), custom_call_target="tpu_custom_call" | custom-call | tf_op jit(solution)/shard_map/outer_turns/pallas_call | solution.py:894
  55.0 6.4 %all-to-all-done.1 = f32[128,8,128]{2,1,0:T(8,128)S(1)} async-done(((f32[128,8,128]{2,1,0:T(8,128)}), f32[128,8,128]{2,1,0:T(8,128)S(1)}, u32[]{:S(2)}, u32[]{:S(2)}) %all-to-all-start.1) | async-done | bytes 524320 | tf_op jit(solution)/shard_map/all_to_all | solution.py:976
  61.5 7.0 %outer.1 = f32[1024,128]{1,0:T(8,128)S(1)} custom-call(f32[1024,128]{1,0:T(8,128)S(1)} %bitcast.23, f32[240,2,16,256]{3,2,1,0:T(8,128)} %outer_turns.1.table_far, bf16[2560,512]{1,0:T(8,128)(2,1)} %constant.34.clone.matrix_far), custom_call_target="tpu_custom_call" | custom-call | tf_op jit(solution)/shard_map/outer/pallas_call | solution.py:945
  68.5 17.8 %all_to_all.15 = f32[128,8,128]{2,1,0:T(8,128)S(1)} all-to-all(f32[128,8,128]{2,1,0:T(8,128)S(1)} %bitcast.24), channel_id=1, replica_groups=mesh['bx'=8,'by'=16] {'bx','by'}, dimensions={0} | all-to-all | bytes 1048576 | tf_op jit(solution)/shard_map/all_to_all | solution.py:976
  86.3 0.3 slice_bitcast_fusion.1
  86.6 1.0 %maximum_bitcast_fusion = f32[16,1,16,1,2,256]{5,4,3,2,1,0:T(2,128)} fusion(f32[16,16,2,128]{3,2,1,0:T(2,128)S(1)} %get-tuple-element.10, f32[16,16,2,128]{3,2,1,0:T(2,128)S(1)} %get-tuple-element.9), kind=kLoop, calls=%fused_computation | loop fusion | flops 131072 | bytes 1048576 | tf_op jit(solution)/shard_map/reshape | solution.py:997
Async XLA Ops:
  1.7 22.4 %all-to-all-start = ((f32[128,4,128]{2,1,0:T(4,128)}), f32[128,4,128]{2,1,0:T(4,128)S(1)}, u32[]{:S(2)}, u32[]{:S(2)}) async-start(f32[128,4,128]{2,1,0:T(4,128)} %bitcast.27), calls=%async_computation | async-start | bytes 524288 | tf_op jit(solution)/shard_map/all_to_all | solution.py:976
  23.0 26.3 %copy-start = (f32[24,256]{1,0:T(8,128)S(1)}, f32[24,256]{1,0:T(8,128)}, u32[]{:S(2)}) copy-start(f32[24,256]{1,0:T(8,128)} %constant.32.clone.node_far.node) | copy-start | bytes 73732
  39.4 22.1 %all-to-all-start.1 = ((f32[128,8,128]{2,1,0:T(8,128)}), f32[128,8,128]{2,1,0:T(8,128)S(1)}, u32[]{:S(2)}, u32[]{:S(2)}) async-start(f32[128,8,128]{2,1,0:T(8,128)} %bitcast.8), calls=%async_computation.1 | async-start | bytes 1048576 | tf_op jit(solution)/shard_map/all_to_all | solution.py:976

commit v9 on v7

--- a/solution.py
+++ b/solution.py
@@ -863,6 +863,33 @@
     )(place, amp)
 
 
+def result_kernel(weights, out, leave):
+    stores = [
+        pltpu.make_async_copy(
+            weights.at[:, :, half],
+            out.at[:, 0, :, 0, :, pl.ds(128 * half, 128)],
+            leave.at[half],
+        )
+        for half in range(2)
+    ]
+    for store in stores:
+        store.start()
+    for store in stores:
+        store.wait()
+
+
+def place_result(weights):
+    return pl.pallas_call(
+        result_kernel,
+        out_shape=jax.ShapeDtypeStruct((LEAVES, 1, LEAVES, 1, 2, BOX_NODES), F32),
+        in_specs=vmem(1),
+        out_specs=far(1)[0],
+        scratch_shapes=[pltpu.SemaphoreType.DMA((2,))],
+        name="result",
+        compiler_params=pltpu.CompilerParams(vmem_limit_bytes=16 << 20),
+    )(weights)
+
+
 def inner_turns(block_first, block_second, slots):
     speeds = np.repeat(inner_speeds()[:, None], 128, axis=1)
     return pl.pallas_call(
@@ -988,9 +1015,7 @@
     speeds = jnp.broadcast_to(speeds[:, None], (7 * 256, 128))
     weights = outer_levels(weights, outer_turns(speeds))
     weights = exchange(weights.reshape(DEVICES, 8, 128))
-    weights = weights.reshape(LEAVES, LEAVES, 2, 2, 128)
-    weights = jnp.concatenate([weights[:, :, 0], weights[:, :, 1]], axis=-1)
-    return weights.reshape(LEAVES, 1, LEAVES, 1, 2, BOX_NODES)
+    return place_result(weights.reshape(LEAVES, LEAVES, 2, 2, 128))
 
 
 def solution(mesh):

time: 85.7 us -> 85.4 us (level)
  other arithmetic: 1.04 us -> 0 us
    reshape x1 -> x0, other arithmetic: 1.04 us -> none  [shards(): return weights.reshape(LEAVES, 1, LEAVES, 1, 2, BOX_NODES)]
where the time goes in v9:
time: 85.4 us; the launch traced here: 85.1 us
  Pallas kernels  38.1 us (45%)
  starting transfers between devices  20.2 us (24%)
  blocking collectives  17.8 us (21%)
  waiting for transfers between devices  7.56 us (9%)
  local copies, waits for them, and re-layouts  1.15 us (1%)
    all_to_all x2, starting transfers between devices, exchange(): lax.all_to_all(array, ('bx', 'by'), split_axis=0, concat_axis=0, tiled=True)  20.2 us
    all_to_all x1, blocking collectives, exchange(): lax.all_to_all(array, ('bx', 'by'), split_axis=0, concat_axis=0, tiled=True)  17.8 us
    pallas_call x1, Pallas kernels, inner_levels(): pl.pallas_call(inner_kernel, out_shape=jax.ShapeDtypeStruct((1024, 128),...  14.1 us
    pallas_call x1, Pallas kernels, inner_turns(): pl.pallas_call(inner_turns_kernel, out_shape=jax.ShapeDtypeStruct((258, 2...  9.7 us
    all_to_all x2, waiting for transfers between devices, exchange(): lax.all_to_all(array, ('bx', 'by'), split_axis=0, concat_axis=0, tiled=True)  7.56 us
    pallas_call x1, Pallas kernels, outer_levels(): pl.pallas_call(outer_kernel, out_shape=jax.ShapeDtypeStruct((1024, 128),...  6.03 us
    pallas_call x1, Pallas kernels, outer_turns(): pl.pallas_call(outer_turns_kernel, out_shape=jax.ShapeDtypeStruct((240, 2...  5.78 us
    pallas_call x1, Pallas kernels, make_payload(): pl.pallas_call(payload_kernel, out_shape=jax.ShapeDtypeStruct((4 * DEVICE...  1.72 us
  transfers between devices with their start and end apart: 2, of which 2 were waited for; matrix products, arithmetic and copies ran while one was open for 1% of the time, Pallas kernels for 18%

profile of v9, /device:TPU:1, one launch (start us, length us, event | category | flops | bytes accessed | tf_op | source)
XLA Modules:
  0.0 85.1 jit_solution(2987994128009195929)
XLA Ops:
  0.0 1.7 %payload.1 = f32[512,128]{1,0:T(8,128)} custom-call(s32[2,128,128]{2,1,0:T(8,128)} %bitcast.18, f32[2,128,128]{2,1,0:T(8,128)} %bitcast.19), custom_call_target="tpu_custom_call" | custom-call | tf_op jit(solution)/shard_map/payload/pallas_call | solution.py:849
  1.7 11.5 %all-to-all-start = ((f32[128,4,128]{2,1,0:T(4,128)}), f32[128,4,128]{2,1,0:T(4,128)S(1)}, u32[]{:S(2)}, u32[]{:S(2)}) async-start(f32[128,4,128]{2,1,0:T(4,128)} %bitcast.17), calls=%async_computation | async-start | bytes 524288 | tf_op jit(solution)/shard_map/all_to_all | solution.py:999
  13.3 9.7 %inner_turns.1.table_far = f32[258,2,16,256]{3,2,1,0:T(8,128)} custom-call(s32[1]{0:T(128)} %bitcast.4.block_first_ref, s32[1]{0:T(128)} %bitcast.5.block_second_ref, s32[64,256]{1,0:T(8,128)} %bitcast.20, f32[24,256]{1,0:T(8,128)} %constant.32.clone.node_far.node, f32[1024,128]{1,0:T(8,128)} %constant.33.clone.speeds_far), custom_call_target="tpu_custom_call" | custom-call | tf_op jit(solution)/shard_map/inner_turns/pallas_call | solution.py:895
  23.0 0.0 copy-start
  23.0 1.1 %all-to-all-done = f32[128,4,128]{2,1,0:T(4,128)S(1)} async-done(((f32[128,4,128]{2,1,0:T(4,128)}), f32[128,4,128]{2,1,0:T(4,128)S(1)}, u32[]{:S(2)}, u32[]{:S(2)}) %all-to-all-start) | async-done | bytes 262176 | tf_op jit(solution)/shard_map/all_to_all | solution.py:999
  24.1 14.1 %inner.1 = f32[1024,128]{1,0:T(8,128)} custom-call(f32[512,128]{1,0:T(8,128)S(1)} %bitcast.16, f32[258,2,16,256]{3,2,1,0:T(8,128)} %inner_turns.1.table_far, bf16[2560,512]{1,0:T(8,128)(2,1)} %constant.34.clone.matrix_far), custom_call_target="tpu_custom_call" | custom-call | tf_op jit(solution)/shard_map/inner/pallas_call | solution.py:940
  38.2 8.7 %all-to-all-start.1 = ((f32[128,8,128]{2,1,0:T(8,128)}), f32[128,8,128]{2,1,0:T(8,128)S(1)}, u32[]{:S(2)}, u32[]{:S(2)}) async-start(f32[128,8,128]{2,1,0:T(8,128)} %bitcast.8), calls=%async_computation.1 | async-start | bytes 1048576 | tf_op jit(solution)/shard_map/all_to_all | solution.py:999
  46.9 0.9 %dynamic-slice_reduce_fusion = f32[1792]{0:T(1024)S(1)} fusion(f32[128,1792]{1,0:T(8,128)} %constant.35.clone, s32[]{:T(128)S(6)} %select_n.4), kind=kLoop, calls=%fused_computation | loop fusion | bytes 14340 | tf_op jit(solution)/shard_map/jit(dynamic_index_in_dim)/dynamic_slice | solution.py:1014
  47.7 0.3 broadcast_in_dim.9.speeds
  48.0 0.0 copy-done
  48.0 5.8 %outer_turns.1.table_far = f32[240,2,16,256]{3,2,1,0:T(8,128)} custom-call(f32[24,256]{1,0:T(8,128)S(1)} %copy-done, f32[1792,128]{1,0:T(8,128)S(1)} %broadcast_in_dim.9.speeds), custom_call_target="tpu_custom_call" | custom-call | tf_op jit(solution)/shard_map/outer_turns/pallas_call | solution.py:917
  53.8 6.4 %all-to-all-done.1 = f32[128,8,128]{2,1,0:T(8,128)S(1)} async-done(((f32[128,8,128]{2,1,0:T(8,128)}), f32[128,8,128]{2,1,0:T(8,128)S(1)}, u32[]{:S(2)}, u32[]{:S(2)}) %all-to-all-start.1) | async-done | bytes 524320 | tf_op jit(solution)/shard_map/all_to_all | solution.py:999
  60.2 6.0 %outer.1 = f32[1024,128]{1,0:T(8,128)S(1)} custom-call(f32[1024,128]{1,0:T(8,128)S(1)} %bitcast.13, f32[240,2,16,256]{3,2,1,0:T(8,128)} %outer_turns.1.table_far, bf16[2560,512]{1,0:T(8,128)(2,1)} %constant.34.clone.matrix_far), custom_call_target="tpu_custom_call" | custom-call | tf_op jit(solution)/shard_map/outer/pallas_call | solution.py:968
  66.3 17.8 %all_to_all.15 = f32[128,8,128]{2,1,0:T(8,128)S(1)} all-to-all(f32[128,8,128]{2,1,0:T(8,128)S(1)} %bitcast.14), channel_id=1, replica_groups=mesh['bx'=8,'by'=16] {'bx','by'}, dimensions={0} | all-to-all | bytes 1048576 | tf_op jit(solution)/shard_map/all_to_all | solution.py:999
  84.1 0.8 result.1
Async XLA Ops:
  1.7 22.4 %all-to-all-start = ((f32[128,4,128]{2,1,0:T(4,128)}), f32[128,4,128]{2,1,0:T(4,128)S(1)}, u32[]{:S(2)}, u32[]{:S(2)}) async-start(f32[128,4,128]{2,1,0:T(4,128)} %bitcast.17), calls=%async_computation | async-start | bytes 524288 | tf_op jit(solution)/shard_map/all_to_all | solution.py:999
  23.0 25.0 %copy-start = (f32[24,256]{1,0:T(8,128)S(1)}, f32[24,256]{1,0:T(8,128)}, u32[]{:S(2)}) copy-start(f32[24,256]{1,0:T(8,128)} %constant.32.clone.node_far.node) | copy-start | bytes 73732
  38.2 22.1 %all-to-all-start.1 = ((f32[128,8,128]{2,1,0:T(8,128)}), f32[128,8,128]{2,1,0:T(8,128)S(1)}, u32[]{:S(2)}, u32[]{:S(2)}) async-start(f32[128,8,128]{2,1,0:T(8,128)} %bitcast.8), calls=%async_computation.1 | async-start | bytes 1048576 | tf_op jit(solution)/shard_map/all_to_all | solution.py:999

commit v10 on v9

--- a/solution.py
+++ b/solution.py
@@ -829,20 +829,32 @@
 
 
 def payload_kernel(place_far, amp_far, out_far, place, amp, out, arrive, leave):
+    part = DEVICES // 2
     fetches = [
-        pltpu.make_async_copy(place_far, place, arrive.at[0]),
-        pltpu.make_async_copy(amp_far, amp, arrive.at[1]),
+        pltpu.make_async_copy(
+            far_ref.at[:, pl.ds(part * half, part)],
+            near_ref.at[:, pl.ds(part * half, part)],
+            arrive.at[2 * half + k],
+        )
+        for half in range(2)
+        for k, (far_ref, near_ref) in enumerate(((place_far, place), (amp_far, amp)))
     ]
     for fetch in fetches:
         fetch.start()
-    for fetch in fetches:
-        fetch.wait()
-    for k in range(2):
-        out[pl.ds(k, DEVICES, stride=4), :] = place[k].astype(F32)
-        out[pl.ds(2 + k, DEVICES, stride=4), :] = amp[k]
-    store = pltpu.make_async_copy(out, out_far, leave)
-    store.start()
-    store.wait()
+    stores = []
+    for half in range(2):
+        for fetch in fetches[2 * half : 2 * half + 2]:
+            fetch.wait()
+        chosen = slice(part * half, part * (half + 1))
+        for k in range(2):
+            start = 4 * part * half + k
+            out[pl.ds(start, part, stride=4), :] = place[k, chosen].astype(F32)
+            out[pl.ds(start + 2, part, stride=4), :] = amp[k, chosen]
+        rows = pl.ds(4 * part * half, 4 * part)
+        stores.append(pltpu.make_async_copy(out.at[rows], out_far.at[rows], leave.at[half]))
+        stores[half].start()
+    for store in stores:
+        store.wait()
 
 
 def make_payload(place, amp):
@@ -855,8 +867,8 @@
             pltpu.VMEM((2, DEVICES, 128), jnp.int32),
             pltpu.VMEM((2, DEVICES, 128), F32),
             pltpu.VMEM((4 * DEVICES, 128), F32),
+            pltpu.SemaphoreType.DMA((4,)),
             pltpu.SemaphoreType.DMA((2,)),
-            pltpu.SemaphoreType.DMA,
         ],
         name="payload",
         compiler_params=pltpu.CompilerParams(vmem_limit_bytes=60 << 20),

time: 85.4 us -> 85.3 us (level)
  no operation moved by 1% of the time
where the time goes in v10:
time: 85.3 us; the launch traced here: 85 us
  Pallas kernels  38 us (45%)
  starting transfers between devices  20.2 us (24%)
  blocking collectives  17.8 us (21%)
  waiting for transfers between devices  7.55 us (9%)
  local copies, waits for them, and re-layouts  1.15 us (1%)
    all_to_all x2, starting transfers between devices, exchange(): lax.all_to_all(array, ('bx', 'by'), split_axis=0, concat_axis=0, tiled=True)  20.2 us
    all_to_all x1, blocking collectives, exchange(): lax.all_to_all(array, ('bx', 'by'), split_axis=0, concat_axis=0, tiled=True)  17.8 us
    pallas_call x1, Pallas kernels, inner_levels(): pl.pallas_call(inner_kernel, out_shape=jax.ShapeDtypeStruct((1024, 128),...  14.1 us
    pallas_call x1, Pallas kernels, inner_turns(): pl.pallas_call(inner_turns_kernel, out_shape=jax.ShapeDtypeStruct((258, 2...  9.7 us
    all_to_all x2, waiting for transfers between devices, exchange(): lax.all_to_all(array, ('bx', 'by'), split_axis=0, concat_axis=0, tiled=True)  7.55 us
    pallas_call x1, Pallas kernels, outer_levels(): pl.pallas_call(outer_kernel, out_shape=jax.ShapeDtypeStruct((1024, 128),...  6.03 us
    pallas_call x1, Pallas kernels, outer_turns(): pl.pallas_call(outer_turns_kernel, out_shape=jax.ShapeDtypeStruct((240, 2...  5.78 us
  transfers between devices with their start and end apart: 2, of which 2 were waited for; matrix products, arithmetic and copies ran while one was open for 1% of the time, Pallas kernels for 18%

profile of v10, /device:TPU:1, one launch (start us, length us, event | category | flops | bytes accessed | tf_op | source)
XLA Modules:
  0.0 85.0 jit_solution(14629614723745337809)
XLA Ops:
  0.0 1.6 %payload.1 = f32[512,128]{1,0:T(8,128)} custom-call(s32[2,128,128]{2,1,0:T(8,128)} %bitcast.18, f32[2,128,128]{2,1,0:T(8,128)} %bitcast.19), custom_call_target="tpu_custom_call" | custom-call | tf_op jit(solution)/shard_map/payload/pallas_call | solution.py:861
  1.7 11.5 %all-to-all-start = ((f32[128,4,128]{2,1,0:T(4,128)}), f32[128,4,128]{2,1,0:T(4,128)S(1)}, u32[]{:S(2)}, u32[]{:S(2)}) async-start(f32[128,4,128]{2,1,0:T(4,128)} %bitcast.17), calls=%async_computation | async-start | bytes 524288 | tf_op jit(solution)/shard_map/all_to_all | solution.py:1011
  13.2 9.7 %inner_turns.1.table_far = f32[258,2,16,256]{3,2,1,0:T(8,128)} custom-call(s32[1]{0:T(128)} %bitcast.4.block_first_ref, s32[1]{0:T(128)} %bitcast.5.block_second_ref, s32[64,256]{1,0:T(8,128)} %bitcast.20, f32[24,256]{1,0:T(8,128)} %constant.32.clone.node_far.node, f32[1024,128]{1,0:T(8,128)} %constant.33.clone.speeds_far), custom_call_target="tpu_custom_call" | custom-call | tf_op jit(solution)/shard_map/inner_turns/pallas_call | solution.py:907
  22.9 0.0 copy-start
  22.9 1.1 %all-to-all-done = f32[128,4,128]{2,1,0:T(4,128)S(1)} async-done(((f32[128,4,128]{2,1,0:T(4,128)}), f32[128,4,128]{2,1,0:T(4,128)S(1)}, u32[]{:S(2)}, u32[]{:S(2)}) %all-to-all-start) | async-done | bytes 262176 | tf_op jit(solution)/shard_map/all_to_all | solution.py:1011
  24.0 14.1 %inner.1 = f32[1024,128]{1,0:T(8,128)} custom-call(f32[512,128]{1,0:T(8,128)S(1)} %bitcast.16, f32[258,2,16,256]{3,2,1,0:T(8,128)} %inner_turns.1.table_far, bf16[2560,512]{1,0:T(8,128)(2,1)} %constant.34.clone.matrix_far), custom_call_target="tpu_custom_call" | custom-call | tf_op jit(solution)/shard_map/inner/pallas_call | solution.py:952
  38.1 8.7 %all-to-all-start.1 = ((f32[128,8,128]{2,1,0:T(8,128)}), f32[128,8,128]{2,1,0:T(8,128)S(1)}, u32[]{:S(2)}, u32[]{:S(2)}) async-start(f32[128,8,128]{2,1,0:T(8,128)} %bitcast.8), calls=%async_computation.1 | async-start | bytes 1048576 | tf_op jit(solution)/shard_map/all_to_all | solution.py:1011
  46.8 0.9 %dynamic-slice_reduce_fusion = f32[1792]{0:T(1024)S(1)} fusion(f32[128,1792]{1,0:T(8,128)} %constant.35.clone, s32[]{:T(128)S(6)} %select_n.4), kind=kLoop, calls=%fused_computation | loop fusion | bytes 14340 | tf_op jit(solution)/shard_map/jit(dynamic_index_in_dim)/dynamic_slice | solution.py:1026
  47.6 0.3 broadcast_in_dim.9.speeds
  47.9 0.0 copy-done
  47.9 5.8 %outer_turns.1.table_far = f32[240,2,16,256]{3,2,1,0:T(8,128)} custom-call(f32[24,256]{1,0:T(8,128)S(1)} %copy-done, f32[1792,128]{1,0:T(8,128)S(1)} %broadcast_in_dim.9.speeds), custom_call_target="tpu_custom_call" | custom-call | tf_op jit(solution)/shard_map/outer_turns/pallas_call | solution.py:929
  53.7 6.4 %all-to-all-done.1 = f32[128,8,128]{2,1,0:T(8,128)S(1)} async-done(((f32[128,8,128]{2,1,0:T(8,128)}), f32[128,8,128]{2,1,0:T(8,128)S(1)}, u32[]{:S(2)}, u32[]{:S(2)}) %all-to-all-start.1) | async-done | bytes 524320 | tf_op jit(solution)/shard_map/all_to_all | solution.py:1011
  60.2 6.0 %outer.1 = f32[1024,128]{1,0:T(8,128)S(1)} custom-call(f32[1024,128]{1,0:T(8,128)S(1)} %bitcast.13, f32[240,2,16,256]{3,2,1,0:T(8,128)} %outer_turns.1.table_far, bf16[2560,512]{1,0:T(8,128)(2,1)} %constant.34.clone.matrix_far), custom_call_target="tpu_custom_call" | custom-call | tf_op jit(solution)/shard_map/outer/pallas_call | solution.py:980
  66.2 17.8 %all_to_all.15 = f32[128,8,128]{2,1,0:T(8,128)S(1)} all-to-all(f32[128,8,128]{2,1,0:T(8,128)S(1)} %bitcast.14), channel_id=1, replica_groups=mesh['bx'=8,'by'=16] {'bx','by'}, dimensions={0} | all-to-all | bytes 1048576 | tf_op jit(solution)/shard_map/all_to_all | solution.py:1011
  84.0 0.8 result.1
Async XLA Ops:
  1.7 22.4 %all-to-all-start = ((f32[128,4,128]{2,1,0:T(4,128)}), f32[128,4,128]{2,1,0:T(4,128)S(1)}, u32[]{:S(2)}, u32[]{:S(2)}) async-start(f32[128,4,128]{2,1,0:T(4,128)} %bitcast.17), calls=%async_computation | async-start | bytes 524288 | tf_op jit(solution)/shard_map/all_to_all | solution.py:1011
  22.9 25.0 %copy-start = (f32[24,256]{1,0:T(8,128)S(1)}, f32[24,256]{1,0:T(8,128)}, u32[]{:S(2)}) copy-start(f32[24,256]{1,0:T(8,128)} %constant.32.clone.node_far.node) | copy-start | bytes 73732
  38.1 22.1 %all-to-all-start.1 = ((f32[128,8,128]{2,1,0:T(8,128)}), f32[128,8,128]{2,1,0:T(8,128)S(1)}, u32[]{:S(2)}, u32[]{:S(2)}) async-start(f32[128,8,128]{2,1,0:T(8,128)} %bitcast.8), calls=%async_computation.1 | async-start | bytes 1048576 | tf_op jit(solution)/shard_map/all_to_all | solution.py:1011
